TPU v7x, 32 devices: a whole 2x2x4 slice. The times are simulated.
32 devices in a mesh: copies: 2 (over y), dom: 4 (over z), mesh: 2 (over core), sub: 2 (over x).
Axes of the slice: x: 2, y: 2, z: 4, core: 2. Of those that a mesh axis runs over, the one named last changes fastest.
Arguments:
- modes_in: float32 [2, 32, 128, 256], P('mesh', 'copies', 'dom', 'sub'), parts along dimension 1, may hold values from -6 to 6
- stiffness: float32 [4, 128, 256], P(('copies', 'mesh'), 'dom', 'sub'), parts along dimension 0, may hold values from 0.5 to 4
- coupling: bfloat16 [2, 4, 2, 96, 128, 128], P('mesh', 'dom', 'sub'), may hold values from -0.5 to 0.5
- pair_own: int32 [2, 4, 2, 96], P('mesh', 'dom', 'sub'), may hold values from 0 to 31
- pair_peer: int32 [2, 4, 2, 96], P('mesh', 'dom', 'sub'), may hold values from 0 to 3
- pair_slot: int32 [2, 4, 2, 96], P('mesh', 'dom', 'sub'), may hold values from 0 to 7
- send_rows: int32 [2, 4, 2, 4, 8], P('mesh', 'dom', 'sub'), may hold values from 0 to 31
Outputs:
- modes_out: float32 [2, 32, 128, 256], P('mesh', 'copies', 'dom', 'sub'), parts along dimension 1
There are 2 independent parts, one for each index of `copies`. A program takes and returns all parts, laid end to end along the dimension named above; an argument that names none is the same for every part. Nothing has to cross between parts.
All inputs are finite; a program needn't handle non-finite values.
Results may differ from a plain program's by a relative error of at most 0.0012.
Values may be sent and summed in bfloat16 or wider, within the bound.
No kernel may reach another device: no remote copies, remote signals or barrier semaphores. Data moves between devices by JAX's collectives and lax.ppermute only.
A program may use at most 64 MiB of HBM per device.

v0:
```python
import jax
import jax.numpy as jnp
from jax import lax
from jax.sharding import PartitionSpec as P

helm_shift = 1.0
neighbours = ((1, 0), (-1, 0), (0, 1), (0, -1))


def padded(cells, sides, width):
    for axis, dim in sides:
        count = lax.axis_size(axis)
        ends = count - 1
        head = lax.slice_in_dim(cells, 0, width, axis=dim)
        tail = lax.slice_in_dim(cells, cells.shape[dim] - width, cells.shape[dim], axis=dim)
        cells = jnp.concatenate(
            [
                lax.ppermute(tail, axis, [(i, (i + 1) % count) for i in range(ends)]),
                cells,
                lax.ppermute(head, axis, [((i + 1) % count, i) for i in range(ends)]),
            ],
            axis=dim,
        )
    return cells


def from_partner(block, axis, distance):
    count = lax.axis_size(axis)
    route = []
    for low in range(count):
        high = low | 1 << distance
        if high != low and high < count:
            route += [(low, high), (high, low)]
    return lax.ppermute(block, axis, route)


def shards(modes_in, stiffness, coupling, pair_own, pair_peer, pair_slot, send_rows):
    values = modes_in[0]
    stiff = stiffness[0]
    mode_count, rows_local, tile_cells = values.shape
    mesh_half = lax.axis_index("mesh")
    shift = helm_shift * mesh_half.astype(jnp.float32)
    value_pad, stiff_pad = (
        padded(modes_in, (("dom", 2), ("sub", 3)), 1),
        padded(stiffness[:, None], (("dom", 2), ("sub", 3)), 1),
    )
    value_pad = value_pad[0]
    stiff_pad = stiff_pad[0, 0]
    result = -shift * values
    for spacing_horizontal, step_y in neighbours:
        near_value = value_pad[
            :,
            1 + spacing_horizontal : 1 + spacing_horizontal + rows_local,
            1 + step_y : 1 + step_y + tile_cells,
        ]
        near_stiff = stiff_pad[
            1 + spacing_horizontal : 1 + spacing_horizontal + rows_local,
            1 + step_y : 1 + step_y + tile_cells,
        ]
        result = result + 0.5 * (stiff + near_stiff) * (values - near_value)
    tile_rows = jnp.transpose(values.astype(jnp.bfloat16), (1, 0, 2))
    row_map = send_rows[0, 0, 0]
    peer_count, count_of_slots = row_map.shape
    outgoing = jnp.take(tile_rows, row_map.reshape(-1), axis=0).reshape(
        peer_count, count_of_slots, mode_count, tile_cells
    )
    incoming = from_partner(
        lax.all_to_all(outgoing, "dom", split_axis=0, concat_axis=0, tiled=True), "mesh", 0
    )
    flat_in = incoming.reshape(peer_count * count_of_slots, mode_count, tile_cells)
    own_rows = pair_own[0, 0, 0]
    slot_index = pair_peer[0, 0, 0] * count_of_slots + pair_slot[0, 0, 0]
    block_groups = coupling[0, 0, 0]
    resident_tile_set = jnp.take(tile_rows, own_rows, axis=0)
    row_range = jnp.arange(rows_local, dtype=jnp.int32)
    slot_range = jnp.arange(peer_count * count_of_slots, dtype=jnp.int32)
    slot_onehot = (slot_index[None, :] == slot_range[:, None]).astype(jnp.float32)
    back_onehot = (row_map.reshape(-1)[None, :] == row_range[:, None]).astype(jnp.float32)
    return_contributions = jnp.einsum(
        "igl,ilt->igt", resident_tile_set, block_groups, preferred_element_type=jnp.float32
    )
    returned = jnp.einsum(
        "kp,pmt->kmt", slot_onehot, return_contributions, precision=lax.Precision.HIGHEST
    )
    returned = returned.reshape(peer_count, count_of_slots, resident_tile_set.shape[1], tile_cells)
    arrived = lax.all_to_all(
        from_partner(returned.astype(jnp.bfloat16), "mesh", 0)
        .astype(returned.dtype)
        .astype(jnp.bfloat16),
        "dom",
        split_axis=0,
        concat_axis=0,
        tiled=True,
    ).astype(jnp.float32)
    flat = arrived.reshape(peer_count * count_of_slots, arrived.shape[2], tile_cells)
    back_total = jnp.einsum("xk,kmt->xmt", back_onehot, flat, precision=lax.Precision.HIGHEST)
    foreign_tile_set = jnp.take(flat_in, slot_index, axis=0)
    self_contributions = jnp.einsum(
        "afs,aks->afk", foreign_tile_set, block_groups, preferred_element_type=jnp.float32
    )
    own_onehot = (own_rows[None, :] == row_range[:, None]).astype(jnp.float32)
    own_total = jnp.einsum(
        "xp,pmt->xmt", own_onehot, self_contributions, precision=lax.Precision.HIGHEST
    )
    coupled = jnp.transpose(own_total + back_total, (1, 0, 2))
    return (result - coupled)[None]


def solution(mesh):
    return jax.shard_map(
        shards,
        mesh=mesh,
        in_specs=(
            P("mesh", "copies", "dom", "sub"),
            P(("copies", "mesh"), "dom", "sub"),
            P("mesh", "dom", "sub", None, None, None),
            P("mesh", "dom", "sub", None),
            P("mesh", "dom", "sub", None),
            P("mesh", "dom", "sub", None),
            P("mesh", "dom", "sub", None, None),
        ),
        out_specs=P("mesh", "copies", "dom", "sub"),
        check_vma=False,
    )
```

profile of v0, /device:TPU:0, one launch (start us, length us, event | category | flops | bytes accessed | tf_op | source)
XLA Modules:
  0.0 72.6 jit_solution(1617366875913750089)
XLA Ops:
  0.0 0.9 %reshape_squeeze.8 = s32[32,1]{0,1:T(1,128)S(1)} reshape(s32[1,1,1,4,8]{4,3,2,1,0:T(4,128)} %param.15) | data formatting | bytes 256 | tf_op jit(solution)/shard_map/reshape;squeeze | solution.py:64
  0.9 0.7 %compare_and_fusion.2 = pred[4,8]{1,0:T(4,128)(4,1)S(1)} fusion(s32[1,1,1,4,8]{4,3,2,1,0:T(4,128)} %param.15), kind=kLoop, calls=%fused_computation.70 | loop fusion | flops 192 | bytes 160 | tf_op jit(solution)/shard_map/jit(_take)/and | solution.py:64
  1.7 1.0 %fusion.25 = bf16[32,16,128]{2,0,1:T(8,128)(2,1)S(1)} fusion(f32[1,16,32,128]{3,2,1,0:T(8,128)} %param.9), kind=kLoop, calls=%fused_computation.38 | loop fusion | flops 65536 | bytes 393216 | tf_op jit(solution)/shard_map/transpose | solution.py:61
  2.6 0.1 copy.10
  2.7 0.6 gather_fusion
  3.3 0.8 %broadcast_select_fusion = bf16[4,8,16,128]{3,2,1,0:T(8,128)(2,1)} fusion(bf16[4,8,16,128]{3,2,1,0:T(8,128)(2,1)S(1)} %bitcast.63, pred[4,8]{1,0:T(4,128)(4,1)S(1)} %compare_and_fusion.2), kind=kLoop, calls=%fused_computation.41 | loop fusion | flops 65536 | bytes 262176 | tf_op jit(solution)/shard_map/jit(_take)/select_n | solution.py:64
  4.1 6.3 %all-to-all-start = ((bf16[4,8,16,128]{3,2,1,0:T(8,128)(2,1)}), bf16[4,8,16,128]{3,2,1,0:T(8,128)(2,1)}, u32[]{:S(2)}, u32[]{:S(2)}) async-start(bf16[4,8,16,128]{3,2,1,0:T(8,128)(2,1)} %broadcast_select_fusion), calls=%async_computation | async-start | bytes 262144 | tf_op jit(solution)/shard_map/all_to_all | solution.py:68
  10.4 1.5 %fusion.45 = (f32[1,16,1,128]{3,2,1,0:T(1,128)}, f32[1,16,1,128]{3,2,1,0:T(1,128)}) fusion(f32[1,16,32,128]{3,2,1,0:T(8,128)} %param.9), kind=kLoop, calls=%fused_computation.76 | loop fusion | bytes 32768 | tf_op jit(solution)/shard_map/slice | solution.py:15
  11.9 1.3 %collective-permute-start.5 = (f32[1,16,1,128]{3,2,1,0:T(1,128)}, f32[1,16,1,128]{3,2,1,0:T(1,128)}, u32[]{:S(2)}, u32[]{:S(2)}) collective-permute-start(f32[1,16,1,128]{3,2,1,0:T(1,128)} %get-tuple-element.11), channel_id=1, source_target_pairs={{4,0},{8,4},{12,8},{5,1},{9,5},{13,9},{6,2},{10,6},{14,10},{7,3},{... | collective-permute-start | bytes 24584 | tf_op jit(solution)/shard_map/ppermute | solution.py:20
  13.2 5.1 %collective-permute-start.4 = (f32[1,16,1,128]{3,2,1,0:T(1,128)}, f32[1,16,1,128]{3,2,1,0:T(1,128)}, u32[]{:S(2)}, u32[]{:S(2)}) collective-permute-start(f32[1,16,1,128]{3,2,1,0:T(1,128)} %get-tuple-element.10), channel_id=1, source_target_pairs={{0,4},{4,8},{8,12},{1,5},{5,9},{9,13},{2,6},{6,10},{10,14},{3,7},{... | collective-permute-start | bytes 24584 | tf_op jit(solution)/shard_map/ppermute | solution.py:18
  18.3 0.7 compare_select_fusion.1
  19.0 1.2 %compare_and_fusion = pred[96]{0:T(512)(128)(4,1)} fusion(s32[1,1,1,96]{3,2,1,0:T(1,128)} %param.12), kind=kLoop, calls=%fused_computation.68 | loop fusion | flops 576 | bytes 480 | tf_op jit(solution)/shard_map/jit(_take)/and | solution.py:74
  20.2 0.6 pad_clamp_fusion
  20.8 1.7 %gather_fusion.2 = bf16[96,16,128]{2,1,0:T(8,128)(2,1)} fusion(bf16[32,16,128]{2,1,0:T(8,128)(2,1)S(1)} %copy.10, s32[1024]{0:T(1024)} %pad_clamp_fusion), kind=kCustom, calls=%fused_computation.1.clone | custom fusion | bytes 786816 | tf_op jit(solution)/shard_map/jit(_take)/gather | solution.py:74
  22.5 1.2 %compare_and_fusion.1 = (pred[96]{0:T(512)(128)(4,1)}, s32[96]{0:T(128)S(1)}) fusion(s32[1,1,1,96]{3,2,1,0:T(1,128)} %param.14, s32[1,1,1,96]{3,2,1,0:T(1,128)} %param.13), kind=kLoop, calls=%fused_computation.69 | loop fusion | flops 768 | bytes 1248 | tf_op jit(solution)/shard_map/jit(_take)/and | solution.py:97
  23.7 2.0 %fusion = f32[96,16,128]{2,1,0:T(8,128)S(1)} fusion(bf16[1,1,1,96,128,128]{5,4,3,2,1,0:T(8,128)(2,1)S(1)} %copy-done, bf16[96,16,128]{2,1,0:T(8,128)(2,1)} %gather_fusion.2, pred[96]{0:T(512)(128)(4,1)} %compare_and_fusion), kind=kOutput, calls=%fused_computation.3 | convolution fusion | flops 50528256 | bytes 4325472 | tf_op jit(solution)/shard_map/igl,ilt->igt/dot_general | solution.py:79
  25.6 0.6 fusion.7
  26.3 0.7 copy.14
  27.0 1.3 %collective-permute-start.1 = (f32[1,1,1,128]{3,2,1,0:T(1,128)S(1)}, f32[1,1,1,128]{3,2,1,0:T(1,128)S(1)}, u32[]{:S(2)}, u32[]{:S(2)}) collective-permute-start(f32[1,1,1,128]{3,2,1,0:T(1,128)S(1)} %get-tuple-element.19), channel_id=1, source_target_pairs={{4,0},{8,4},{12,8},{5,1},{9,5},{13,9},{6,2},{10,6},{14,10},{7,3},{... | collective-permute-start | bytes 1544 | tf_op jit(solution)/shard_map/ppermute | solution.py:20
  28.3 4.5 %collective-permute-start = (f32[1,1,1,128]{3,2,1,0:T(1,128)S(1)}, f32[1,1,1,128]{3,2,1,0:T(1,128)S(1)}, u32[]{:S(2)}, u32[]{:S(2)}) collective-permute-start(f32[1,1,1,128]{3,2,1,0:T(1,128)S(1)} %get-tuple-element.18), channel_id=1, source_target_pairs={{0,4},{4,8},{8,12},{1,5},{5,9},{9,13},{2,6},{6,10},{10,14},{3,7},{... | collective-permute-start | bytes 1544 | tf_op jit(solution)/shard_map/ppermute | solution.py:18
  32.8 0.6 pad_clamp_fusion.1
  33.4 0.6 reshape_squeeze.9
  34.0 0.1 collective-permute-done
  34.1 0.1 fusion.46
  34.2 1.3 %collective-permute-start.3 = (f32[1,1,34,1]{3,2,1,0:T(8,128)S(1)}, f32[1,1,34,1]{3,2,1,0:T(8,128)S(1)}, u32[]{:S(2)}, u32[]{:S(2)}) collective-permute-start(f32[1,1,34,1]{3,2,1,0:T(8,128)S(1)} %get-tuple-element.17), channel_id=1, source_target_pairs={{1,0},{3,2},{5,4},{7,6},{9,8},{11,10},{13,12},{15,14},{17,16},{19,... | collective-permute-start | bytes 416 | tf_op jit(solution)/shard_map/ppermute | solution.py:20
  35.5 4.5 %collective-permute-start.2 = (f32[1,1,34,1]{3,2,1,0:T(8,128)S(1)}, f32[1,1,34,1]{3,2,1,0:T(8,128)S(1)}, u32[]{:S(2)}, u32[]{:S(2)}) collective-permute-start(f32[1,1,34,1]{3,2,1,0:T(8,128)S(1)} %get-tuple-element.16), channel_id=1, source_target_pairs={{0,1},{2,3},{4,5},{6,7},{8,9},{10,11},{12,13},{14,15},{16,17},{18,... | collective-permute-start | bytes 416 | tf_op jit(solution)/shard_map/ppermute | solution.py:18
  40.0 0.0 collective-permute-done.3
  40.0 1.4 %collective-permute-done.2 = f32[1,1,34,1]{3,2,1,0:T(8,128)S(1)} collective-permute-done((f32[1,1,34,1]{3,2,1,0:T(8,128)S(1)}, f32[1,1,34,1]{3,2,1,0:T(8,128)S(1)}, u32[]{:S(2)}, u32[]{:S(2)}) %collective-permute-start.2) | collective-permute-done | bytes 168 | tf_op jit(solution)/shard_map/ppermute | solution.py:18
  41.5 0.7 maximum_bitcast_fusion.1
  42.2 0.0 collective-permute-done.5
  42.2 0.0 collective-permute-done.4
  42.2 0.8 %pad_maximum_fusion = f32[1,16,34,128]{3,2,1,0:T(8,128)S(1)} fusion(f32[1,16,1,128]{3,2,1,0:T(1,128)} %collective-permute-done.5, f32[1,16,32,128]{3,2,1,0:T(8,128)S(1)} %copy-done.1, f32[1,16,1,128]{3,2,1,0:T(1,128)} %collective-permute-done.4), kind=kLoop, calls=%fused_computation.21 | loop fusion | flops 139264 | bytes 557056 | tf_op jit(solution)/shard_map/concatenate | solution.py:16
  43.0 0.9 %fusion.44 = (f32[1,16,34,1]{3,2,1,0:T(8,128)}, f32[1,16,34,1]{3,2,1,0:T(8,128)}) fusion(f32[1,16,34,128]{3,2,1,0:T(8,128)S(1)} %pad_maximum_fusion), kind=kLoop, calls=%fused_computation.75 | loop fusion | bytes 8704 | tf_op jit(solution)/shard_map/slice | solution.py:15
  43.9 1.3 %collective-permute-start.7 = (f32[1,16,34,1]{3,2,1,0:T(8,128)}, f32[1,16,34,1]{3,2,1,0:T(8,128)}, u32[]{:S(2)}, u32[]{:S(2)}) collective-permute-start(f32[1,16,34,1]{3,2,1,0:T(8,128)} %get-tuple-element.9), channel_id=1, source_target_pairs={{1,0},{3,2},{5,4},{7,6},{9,8},{11,10},{13,12},{15,14},{17,16},{19,... | collective-permute-start | bytes 6536 | tf_op jit(solution)/shard_map/ppermute | solution.py:20
  45.2 6.0 %collective-permute-start.6 = (f32[1,16,34,1]{3,2,1,0:T(8,128)}, f32[1,16,34,1]{3,2,1,0:T(8,128)}, u32[]{:S(2)}, u32[]{:S(2)}) collective-permute-start(f32[1,16,34,1]{3,2,1,0:T(8,128)} %get-tuple-element.8), channel_id=1, source_target_pairs={{0,1},{2,3},{4,5},{6,7},{8,9},{10,11},{12,13},{14,15},{16,17},{18,... | collective-permute-start | bytes 6536 | tf_op jit(solution)/shard_map/ppermute | solution.py:18
  51.2 0.0 all-to-all-done
  51.2 0.0 collective-permute-start.8
  51.2 1.6 %fusion.31 = (f32[32,128]{1,0:T(8,128)}, f32[32,128]{1,0:T(8,128)}, f32[32,128]{1,0:T(8,128)}, f32[32,128]{1,0:T(8,128)}) fusion(f32[34,130]{1,0:T(8,128)} %maximum_bitcast_fusion.1, f32[1,32,128]{2,1,0:T(8,128)S(1)} %copy-done.2), kind=kLoop, calls=%fused_computation.51 | loop fusion | flops 32768 | bytes 147456 | tf_op jit(solution)/shard_map/mul | solution.py:60
  52.8 1.6 %collective-permute-done.7 = f32[1,16,34,1]{3,2,1,0:T(8,128)} collective-permute-done((f32[1,16,34,1]{3,2,1,0:T(8,128)}, f32[1,16,34,1]{3,2,1,0:T(8,128)}, u32[]{:S(2)}, u32[]{:S(2)}) %collective-permute-start.7) | collective-permute-done | bytes 2208 | tf_op jit(solution)/shard_map/ppermute | solution.py:20
  54.4 1.9 %collective-permute-done.6 = f32[1,16,34,1]{3,2,1,0:T(8,128)} collective-permute-done((f32[1,16,34,1]{3,2,1,0:T(8,128)}, f32[1,16,34,1]{3,2,1,0:T(8,128)}, u32[]{:S(2)}, u32[]{:S(2)}) %collective-permute-start.6) | collective-permute-done | bytes 2208 | tf_op jit(solution)/shard_map/ppermute | solution.py:18
  56.3 2.3 %maximum_bitcast_fusion = f32[16,34,130]{2,1,0:T(8,128)} fusion(f32[1,16,34,1]{3,2,1,0:T(8,128)} %collective-permute-done.7, f32[1,16,1,128]{3,2,1,0:T(1,128)} %collective-permute-done.5, f32[1,16,32,128]{3,2,1,0:T(8,128)S(1)} %copy-done.1, f32[1,16,1,128]{3,2,1,0:T(1,128)} %collective-permute-done.4, f32[1,16,34,1]{3,2,1,0:T(8,128)} %collective-permute-done.6), kind=kLoop, calls=%fused_computation.16 | loop fusion | flops 282880 | bytes 565760 | tf_op jit(solution)/shard_map/squeeze | solution.py:47
  58.7 0.0 collective-permute-done.9
  58.7 5.1 %all-to-all-start.1 = ((bf16[4,8,16,128]{3,1,2,0:T(8,128)(2,1)}), bf16[4,8,16,128]{3,1,2,0:T(8,128)(2,1)}, u32[]{:S(2)}, u32[]{:S(2)}) async-start(bf16[4,8,16,128]{3,1,2,0:T(8,128)(2,1)} %collective-permute-done.9), calls=%async_computation.1 | async-start | bytes 262144 | tf_op jit(solution)/shard_map/all_to_all | solution.py:86
  63.7 1.7 %gather_fusion.1 = bf16[96,16,128]{2,1,0:T(8,128)(2,1)} fusion(bf16[32,16,128]{2,1,0:T(8,128)(2,1)S(1)} %bitcast.62, s32[1024]{0:T(1024)} %pad_clamp_fusion.1), kind=kCustom, calls=%fused_computation.clone | custom fusion | bytes 786816 | tf_op jit(solution)/shard_map/jit(_take)/gather | solution.py:97
  65.4 2.8 %fusion.2 = f32[96,16,128]{2,1,0:T(8,128)S(1)} fusion(bf16[1,1,1,96,128,128]{5,4,3,2,1,0:T(8,128)(2,1)S(1)} %copy-done, bf16[96,16,128]{2,1,0:T(8,128)(2,1)} %gather_fusion.1, pred[96]{0:T(512)(128)(4,1)} %get-tuple-element.6), kind=kOutput, calls=%fused_computation.5 | convolution fusion | flops 50528256 | bytes 4325472 | tf_op jit(solution)/shard_map/afs,aks->afk/dot_general | solution.py:98
  68.2 1.3 %fusion.9 = f32[32,16,128]{2,0,1:T(8,128)} fusion(f32[96,16,128]{2,1,0:T(8,128)S(1)} %fusion.2, s32[96]{0:T(128)S(1)} %bitcast.67), kind=kOutput, calls=%fused_computation.14 | convolution fusion | flops 75500544 | bytes 1048960 | tf_op jit(solution)/shard_map/xp,pmt->xmt/dot_general | solution.py:102
  69.6 0.2 all-to-all-done.1
  69.8 2.8 %fusion.6 = f32[1,16,32,128]{3,2,1,0:T(8,128)} fusion(f32[32,16,128]{2,0,1:T(8,128)} %fusion.9, f32[16,34,130]{2,1,0:T(8,128)} %maximum_bitcast_fusion, f32[1,16,32,128]{3,2,1,0:T(8,128)S(1)} %copy-done.1, bf16[4,8,16,128]{3,1,2,0:T(8,128)(2,1)} %all-to-all-done.1, f32[32,128]{1,0:T(8,128)S(1)} %copy-done.5, f32[32,128]{1,0:T(8,128)S(1)} %copy-done.6, ...), kind=kOutput, calls=%fused_computation.10 | convolution fusion | flops 5178368 | bytes 2031748 | tf_op jit(solution)/shard_map/xk,kmt->xmt/dot_general | solution.py:96
  (28 shorter events, 0.1 us)
Async XLA Ops:
  0.0 23.7 %copy-start = (bf16[1,1,1,96,128,128]{5,4,3,2,1,0:T(8,128)(2,1)S(1)}, bf16[1,1,1,96,128,128]{5,4,3,2,1,0:T(8,128)(2,1)}, u32[]{:S(2)}) copy-start(bf16[1,1,1,96,128,128]{5,4,3,2,1,0:T(8,128)(2,1)} %param.11) | copy-start | bytes 9437188
  4.1 47.1 %all-to-all-start = ((bf16[4,8,16,128]{3,2,1,0:T(8,128)(2,1)}), bf16[4,8,16,128]{3,2,1,0:T(8,128)(2,1)}, u32[]{:S(2)}, u32[]{:S(2)}) async-start(bf16[4,8,16,128]{3,2,1,0:T(8,128)(2,1)} %broadcast_select_fusion), calls=%async_computation | async-start | bytes 262144 | tf_op jit(solution)/shard_map/all_to_all | solution.py:68
  11.9 30.3 %collective-permute-start.5 = (f32[1,16,1,128]{3,2,1,0:T(1,128)}, f32[1,16,1,128]{3,2,1,0:T(1,128)}, u32[]{:S(2)}, u32[]{:S(2)}) collective-permute-start(f32[1,16,1,128]{3,2,1,0:T(1,128)} %get-tuple-element.11), channel_id=1, source_target_pairs={{4,0},{8,4},{12,8},{5,1},{9,5},{13,9},{6,2},{10,6},{14,10},{7,3},{... | collective-permute-start | bytes 24584 | tf_op jit(solution)/shard_map/ppermute | solution.py:20
  13.2 29.0 %collective-permute-start.4 = (f32[1,16,1,128]{3,2,1,0:T(1,128)}, f32[1,16,1,128]{3,2,1,0:T(1,128)}, u32[]{:S(2)}, u32[]{:S(2)}) collective-permute-start(f32[1,16,1,128]{3,2,1,0:T(1,128)} %get-tuple-element.10), channel_id=1, source_target_pairs={{0,4},{4,8},{8,12},{1,5},{5,9},{9,13},{2,6},{6,10},{10,14},{3,7},{... | collective-permute-start | bytes 24584 | tf_op jit(solution)/shard_map/ppermute | solution.py:18
  20.8 6.2 %copy-start.2 = (f32[1,32,128]{2,1,0:T(8,128)S(1)}, f32[1,32,128]{2,1,0:T(8,128)}, u32[]{:S(2)}) copy-start(f32[1,32,128]{2,1,0:T(8,128)} %param.10) | copy-start | bytes 49156
  20.8 21.4 %copy-start.1 = (f32[1,16,32,128]{3,2,1,0:T(8,128)S(1)}, f32[1,16,32,128]{3,2,1,0:T(8,128)}, u32[]{:S(2)}) copy-start(f32[1,16,32,128]{3,2,1,0:T(8,128)} %param.9) | copy-start | bytes 786436
  22.5 11.0 %copy-start.3 = (s32[1,1,1,4,8]{4,3,2,1,0:T(4,128)S(1)}, s32[1,1,1,4,8]{4,3,2,1,0:T(4,128)}, u32[]{:S(2)}) copy-start(s32[1,1,1,4,8]{4,3,2,1,0:T(4,128)} %param.15) | copy-start | bytes 388
  26.9 31.7 %collective-permute-start.9 = (bf16[4,8,16,128]{3,1,2,0:T(8,128)(2,1)}, bf16[4,8,16,128]{3,1,2,0:T(8,128)(2,1)}, u32[]{:S(2)}, u32[]{:S(2)}) collective-permute-start(bf16[4,8,16,128]{3,1,2,0:T(8,128)(2,1)} %copy.14), channel_id=1, source_target_pairs={{0,2},{2,0},{1,3},{3,1},{4,6},{6,4},{5,7},{7,5},{8,10},{10,8},{9,1... | collective-permute-start | bytes 393224 | tf_op jit(solution)/shard_map/ppermute | solution.py:34
  27.0 7.0 %collective-permute-start.1 = (f32[1,1,1,128]{3,2,1,0:T(1,128)S(1)}, f32[1,1,1,128]{3,2,1,0:T(1,128)S(1)}, u32[]{:S(2)}, u32[]{:S(2)}) collective-permute-start(f32[1,1,1,128]{3,2,1,0:T(1,128)S(1)} %get-tuple-element.19), channel_id=1, source_target_pairs={{4,0},{8,4},{12,8},{5,1},{9,5},{13,9},{6,2},{10,6},{14,10},{7,3},{... | collective-permute-start | bytes 1544 | tf_op jit(solution)/shard_map/ppermute | solution.py:20
  28.3 5.8 %collective-permute-start = (f32[1,1,1,128]{3,2,1,0:T(1,128)S(1)}, f32[1,1,1,128]{3,2,1,0:T(1,128)S(1)}, u32[]{:S(2)}, u32[]{:S(2)}) collective-permute-start(f32[1,1,1,128]{3,2,1,0:T(1,128)S(1)} %get-tuple-element.18), channel_id=1, source_target_pairs={{0,4},{4,8},{8,12},{1,5},{5,9},{9,13},{2,6},{6,10},{10,14},{3,7},{... | collective-permute-start | bytes 1544 | tf_op jit(solution)/shard_map/ppermute | solution.py:18
  34.2 5.9 %collective-permute-start.3 = (f32[1,1,34,1]{3,2,1,0:T(8,128)S(1)}, f32[1,1,34,1]{3,2,1,0:T(8,128)S(1)}, u32[]{:S(2)}, u32[]{:S(2)}) collective-permute-start(f32[1,1,34,1]{3,2,1,0:T(8,128)S(1)} %get-tuple-element.17), channel_id=1, source_target_pairs={{1,0},{3,2},{5,4},{7,6},{9,8},{11,10},{13,12},{15,14},{17,16},{19,... | collective-permute-start | bytes 416 | tf_op jit(solution)/shard_map/ppermute | solution.py:20
  35.5 6.0 %collective-permute-start.2 = (f32[1,1,34,1]{3,2,1,0:T(8,128)S(1)}, f32[1,1,34,1]{3,2,1,0:T(8,128)S(1)}, u32[]{:S(2)}, u32[]{:S(2)}) collective-permute-start(f32[1,1,34,1]{3,2,1,0:T(8,128)S(1)} %get-tuple-element.16), channel_id=1, source_target_pairs={{0,1},{2,3},{4,5},{6,7},{8,9},{10,11},{12,13},{14,15},{16,17},{18,... | collective-permute-start | bytes 416 | tf_op jit(solution)/shard_map/ppermute | solution.py:18
  43.9 10.5 %collective-permute-start.7 = (f32[1,16,34,1]{3,2,1,0:T(8,128)}, f32[1,16,34,1]{3,2,1,0:T(8,128)}, u32[]{:S(2)}, u32[]{:S(2)}) collective-permute-start(f32[1,16,34,1]{3,2,1,0:T(8,128)} %get-tuple-element.9), channel_id=1, source_target_pairs={{1,0},{3,2},{5,4},{7,6},{9,8},{11,10},{13,12},{15,14},{17,16},{19,... | collective-permute-start | bytes 6536 | tf_op jit(solution)/shard_map/ppermute | solution.py:20
  45.2 11.1 %collective-permute-start.6 = (f32[1,16,34,1]{3,2,1,0:T(8,128)}, f32[1,16,34,1]{3,2,1,0:T(8,128)}, u32[]{:S(2)}, u32[]{:S(2)}) collective-permute-start(f32[1,16,34,1]{3,2,1,0:T(8,128)} %get-tuple-element.8), channel_id=1, source_target_pairs={{0,1},{2,3},{4,5},{6,7},{8,9},{10,11},{12,13},{14,15},{16,17},{18,... | collective-permute-start | bytes 6536 | tf_op jit(solution)/shard_map/ppermute | solution.py:18
  51.2 12.5 %collective-permute-start.8 = (bf16[4,8,16,128]{3,2,1,0:T(8,128)(2,1)}, bf16[4,8,16,128]{3,2,1,0:T(8,128)(2,1)S(1)}, u32[]{:S(2)}, u32[]{:S(2)}) collective-permute-start(bf16[4,8,16,128]{3,2,1,0:T(8,128)(2,1)} %all-to-all-done), channel_id=1, source_target_pairs={{0,2},{2,0},{1,3},{3,1},{4,6},{6,4},{5,7},{7,5},{8,10},{10,8},{9,1... | collective-permute-start | bytes 393224 | tf_op jit(solution)/shard_map/ppermute | solution.py:34
  58.7 11.1 %all-to-all-start.1 = ((bf16[4,8,16,128]{3,1,2,0:T(8,128)(2,1)}), bf16[4,8,16,128]{3,1,2,0:T(8,128)(2,1)}, u32[]{:S(2)}, u32[]{:S(2)}) async-start(bf16[4,8,16,128]{3,1,2,0:T(8,128)(2,1)} %collective-permute-done.9), calls=%async_computation.1 | async-start | bytes 262144 | tf_op jit(solution)/shard_map/all_to_all | solution.py:86
  63.7 6.0 %copy-start.4 = (f32[32,128]{1,0:T(8,128)S(1)}, f32[32,128]{1,0:T(8,128)}, u32[]{:S(2)}) copy-start(f32[32,128]{1,0:T(8,128)} %get-tuple-element.12) | copy-start | bytes 49156
  65.4 2.8 %copy-start.8 = (s32[1,1,1,96]{3,2,1,0:T(1,128)S(1)}, s32[1,1,1,96]{3,2,1,0:T(1,128)}, u32[]{:S(2)}) copy-start(s32[1,1,1,96]{3,2,1,0:T(1,128)} %param.12) | copy-start | bytes 1156
  65.4 4.3 %copy-start.5 = (f32[32,128]{1,0:T(8,128)S(1)}, f32[32,128]{1,0:T(8,128)}, u32[]{:S(2)}) copy-start(f32[32,128]{1,0:T(8,128)} %get-tuple-element.13) | copy-start | bytes 49156
  65.4 4.4 %copy-start.6 = (f32[32,128]{1,0:T(8,128)S(1)}, f32[32,128]{1,0:T(8,128)}, u32[]{:S(2)}) copy-start(f32[32,128]{1,0:T(8,128)} %get-tuple-element.14) | copy-start | bytes 49156
  65.4 4.4 %copy-start.7 = (f32[32,128]{1,0:T(8,128)S(1)}, f32[32,128]{1,0:T(8,128)}, u32[]{:S(2)}) copy-start(f32[32,128]{1,0:T(8,128)} %get-tuple-element.15) | copy-start | bytes 49156
  65.4 4.4 %copy-start.9 = (s32[32]{0:T(128)S(1)}, s32[32]{0:T(128)}, u32[]{:S(2)}) copy-start(s32[32]{0:T(128)} %reshape_squeeze.9) | copy-start | bytes 388
where the time goes:
time: 73.5 us; the launch traced here: 72.6 us
  starting transfers between devices  36.8 us (50%)
  other arithmetic  12.2 us (17%)
  matrix products  9.57 us (13%)
  local copies, waits for them, and re-layouts  8.68 us (12%)
  waiting for transfers between devices  5.25 us (7%)
    ppermute x4, starting transfers between devices, padded(): lax.ppermute(tail, axis, [(i, (i + 1) % count) for i in range(ends)])  20.2 us
    all_to_all x1, starting transfers between devices, shards(): lax.all_to_all(outgoing, 'dom', split_axis=0, concat_axis=0, tiled=True)  6.32 us
    ppermute x4, starting transfers between devices, padded(): lax.ppermute(head, axis, [((i + 1) % count, i) for i in range(ends)])  5.14 us
    all_to_all x1, starting transfers between devices, shards(): lax.all_to_all(from_partner(returned.astype(jnp.bfloat16), 'mesh', 0).ast...  5.06 us
    ppermute x4, waiting for transfers between devices, padded(): lax.ppermute(tail, axis, [(i, (i + 1) % count) for i in range(ends)])  3.43 us
    dot_general x1, matrix products, shards(): jnp.einsum('xk,kmt->xmt', back_onehot, flat, precision=lax.Precision.HIGH...  2.84 us
    dot_general x1, matrix products, shards(): jnp.einsum('afs,aks->afk', foreign_tile_set, block_groups, preferred_elem...  2.81 us
    slice x4, local copies, waits for them, and re-layouts, padded(): lax.slice_in_dim(cells, cells.shape[dim] - width, cells.shape[dim], axis=...  2.49 us
  transfers between devices with their start and end apart: 12, of which 5 were waited for; matrix products, arithmetic and copies ran while one was open for 32% of the time, Pallas kernels for 0%

commit v1 on v0

v1 whole, which is shorter than its diff:
```python
import functools

import jax
import jax.numpy as jnp
from jax import lax
from jax.experimental import pallas as pl
from jax.experimental.pallas import tpu as pltpu
from jax.sharding import PartitionSpec as P

helm_shift = 1.0
PIECES = 4
CHUNK = 16
LANES = 64
VMEM = pl.BlockSpec(memory_space=pltpu.VMEM)
HBM = pl.BlockSpec(memory_space=pltpu.HBM)


def pieces(x):
    high = x.astype(jnp.bfloat16)
    rest = x - high.astype(jnp.float32)
    middle = rest.astype(jnp.bfloat16)
    low = (rest - middle.astype(jnp.float32)).astype(jnp.bfloat16)
    return high, middle, low


def whole(high, middle, low):
    f = jnp.float32
    return high.astype(f) + (middle.astype(f) + low.astype(f))


def load(sources, targets, sems):
    copies = [pltpu.make_async_copy(a, b, sems.at[i]) for i, (a, b) in enumerate(zip(sources, targets))]
    for copy in copies:
        copy.start()
    return copies


def before(doms, slots, rows, own_in, peer_in, slot_in, send_in, modes_in, stiff_in, coupling, *refs):
    outs, (edges, column, blocks) = refs[:doms], refs[doms : doms + 3]
    own, peer, slot, send, modes, stiff, tiles, sums, sems, block_sems = refs[doms + 3 :]
    sources = (own_in, peer_in, slot_in, send_in, modes_in, stiff_in)
    copies = load(sources, (own, peer, slot, send, modes, stiff), sems)
    parts = [pl.ds(i, CHUNK) for i in range(0, blocks.shape[0], CHUNK)]
    block_copies = load([coupling.at[0, 0, 0, part] for part in parts], [blocks.at[part] for part in parts], block_sems)
    d = lax.axis_index("dom")
    count, cells = tiles.shape[1:]
    sums[...] = jnp.zeros_like(sums)
    for copy in copies:
        copy.wait()
    for r in range(rows):
        tiles[r] = modes[pl.ds(r, count, stride=rows), :].astype(jnp.bfloat16)

    def edge_tiles(target, first, row):
        edge = modes[pl.ds(row, count, stride=rows), :]
        for i, piece in enumerate(pieces(edge)):
            target[first + i] = piece
        edge = jnp.broadcast_to(stiff[0, pl.ds(row, 1), :], edge.shape)
        line = lax.broadcasted_iota(jnp.int32, edge.shape, 0)
        high, middle, low = (p.astype(jnp.float32) for p in pieces(edge))
        mixed = jnp.where(line == 0, high, jnp.where(line == 1, middle, low))
        target[first + 3] = mixed.astype(jnp.bfloat16)

    even = d % 2 == 0
    if doms > 1:
        edge_tiles(outs[1], 2 * slots, jnp.where(even, rows - 1, 0))
    edge_tiles(edges, 0, jnp.where(even, 0, rows - 1))
    for k in range(doms):
        for j in range(slots):
            outs[k][j] = tiles[send[0, 0, 0, d ^ k, j]]
    lane = lax.broadcasted_iota(jnp.int32, (rows, cells), 1)
    packed = jnp.zeros((rows, cells), jnp.float32)
    for m in range(count + 1):
        here = stiff[0] if m == count else modes[m * rows : (m + 1) * rows, :]
        packed = jnp.where(lane == m, here[:, :1], packed)
        packed = jnp.where(lane == LANES + m, here[:, -1:], packed)
    column[...] = packed
    for c, copy in enumerate(block_copies):
        copy.wait()
        for p in range(c * CHUNK, (c + 1) * CHUNK):
            term = jnp.dot(tiles[own[0, 0, 0, p]], blocks[p], preferred_element_type=jnp.float32)
            sums[peer[0, 0, 0, p] * slots + slot[0, 0, 0, p]] += term
    for k in range(doms):
        for j in range(slots):
            outs[k][slots + j] = sums[(d ^ k) * slots + j].astype(jnp.bfloat16)


def pick(slots, arrived, halo):
    halo[...] = arrived[2 * slots : 2 * slots + PIECES]


def after(doms, slots, subs, rows, own_in, peer_in, slot_in, send_in, modes_in, stiff_in, blocks, near, far, *refs):
    arrived, columns, out = refs[:doms], refs[doms:-11], refs[-11]
    own, peer, slot, send, modes, stiff, foreign, total, back, sems = refs[-10:]
    sources = (own_in, peer_in, slot_in, send_in, modes_in, stiff_in)
    copies = load(sources, (own, peer, slot, send, modes, stiff), sems)
    d = lax.axis_index("dom")
    s = lax.axis_index("sub")
    shift = helm_shift * lax.axis_index("mesh").astype(jnp.float32)
    count, cells = foreign.shape[1:]
    total[...] = jnp.zeros_like(total)
    for k in range(doms):
        for j in range(slots):
            foreign[(d ^ k) * slots + j] = arrived[k][j]
            back[(d ^ k) * slots + j] = arrived[k][slots + j].astype(jnp.float32)
    for copy in copies:
        copy.wait()
    for g in range(doms):
        for j in range(slots):
            total[send[0, 0, 0, g, j]] += back[g * slots + j]
    for p in range(blocks.shape[0]):
        term = lax.dot_general(
            foreign[peer[0, 0, 0, p] * slots + slot[0, 0, 0, p]],
            blocks[p],
            (((1,), (1,)), ((), ())),
            preferred_element_type=jnp.float32,
        )
        total[own[0, 0, 0, p]] += term
    lane = lax.broadcasted_iota(jnp.int32, (rows, cells), 1)
    line = lax.broadcasted_iota(jnp.int32, (rows, cells), 0)
    first_lane, last_lane = lane == 0, lane == cells - 1
    first_line, last_line = line == 0, line == rows - 1
    if subs == 1:
        left = right = jnp.zeros(lane.shape, jnp.float32)
    elif subs == 2:
        left, right = jnp.where(s == 1, columns[0][...], 0.0), jnp.where(s == 0, columns[0][...], 0.0)
    else:
        left, right = columns[0][...], columns[1][...]

    def around(here, above, below, m):
        return (
            jnp.where(first_line, above, pltpu.roll(here, 1, 0)),
            jnp.where(last_line, below, pltpu.roll(here, rows - 1, 0)),
            jnp.where(first_lane, left[:, LANES + m : LANES + m + 1], pltpu.roll(here, 1, 1)),
            jnp.where(last_lane, right[:, m : m + 1], pltpu.roll(here, cells - 1, 1)),
        )

    even = d % 2 == 0
    inner = [whole(*(ref[i] for i in range(3))) for ref in (near, far)]
    coefficients = [whole(*(ref[3, i : i + 1] for i in range(3))) for ref in (near, far)]
    above, below = (jnp.where(even, inner[1 - i], inner[i]) for i in range(2))
    stiff_above, stiff_below = (jnp.where(even, coefficients[1 - i], coefficients[i]) for i in range(2))
    weights = [0.5 * (stiff[0] + beside) for beside in around(stiff[0], stiff_above, stiff_below, count)]
    for m in range(count):
        here = modes[m * rows : (m + 1) * rows, :]
        result = -shift * here
        for weight, beside in zip(weights, around(here, above[m : m + 1], below[m : m + 1], m)):
            result = result + weight * (here - beside)
        out[m * rows : (m + 1) * rows, :] = result - total[:, m, :]


def shards(doms, subs, modes_in, stiffness, coupling, pair_own, pair_peer, pair_slot, send_rows):
    _, count, rows, cells = modes_in.shape
    slots, pairs = send_rows.shape[-1], coupling.shape[3]
    flat = modes_in.reshape(count * rows, cells)
    inputs = (pair_own, pair_peer, pair_slot, send_rows, flat, stiffness, coupling)
    *inputs, coupling = [pltpu.with_memory_space_constraint(a, pltpu.HBM) for a in inputs]
    params = pltpu.CompilerParams(vmem_limit_bytes=32 * 1024 * 1024)
    held = [pltpu.SMEM(a.shape, a.dtype) for a in inputs[:4]] + [pltpu.VMEM(a.shape, a.dtype) for a in inputs[4:]]
    like = jax.ShapeDtypeStruct
    *outgoing, edges, column, blocks = pl.pallas_call(
        functools.partial(before, doms, slots, rows),
        out_shape=[like((2 * slots + PIECES * (k == 1), count, cells), jnp.bfloat16) for k in range(doms)]
        + [
            like((PIECES, count, cells), jnp.bfloat16),
            like((rows, cells), jnp.float32),
            like((pairs, cells, cells), jnp.bfloat16),
        ],
        in_specs=[HBM] * 7,
        out_specs=[VMEM] * (doms + 3),
        scratch_shapes=held
        + [
            pltpu.VMEM((rows, count, cells), jnp.bfloat16),
            pltpu.VMEM((doms * slots, count, cells), jnp.float32),
            pltpu.SemaphoreType.DMA((len(inputs),)),
            pltpu.SemaphoreType.DMA((pairs // CHUNK,)),
        ],
        compiler_params=params,
        name="before",
    )(*inputs, coupling)
    order = list(range(doms - 1, 0, -1)) + [0]
    if doms == 4:
        order = [3, 1, 2, 0]
    arrived = {}
    for k in order:
        route = [(2 * d + h, 2 * (d ^ k) + 1 - h) for d in range(doms) for h in range(2)]
        arrived[k] = lax.ppermute(outgoing[k], ("dom", "mesh"), route)
    if subs == 1:
        columns = []
    elif subs == 2:
        columns = [lax.ppermute(column, "sub", [(0, 1), (1, 0)])]
    else:
        columns = [
            lax.ppermute(column, "sub", [(i, i + 1) for i in range(subs - 1)]),
            lax.ppermute(column, "sub", [(i + 1, i) for i in range(subs - 1)]),
        ]
    cuts = [(i, i + 1) for i in range(1, doms - 1, 2)]
    far = lax.ppermute(edges, "dom", cuts + [(j, i) for i, j in cuts])
    near = pl.pallas_call(
        functools.partial(pick, slots),
        out_shape=like((PIECES, count, cells), jnp.bfloat16),
        in_specs=[VMEM],
        out_specs=VMEM,
        compiler_params=params,
        name="pick",
    )(arrived[1])
    near = lax.ppermute(near, "mesh", [(0, 1), (1, 0)])
    out = pl.pallas_call(
        functools.partial(after, doms, slots, subs, rows),
        out_shape=like(flat.shape, jnp.float32),
        in_specs=[HBM] * 6 + [VMEM] * (3 + doms + len(columns)),
        out_specs=VMEM,
        scratch_shapes=held
        + [
            pltpu.VMEM((doms * slots, count, cells), jnp.bfloat16),
            pltpu.VMEM((rows, count, cells), jnp.float32),
            pltpu.VMEM((doms * slots, count, cells), jnp.float32),
            pltpu.SemaphoreType.DMA((len(inputs),)),
        ],
        compiler_params=params,
        name="after",
    )(*inputs, blocks, near, far, *(arrived[k] for k in range(doms)), *columns)
    return out.reshape(modes_in.shape)


def solution(mesh):
    return jax.shard_map(
        functools.partial(shards, mesh.shape["dom"], mesh.shape["sub"]),
        mesh=mesh,
        in_specs=(
            P("mesh", "copies", "dom", "sub"),
            P(("copies", "mesh"), "dom", "sub"),
            P("mesh", "dom", "sub", None, None, None),
            P("mesh", "dom", "sub", None),
            P("mesh", "dom", "sub", None),
            P("mesh", "dom", "sub", None),
            P("mesh", "dom", "sub", None, None),
        ),
        out_specs=P("mesh", "copies", "dom", "sub"),
        check_vma=False,
    )
```

time: 73.5 us -> 20 us (0.27)
  the two profiles are of different devices: /device:TPU:0 before, /device:TPU:19 now
where the time goes in v1:
time: 20 us; the launch traced here: 19.8 us
  Pallas kernels  7.62 us (38%)
  starting transfers between devices  6.89 us (34%)
  waiting for transfers between devices  5.24 us (26%)
    ppermute x1, waiting for transfers between devices, shards(): far = lax.ppermute(edges, 'dom', cuts + [(j, i) for i, j in cuts])  4.41 us
    pallas_call x1, Pallas kernels, shards(): pl.pallas_call(functools.partial(after, doms, slots, subs, rows), out_sha...  3.93 us
    pallas_call x1, Pallas kernels, shards(): pl.pallas_call(functools.partial(before, doms, slots, rows), out_shape=[l...  3.69 us
    ppermute x4, starting transfers between devices, shards(): arrived[k] = lax.ppermute(outgoing[k], ('dom', 'mesh'), route)  3.58 us
    ppermute x1, starting transfers between devices, shards(): far = lax.ppermute(edges, 'dom', cuts + [(j, i) for i, j in cuts])  2.1 us
    ppermute x1, starting transfers between devices, shards(): near = lax.ppermute(near, 'mesh', [(0, 1), (1, 0)])  0.89 us
    ppermute x1, waiting for transfers between devices, shards(): near = lax.ppermute(near, 'mesh', [(0, 1), (1, 0)])  0.82 us
  transfers between devices with their start and end apart: 7, of which 2 were waited for; matrix products, arithmetic and copies ran while one was open for 0% of the time, Pallas kernels for 0%

profile of v1, /device:TPU:19, one launch (start us, length us, event | category | flops | bytes accessed | tf_op | source)
XLA Modules:
  0.0 19.8 jit_solution(5696048015661690377)
XLA Ops:
  0.0 3.7 %before.1 = (bf16[16,16,128]{2,1,0:T(8,128)(2,1)S(1)}, bf16[20,16,128]{2,1,0:T(8,128)(2,1)S(1)}, bf16[16,16,128]{2,1,0:T(8,128)(2,1)S(1)}, bf16[16,16,128]{2,1,0...) custom-call(s32[1,1,1,96]{3,2,1,0:T(1,128)} %own_in.3, ...), custom_call_target="tpu_custom_call" | custom-call | tf_op jit(solution)/shard_map/before/pallas_call | solution.py:160
  3.7 1.9 %collective-permute-start = (bf16[20,16,128]{2,1,0:T(8,128)(2,1)S(1)}, bf16[20,16,128]{2,1,0:T(8,128)(2,1)S(1)}, u32[]{:S(2)}, u32[]{:S(2)}) collective-permute-start(bf16[20,16,128]{2,1,0:T(8,128)(2,1)S(1)} %get-tuple-element.13), channel_id=1, source_target_pairs={{0,6},{2,4},{4,2},{6,0},{8,14},{10,12},{12,10},{14,8},{1,7},{3,5},... | collective-permute-start | bytes 245768 | tf_op jit(solution)/shard_map/ppermute | solution.py:186
  5.6 0.0 collective-permute-start.3
  5.6 0.4 %collective-permute-start.4 = (bf16[16,16,128]{2,1,0:T(8,128)(2,1)S(1)}, bf16[16,16,128]{2,1,0:T(8,128)(2,1)S(1)}, u32[]{:S(2)}, u32[]{:S(2)}) collective-permute-start(bf16[16,16,128]{2,1,0:T(8,128)(2,1)S(1)} %get-tuple-element.16), channel_id=1, source_target_pairs={{0,10},{2,8},{4,14},{6,12},{8,2},{10,0},{12,6},{14,4},{1,11},{3,9}... | collective-permute-start | bytes 196616 | tf_op jit(solution)/shard_map/ppermute | solution.py:186
  6.1 1.2 %collective-permute-start.5 = (bf16[16,16,128]{2,1,0:T(8,128)(2,1)S(1)}, bf16[16,16,128]{2,1,0:T(8,128)(2,1)S(1)}, u32[]{:S(2)}, u32[]{:S(2)}) collective-permute-start(bf16[16,16,128]{2,1,0:T(8,128)(2,1)S(1)} %get-tuple-element.17), channel_id=1, source_target_pairs={{0,14},{2,12},{4,10},{6,8},{8,6},{10,4},{12,2},{14,0},{1,15},{3,13... | collective-permute-start | bytes 196616 | tf_op jit(solution)/shard_map/ppermute | solution.py:186
  7.3 2.1 %collective-permute-start.2 = (bf16[4,16,128]{2,1,0:T(8,128)(2,1)S(1)}, bf16[4,16,128]{2,1,0:T(8,128)(2,1)S(1)}, u32[]{:S(2)}, u32[]{:S(2)}) collective-permute-start(bf16[4,16,128]{2,1,0:T(8,128)(2,1)S(1)} %get-tuple-element.14), channel_id=1, source_target_pairs={{4,8},{8,4},{5,9},{9,5},{6,10},{10,6},{7,11},{11,7},{20,24},{24,20... | collective-permute-start | bytes 49160 | tf_op jit(solution)/shard_map/ppermute | solution.py:197
  9.4 0.0 collective-permute-done.arrived.refs_1_
  9.4 0.3 %collective-permute-start.6 = (f32[32,128]{1,0:T(8,128)S(1)}, f32[32,128]{1,0:T(8,128)S(1)}, u32[]{:S(2)}, u32[]{:S(2)}) collective-permute-start(f32[32,128]{1,0:T(8,128)S(1)} %get-tuple-element.18), channel_id=1, source_target_pairs={{0,1},{1,0},{2,3},{3,2},{4,5},{5,4},{6,7},{7,6},{8,9},{9,8},{10,11... | collective-permute-start | bytes 49160 | tf_op jit(solution)/shard_map/ppermute | solution.py:190
  9.7 4.4 %collective-permute-done.2.far = bf16[4,16,128]{2,1,0:T(8,128)(2,1)S(1)} collective-permute-done((bf16[4,16,128]{2,1,0:T(8,128)(2,1)S(1)}, bf16[4,16,128]{2,1,0:T(8,128)(2,1)S(1)}, u32[]{:S(2)}, u32[]{:S(2)}) %collective-permute-start.2) | collective-permute-done | bytes 16416 | tf_op jit(solution)/shard_map/ppermute | solution.py:197
  14.1 0.9 %collective-permute-start.1 = (bf16[4,16,128]{2,1,0:T(8,128)(2,1)S(1)}, bf16[4,16,128]{2,1,0:T(8,128)(2,1)S(1)}, u32[]{:S(2)}, u32[]{:S(2)}) collective-permute-start(bf16[4,16,128]{2,1,0:T(8,128)(2,1)S(1)} %pick.1), channel_id=1, source_target_pairs={{0,2},{2,0},{1,3},{3,1},{4,6},{6,4},{5,7},{7,5},{8,10},{10,8},{9,1... | collective-permute-start | bytes 49160 | tf_op jit(solution)/shard_map/ppermute | solution.py:206
  15.0 0.0 collective-permute-done.6.refs_4_
  15.0 0.0 collective-permute-done.3.refs_0_
  15.0 0.0 collective-permute-done.4.refs_2_
  15.0 0.0 collective-permute-done.5.refs_3_
  15.0 0.8 %collective-permute-done.1.near = bf16[4,16,128]{2,1,0:T(8,128)(2,1)S(1)} collective-permute-done((bf16[4,16,128]{2,1,0:T(8,128)(2,1)S(1)}, bf16[4,16,128]{2,1,0:T(8,128)(2,1)S(1)}, u32[]{:S(2)}, u32[]{:S(2)}) %collective-permute-start.1) | collective-permute-done | bytes 16416 | tf_op jit(solution)/shard_map/ppermute | solution.py:206
  15.9 3.9 %after.1 = f32[512,128]{1,0:T(8,128)} custom-call(s32[1,1,1,96]{3,2,1,0:T(1,128)} %own_in.3, s32[1,1,1,96]{3,2,1,0:T(1,128)} %peer_in.3, s32[1,1,1,96]{3,2,1,0:T(1,128)} %slot_in.3, s32[1,1,1,4,8]{4,3,2,1,0:T(4,128)} %send_in.3, f32[512,128]{1,0:T(8,128)} %bitcast.3, f32[1,32,128]{2,1,0:T(8,128)} %stiff_in.3, ...), custom_call_target="tpu_custom_call" | custom-call | tf_op jit(solution)/shard_map/after/pallas_call | solution.py:207
  (1 shorter events, 0.0 us)
Async XLA Ops:
  3.7 5.7 %collective-permute-start = (bf16[20,16,128]{2,1,0:T(8,128)(2,1)S(1)}, bf16[20,16,128]{2,1,0:T(8,128)(2,1)S(1)}, u32[]{:S(2)}, u32[]{:S(2)}) collective-permute-start(bf16[20,16,128]{2,1,0:T(8,128)(2,1)S(1)} %get-tuple-element.13), channel_id=1, source_target_pairs={{0,6},{2,4},{4,2},{6,0},{8,14},{10,12},{12,10},{14,8},{1,7},{3,5},... | collective-permute-start | bytes 245768 | tf_op jit(solution)/shard_map/ppermute | solution.py:186
  5.6 9.4 %collective-permute-start.3 = (bf16[16,16,128]{2,1,0:T(8,128)(2,1)S(1)}, bf16[16,16,128]{2,1,0:T(8,128)(2,1)S(1)}, u32[]{:S(2)}, u32[]{:S(2)}) collective-permute-start(bf16[16,16,128]{2,1,0:T(8,128)(2,1)S(1)} %get-tuple-element.15), channel_id=1, source_target_pairs={{0,2},{2,0},{4,6},{6,4},{8,10},{10,8},{12,14},{14,12},{1,3},{3,1},... | collective-permute-start | bytes 196616 | tf_op jit(solution)/shard_map/ppermute | solution.py:186
  5.6 9.4 %collective-permute-start.4 = (bf16[16,16,128]{2,1,0:T(8,128)(2,1)S(1)}, bf16[16,16,128]{2,1,0:T(8,128)(2,1)S(1)}, u32[]{:S(2)}, u32[]{:S(2)}) collective-permute-start(bf16[16,16,128]{2,1,0:T(8,128)(2,1)S(1)} %get-tuple-element.16), channel_id=1, source_target_pairs={{0,10},{2,8},{4,14},{6,12},{8,2},{10,0},{12,6},{14,4},{1,11},{3,9}... | collective-permute-start | bytes 196616 | tf_op jit(solution)/shard_map/ppermute | solution.py:186
  6.1 9.0 %collective-permute-start.5 = (bf16[16,16,128]{2,1,0:T(8,128)(2,1)S(1)}, bf16[16,16,128]{2,1,0:T(8,128)(2,1)S(1)}, u32[]{:S(2)}, u32[]{:S(2)}) collective-permute-start(bf16[16,16,128]{2,1,0:T(8,128)(2,1)S(1)} %get-tuple-element.17), channel_id=1, source_target_pairs={{0,14},{2,12},{4,10},{6,8},{8,6},{10,4},{12,2},{14,0},{1,15},{3,13... | collective-permute-start | bytes 196616 | tf_op jit(solution)/shard_map/ppermute | solution.py:186
  7.3 6.9 %collective-permute-start.2 = (bf16[4,16,128]{2,1,0:T(8,128)(2,1)S(1)}, bf16[4,16,128]{2,1,0:T(8,128)(2,1)S(1)}, u32[]{:S(2)}, u32[]{:S(2)}) collective-permute-start(bf16[4,16,128]{2,1,0:T(8,128)(2,1)S(1)} %get-tuple-element.14), channel_id=1, source_target_pairs={{4,8},{8,4},{5,9},{9,5},{6,10},{10,6},{7,11},{11,7},{20,24},{24,20... | collective-permute-start | bytes 49160 | tf_op jit(solution)/shard_map/ppermute | solution.py:197
  9.4 5.6 %collective-permute-start.6 = (f32[32,128]{1,0:T(8,128)S(1)}, f32[32,128]{1,0:T(8,128)S(1)}, u32[]{:S(2)}, u32[]{:S(2)}) collective-permute-start(f32[32,128]{1,0:T(8,128)S(1)} %get-tuple-element.18), channel_id=1, source_target_pairs={{0,1},{1,0},{2,3},{3,2},{4,5},{5,4},{6,7},{7,6},{8,9},{9,8},{10,11... | collective-permute-start | bytes 49160 | tf_op jit(solution)/shard_map/ppermute | solution.py:190
  14.1 1.7 %collective-permute-start.1 = (bf16[4,16,128]{2,1,0:T(8,128)(2,1)S(1)}, bf16[4,16,128]{2,1,0:T(8,128)(2,1)S(1)}, u32[]{:S(2)}, u32[]{:S(2)}) collective-permute-start(bf16[4,16,128]{2,1,0:T(8,128)(2,1)S(1)} %pick.1), channel_id=1, source_target_pairs={{0,2},{2,0},{1,3},{3,1},{4,6},{6,4},{5,7},{7,5},{8,10},{10,8},{9,1... | collective-permute-start | bytes 49160 | tf_op jit(solution)/shard_map/ppermute | solution.py:206

commit v2 on v1

v2 whole, which is shorter than its diff:
```python
import functools

import jax
import jax.numpy as jnp
from jax import lax
from jax.experimental import pallas as pl
from jax.experimental.pallas import tpu as pltpu
from jax.sharding import PartitionSpec as P

helm_shift = 1.0
PIECES = 3
VMEM = pl.BlockSpec(memory_space=pltpu.VMEM)
ANY = pl.BlockSpec(memory_space=pl.ANY)
HBM = pl.BlockSpec(memory_space=pltpu.HBM)


def has_halo(k):
    return k > 0 and k & (k + 1) == 0


def pieces(x):
    high = x.astype(jnp.bfloat16)
    return high, (x - high.astype(jnp.float32)).astype(jnp.bfloat16)


def whole(high, low):
    return high.astype(jnp.float32) + low.astype(jnp.float32)


def pair_dot(a, b, blocks):
    none = jnp.zeros_like(a)
    rows = jnp.concatenate([jnp.concatenate([a, none], 1), jnp.concatenate([none, b], 1)], 0)
    both = jnp.dot(rows, blocks.reshape(2 * blocks.shape[1], -1), preferred_element_type=jnp.float32)
    return both[: a.shape[0]], both[a.shape[0] :]


def load(sources, targets, sems):
    copies = [pltpu.make_async_copy(a, b, sems.at[i]) for i, (a, b) in enumerate(zip(sources, targets))]
    for copy in copies:
        copy.start()
    return copies


def before(doms, slots, rows, own_in, peer_in, slot_in, send_in, modes_in, stiff_in, coupling, *refs):
    outs, (column, blocks, modes, stiff) = refs[:doms], refs[doms : doms + 4]
    own, peer, slot, send, tiles, sums, sems, block_sems = refs[doms + 4 :]
    sources = (own_in, peer_in, slot_in, send_in, modes_in, stiff_in)
    copies = load(sources, (own, peer, slot, send, modes, stiff), sems)
    half = blocks.shape[0] // 2
    parts = [pl.ds(0, half), pl.ds(half, half)]
    block_copies = load([coupling.at[0, 0, 0, part] for part in parts], [blocks.at[part] for part in parts], block_sems)
    d = lax.axis_index("dom")
    count, cells = tiles.shape[1:]
    sums[...] = jnp.zeros_like(sums)
    for copy in copies:
        copy.wait()
    for r in range(rows):
        tiles[r] = modes[pl.ds(r, count, stride=rows), :].astype(jnp.bfloat16)

    for k in filter(has_halo, range(doms)):
        row = jnp.where(d ^ k > d, rows - 1, 0)
        edge = modes[pl.ds(row, count, stride=rows), :]
        for i, piece in enumerate(pieces(edge)):
            outs[k][2 * slots + i] = piece
        edge = jnp.broadcast_to(stiff[0, pl.ds(row, 1), :], edge.shape)
        line = lax.broadcasted_iota(jnp.int32, edge.shape, 0)
        high, low = (p.astype(jnp.float32) for p in pieces(edge))
        outs[k][2 * slots + 2] = jnp.where(line == 0, high, low).astype(jnp.bfloat16)
    for k in range(doms):
        for j in range(slots):
            outs[k][j] = tiles[send[0, 0, 0, d ^ k, j]]
    lane = lax.broadcasted_iota(jnp.int32, (rows, cells), 1)
    ends = [jnp.zeros((rows, cells), jnp.float32)] * 2
    for m in range(count + 1):
        here = stiff[0] if m == count else modes[m * rows : (m + 1) * rows, :]
        ends = [jnp.where(lane == m, end, packed) for end, packed in zip((here[:, :1], here[:, -1:]), ends)]
    for side in range(2):
        column[side] = ends[side]
    for c, copy in enumerate(block_copies):
        copy.wait()
        for p in range(c * half, (c + 1) * half, 2):
            terms = pair_dot(tiles[own[0, 0, 0, p]], tiles[own[0, 0, 0, p + 1]], blocks[p : p + 2])
            for q, term in zip((p, p + 1), terms):
                sums[peer[0, 0, 0, q] * slots + slot[0, 0, 0, q]] += term
    for k in range(doms):
        for j in range(slots):
            outs[k][slots + j] = sums[(d ^ k) * slots + j].astype(jnp.bfloat16)


def turn(slots, own_in, peer_in, slot_in, send_in, blocks, turned, table, own, peer, slot, send, sems):
    copies = load((own_in, peer_in, slot_in, send_in), (own, peer, slot, send), sems)
    for p in range(blocks.shape[0]):
        turned[p] = blocks[p].T
    for copy in copies:
        copy.wait()
    pairs, (doms, caps) = own.shape[-1], send.shape[-2:]
    table[...] = jnp.zeros_like(table)
    table[0:1, :pairs] = own[0, 0]
    table[1:2, :pairs] = peer[0, 0] * slots + slot[0, 0]
    table[2 : 2 + doms, :caps] = send[0, 0, 0]


def pick(doms, slots, *refs):
    arrived, halo = dict(zip(filter(has_halo, exchange(doms)), refs)), refs[-1]
    d = lax.axis_index("dom")
    halo[...] = jnp.zeros_like(halo)
    for k, ref in arrived.items():
        for side, step in enumerate((-1, 1)):

            @pl.when(d ^ k == d + step)
            def _():
                halo[side] = ref[2 * slots : 2 * slots + PIECES]


def couple(doms, slots, subs, table_in, modes, stiff, turned, *refs):
    arrived, columns = dict(zip(exchange(doms), refs)), refs[doms:-5]
    total, table, foreign, back, sem = refs[-5:]
    rows = stiff.shape[1]
    copy = pltpu.make_async_copy(table_in, table, sem)
    copy.start()
    d = lax.axis_index("dom")
    s = lax.axis_index("sub")
    shift = helm_shift * lax.axis_index("mesh").astype(jnp.float32)
    count, cells = foreign.shape[1:]
    for k in range(doms):
        for j in range(slots):
            foreign[(d ^ k) * slots + j] = arrived[k][j]
            back[(d ^ k) * slots + j] = arrived[k][slots + j].astype(jnp.float32)
    lane = lax.broadcasted_iota(jnp.int32, (rows, cells), 1)
    line = lax.broadcasted_iota(jnp.int32, (rows, cells), 0)
    first_lane, last_lane = lane == 0, lane == cells - 1
    first_line, last_line = line == 0, line == rows - 1
    if subs == 1:
        left = right = jnp.zeros(lane.shape, jnp.float32)
    elif subs == 2:
        left, right = jnp.where(s == 1, columns[0][1], 0.0), jnp.where(s == 0, columns[0][0], 0.0)
    else:
        left, right = columns[0][1], columns[1][0]

    def near_by(here, m):
        return (
            jnp.where(first_line, here, pltpu.roll(here, 1, 0)),
            jnp.where(last_line, here, pltpu.roll(here, rows - 1, 0)),
            jnp.where(first_lane, left[:, m : m + 1], pltpu.roll(here, 1, 1)),
            jnp.where(last_lane, right[:, m : m + 1], pltpu.roll(here, cells - 1, 1)),
        )

    weights = [0.5 * (stiff[0] + near) for near in near_by(stiff[0], count)]
    for m in range(count):
        here = modes[m * rows : (m + 1) * rows, :]
        result = -shift * here
        for weight, near in zip(weights, near_by(here, m)):
            result = result + weight * (here - near)
        total[pl.ds(m, rows, stride=count), :] = result
    copy.wait()

    def subtract(row, term):
        part = pl.ds(pl.multiple_of(row * count, count), count)
        total[part, :] -= term

    for g in range(doms):
        for j in range(slots):
            subtract(table[2 + g, j], back[g * slots + j])
    for p in range(0, turned.shape[0], 2):
        first, second = (foreign[table[1, q]] for q in (p, p + 1))
        for q, term in zip((p, p + 1), pair_dot(first, second, turned[p : p + 2])):
            subtract(table[0, q], term)


def finish(total, modes, stiff, halo, out):
    rows = stiff.shape[1]
    count = total.shape[0] // rows
    for m in range(count):
        out[m * rows : (m + 1) * rows, :] = total[pl.ds(m, rows, stride=count), :]
    for side, row in enumerate((0, rows - 1)):
        here = modes[pl.ds(row, count, stride=rows), :]
        near = whole(halo[side, 0], halo[side, 1])
        weight = 0.5 * (stiff[0, row : row + 1, :] + whole(halo[side, 2, 0:1], halo[side, 2, 1:2]))
        out[pl.ds(row, count, stride=rows), :] = total[row * count : (row + 1) * count, :] + weight * (here - near)


def exchange(doms):
    if doms == 4:
        return [3, 1, 2, 0]
    return list(range(doms))


def shards(doms, subs, modes_in, stiffness, coupling, pair_own, pair_peer, pair_slot, send_rows):
    _, count, rows, cells = modes_in.shape
    slots, pairs = send_rows.shape[-1], coupling.shape[3]
    flat = modes_in.reshape(count * rows, cells)
    inputs = (pair_own, pair_peer, pair_slot, send_rows, flat, stiffness, coupling)
    *inputs, coupling = [pltpu.with_memory_space_constraint(a, pltpu.HBM) for a in inputs]
    params = pltpu.CompilerParams(vmem_limit_bytes=32 * 1024 * 1024)
    like = jax.ShapeDtypeStruct
    indices = inputs[:4]
    *outgoing, column, blocks, modes, stiff = pl.pallas_call(
        functools.partial(before, doms, slots, rows),
        out_shape=[like((2 * slots + PIECES * has_halo(k), count, cells), jnp.bfloat16) for k in range(doms)]
        + [
            like((2, rows, cells), jnp.float32),
            like((pairs, cells, cells), jnp.bfloat16),
            like(flat.shape, jnp.float32),
            like(stiffness.shape, jnp.float32),
        ],
        in_specs=[HBM] * 7,
        out_specs=[VMEM] * (doms + 4),
        scratch_shapes=[pltpu.SMEM(a.shape, a.dtype) for a in indices]
        + [
            pltpu.VMEM((rows, count, cells), jnp.bfloat16),
            pltpu.VMEM((doms * slots, count, cells), jnp.float32),
            pltpu.SemaphoreType.DMA((len(inputs),)),
            pltpu.SemaphoreType.DMA((2,)),
        ],
        compiler_params=params,
        name="before",
    )(*inputs, coupling)
    arrived = {}
    for k in exchange(doms):
        route = [(2 * d + h, 2 * (d ^ k) + 1 - h) for d in range(doms) for h in range(2)]
        arrived[k] = lax.ppermute(outgoing[k], ("dom", "mesh"), route)
    if subs == 1:
        columns = []
    elif subs == 2:
        columns = [lax.ppermute(column, "sub", [(0, 1), (1, 0)])]
    else:
        columns = [
            lax.ppermute(column, "sub", [(i, i + 1) for i in range(subs - 1)]),
            lax.ppermute(column, "sub", [(i + 1, i) for i in range(subs - 1)]),
        ]
    turned, table = pl.pallas_call(
        functools.partial(turn, slots),
        out_shape=[like(blocks.shape, blocks.dtype), like((-(-(2 + doms) // 8) * 8, cells), jnp.int32)],
        in_specs=[HBM] * 4 + [VMEM],
        out_specs=[VMEM] * 2,
        scratch_shapes=[pltpu.VMEM(a.shape, a.dtype) for a in indices] + [pltpu.SemaphoreType.DMA((4,))],
        compiler_params=params,
        cost_estimate=pl.CostEstimate(flops=0, bytes_accessed=8 << 20, transcendentals=0),
        name="turn",
    )(*indices, blocks)
    halo = pl.pallas_call(
        functools.partial(pick, doms, slots),
        out_shape=like((2, PIECES, count, cells), jnp.bfloat16),
        in_specs=[VMEM] * sum(map(has_halo, range(doms))) + [ANY],
        out_specs=VMEM,
        compiler_params=params,
        name="pick",
    )(*(arrived[k] for k in exchange(doms) if has_halo(k)), turned)
    halo = lax.ppermute(halo, "mesh", [(0, 1), (1, 0)])
    total = pl.pallas_call(
        functools.partial(couple, doms, slots, subs),
        out_shape=like((rows * count, cells), jnp.float32),
        in_specs=[VMEM] * (4 + doms + len(columns)),
        out_specs=VMEM,
        scratch_shapes=[
            pltpu.SMEM(table.shape, table.dtype),
            pltpu.VMEM((doms * slots, count, cells), jnp.bfloat16),
            pltpu.VMEM((doms * slots, count, cells), jnp.float32),
            pltpu.SemaphoreType.DMA,
        ],
        compiler_params=params,
        cost_estimate=pl.CostEstimate(flops=0, bytes_accessed=8 << 20, transcendentals=0),
        name="couple",
    )(table, modes, stiff, turned, *(arrived[k] for k in exchange(doms)), *columns)
    out = pl.pallas_call(
        finish,
        out_shape=like(flat.shape, jnp.float32),
        in_specs=[VMEM] * 4,
        out_specs=VMEM,
        compiler_params=params,
        name="finish",
    )(total, modes, stiff, halo)
    return out.reshape(modes_in.shape)


def solution(mesh):
    return jax.shard_map(
        functools.partial(shards, mesh.shape["dom"], mesh.shape["sub"]),
        mesh=mesh,
        in_specs=(
            P("mesh", "copies", "dom", "sub"),
            P(("copies", "mesh"), "dom", "sub"),
            P("mesh", "dom", "sub", None, None, None),
            P("mesh", "dom", "sub", None),
            P("mesh", "dom", "sub", None),
            P("mesh", "dom", "sub", None),
            P("mesh", "dom", "sub", None, None),
        ),
        out_specs=P("mesh", "copies", "dom", "sub"),
        check_vma=False,
    )
```

time: 20 us -> 16 us (0.80)
  the two profiles are of different devices: /device:TPU:19 before, /device:TPU:1 now
where the time goes in v2:
time: 16 us; the launch traced here: 15.8 us
  starting transfers between devices  6.98 us (44%)
  Pallas kernels  5.63 us (35%)
  waiting for transfers between devices  3.16 us (20%)
    ppermute x4, starting transfers between devices, shards(): arrived[k] = lax.ppermute(outgoing[k], ('dom', 'mesh'), route)  5.53 us
    ppermute x4, waiting for transfers between devices, shards(): arrived[k] = lax.ppermute(outgoing[k], ('dom', 'mesh'), route)  3.16 us
    pallas_call x1, Pallas kernels, shards(): pl.pallas_call(functools.partial(before, doms, slots, rows), out_shape=[l...  2.54 us
    pallas_call x1, Pallas kernels, shards(): pl.pallas_call(functools.partial(couple, doms, slots, subs), out_shape=li...  1.37 us
    ppermute x1, starting transfers between devices, shards(): columns = [lax.ppermute(column, 'sub', [(0, 1), (1, 0)])]  1.21 us
    pallas_call x1, Pallas kernels, shards(): pl.pallas_call(functools.partial(turn, slots), out_shape=[like(blocks.sha...  0.91 us
    pallas_call x1, Pallas kernels, shards(): pl.pallas_call(finish, out_shape=like(flat.shape, jnp.float32), in_specs=...  0.81 us
  transfers between devices with their start and end apart: 6, of which 2 were waited for; matrix products, arithmetic and copies ran while one was open for 0% of the time, Pallas kernels for 14%

profile of v2, /device:TPU:1, one launch (start us, length us, event | category | flops | bytes accessed | tf_op | source)
XLA Modules:
  0.0 15.8 jit_solution(6839130820579120783)
XLA Ops:
  0.0 2.5 %before.1 = (bf16[16,16,128]{2,1,0:T(8,128)(2,1)S(1)}, bf16[19,16,128]{2,1,0:T(8,128)(2,1)S(1)}, bf16[16,16,128]{2,1,0:T(8,128)(2,1)S(1)}, bf16[19,16,128]{2,1,0...) custom-call(s32[1,1,1,96]{3,2,1,0:T(1,128)} %own_in.3, ...), custom_call_target="tpu_custom_call" | custom-call | tf_op jit(solution)/shard_map/before/pallas_call | solution.py:197
  2.5 4.8 %collective-permute-start = (bf16[19,16,128]{2,1,0:T(8,128)(2,1)S(1)}, bf16[19,16,128]{2,1,0:T(8,128)(2,1)S(1)}, u32[]{:S(2)}, u32[]{:S(2)}) collective-permute-start(bf16[19,16,128]{2,1,0:T(8,128)(2,1)S(1)} %get-tuple-element.20), channel_id=1, source_target_pairs={{0,14},{2,12},{4,10},{6,8},{8,6},{10,4},{12,2},{14,0},{1,15},{3,13... | collective-permute-start | bytes 233480 | tf_op jit(solution)/shard_map/ppermute | solution.py:221
  7.3 0.0 collective-permute-start.1
  7.3 0.1 collective-permute-start.2
  7.4 0.7 %collective-permute-start.3 = (bf16[16,16,128]{2,1,0:T(8,128)(2,1)S(1)}, bf16[16,16,128]{2,1,0:T(8,128)(2,1)S(1)}, u32[]{:S(2)}, u32[]{:S(2)}) collective-permute-start(bf16[16,16,128]{2,1,0:T(8,128)(2,1)S(1)} %get-tuple-element.23), channel_id=1, source_target_pairs={{0,2},{2,0},{4,6},{6,4},{8,10},{10,8},{12,14},{14,12},{1,3},{3,1},... | collective-permute-start | bytes 196616 | tf_op jit(solution)/shard_map/ppermute | solution.py:221
  8.1 1.2 %collective-permute-start.4 = (f32[2,32,128]{2,1,0:T(8,128)S(1)}, f32[2,32,128]{2,1,0:T(8,128)S(1)}, u32[]{:S(2)}, u32[]{:S(2)}) collective-permute-start(f32[2,32,128]{2,1,0:T(8,128)S(1)} %get-tuple-element.24), channel_id=1, source_target_pairs={{0,1},{1,0},{2,3},{3,2},{4,5},{5,4},{6,7},{7,6},{8,9},{9,8},{10,11... | collective-permute-start | bytes 98312 | tf_op jit(solution)/shard_map/ppermute | solution.py:225
  9.3 0.9 %turn.1 = (bf16[96,128,128]{2,1,0:T(8,128)(2,1)S(1)}, s32[8,128]{1,0:T(8,128)S(1)}) custom-call(s32[1,1,1,96]{3,2,1,0:T(1,128)} %own_in.3, s32[1,1,1,96]{3,2,1,0:T(1,128)} %peer_in.3, s32[1,1,1,96]{3,2,1,0:T(1,128)} %slot_in.3, s32[1,1,1,4,8]{4,3,2,1,0:T(4,128)} %send_in.3, bf16[96,128,128]{2,1,0:T(8,128)(2,1)S(1)} %get-tuple-element.15.blocks), custom_call_target="tpu_custom_call" | custom-call | bytes 8388608 | tf_op jit(solution)/shard_map/turn/pallas_call | solution.py:231
  10.2 0.0 collective-permute-done.refs_0_
  10.2 2.7 %collective-permute-done.1.refs_1_ = bf16[19,16,128]{2,1,0:T(8,128)(2,1)S(1)} collective-permute-done((bf16[19,16,128]{2,1,0:T(8,128)(2,1)S(1)}, bf16[19,16,128]{2,1,0:T(8,128)(2,1)S(1)}, u32[]{:S(2)}, u32[]{:S(2)}) %collective-permute-start.1) | collective-permute-done | bytes 77856 | tf_op jit(solution)/shard_map/ppermute | solution.py:221
  12.9 0.2 %collective-permute-start.5 = (bf16[2,3,16,128]{3,2,1,0:T(8,128)(2,1)S(1)}, bf16[2,3,16,128]{3,2,1,0:T(8,128)(2,1)S(1)}, u32[]{:S(2)}, u32[]{:S(2)}) collective-permute-start(bf16[2,3,16,128]{3,2,1,0:T(8,128)(2,1)S(1)} %pick.1), channel_id=1, source_target_pairs={{0,2},{2,0},{1,3},{3,1},{4,6},{6,4},{5,7},{7,5},{8,10},{10,8},{9,1... | collective-permute-start | bytes 73736 | tf_op jit(solution)/shard_map/ppermute | solution.py:249
  13.1 0.0 collective-permute-done.4.refs_4_
  13.1 0.5 %collective-permute-done.2.refs_2_ = bf16[16,16,128]{2,1,0:T(8,128)(2,1)S(1)} collective-permute-done((bf16[16,16,128]{2,1,0:T(8,128)(2,1)S(1)}, bf16[16,16,128]{2,1,0:T(8,128)(2,1)S(1)}, u32[]{:S(2)}, u32[]{:S(2)}) %collective-permute-start.2) | collective-permute-done | bytes 65568 | tf_op jit(solution)/shard_map/ppermute | solution.py:221
  13.6 0.0 collective-permute-done.3.refs_3_
  13.6 1.4 %couple.1.total = f32[512,128]{1,0:T(8,128)S(1)} custom-call(s32[8,128]{1,0:T(8,128)S(1)} %get-tuple-element.16.table_in, f32[512,128]{1,0:T(8,128)S(1)} %get-tuple-element.17.modes, f32[1,32,128]{2,1,0:T(8,128)S(1)} %get-tuple-element.18.stiff, bf16[96,128,128]{2,1,0:T(8,128)(2,1)S(1)} %get-tuple-element.19.turned.refs_2_, ...), custom_call_target="tpu_custom_call" | custom-call | bytes 8388608 | tf_op jit(solution)/shard_map/couple/pallas_call | solution.py:250
  15.0 0.0 collective-permute-done.5.halo
  15.0 0.8 %finish.1 = f32[512,128]{1,0:T(8,128)} custom-call(f32[512,128]{1,0:T(8,128)S(1)} %couple.1.total, f32[512,128]{1,0:T(8,128)S(1)} %get-tuple-element.17.modes, f32[1,32,128]{2,1,0:T(8,128)S(1)} %get-tuple-element.18.stiff, bf16[2,3,16,128]{3,2,1,0:T(8,128)(2,1)S(1)} %collective-permute-done.5.halo), custom_call_target="tpu_custom_call" | custom-call | tf_op jit(solution)/shard_map/finish/pallas_call | solution.py:265
  (1 shorter events, 0.0 us)
Async XLA Ops:
  2.5 7.7 %collective-permute-start = (bf16[19,16,128]{2,1,0:T(8,128)(2,1)S(1)}, bf16[19,16,128]{2,1,0:T(8,128)(2,1)S(1)}, u32[]{:S(2)}, u32[]{:S(2)}) collective-permute-start(bf16[19,16,128]{2,1,0:T(8,128)(2,1)S(1)} %get-tuple-element.20), channel_id=1, source_target_pairs={{0,14},{2,12},{4,10},{6,8},{8,6},{10,4},{12,2},{14,0},{1,15},{3,13... | collective-permute-start | bytes 233480 | tf_op jit(solution)/shard_map/ppermute | solution.py:221
  7.3 5.6 %collective-permute-start.1 = (bf16[19,16,128]{2,1,0:T(8,128)(2,1)S(1)}, bf16[19,16,128]{2,1,0:T(8,128)(2,1)S(1)}, u32[]{:S(2)}, u32[]{:S(2)}) collective-permute-start(bf16[19,16,128]{2,1,0:T(8,128)(2,1)S(1)} %get-tuple-element.21), channel_id=1, source_target_pairs={{0,6},{2,4},{4,2},{6,0},{8,14},{10,12},{12,10},{14,8},{1,7},{3,5},... | collective-permute-start | bytes 233480 | tf_op jit(solution)/shard_map/ppermute | solution.py:221
  7.3 6.3 %collective-permute-start.2 = (bf16[16,16,128]{2,1,0:T(8,128)(2,1)S(1)}, bf16[16,16,128]{2,1,0:T(8,128)(2,1)S(1)}, u32[]{:S(2)}, u32[]{:S(2)}) collective-permute-start(bf16[16,16,128]{2,1,0:T(8,128)(2,1)S(1)} %get-tuple-element.22), channel_id=1, source_target_pairs={{0,10},{2,8},{4,14},{6,12},{8,2},{10,0},{12,6},{14,4},{1,11},{3,9}... | collective-permute-start | bytes 196616 | tf_op jit(solution)/shard_map/ppermute | solution.py:221
  7.4 6.2 %collective-permute-start.3 = (bf16[16,16,128]{2,1,0:T(8,128)(2,1)S(1)}, bf16[16,16,128]{2,1,0:T(8,128)(2,1)S(1)}, u32[]{:S(2)}, u32[]{:S(2)}) collective-permute-start(bf16[16,16,128]{2,1,0:T(8,128)(2,1)S(1)} %get-tuple-element.23), channel_id=1, source_target_pairs={{0,2},{2,0},{4,6},{6,4},{8,10},{10,8},{12,14},{14,12},{1,3},{3,1},... | collective-permute-start | bytes 196616 | tf_op jit(solution)/shard_map/ppermute | solution.py:221
  8.1 5.1 %collective-permute-start.4 = (f32[2,32,128]{2,1,0:T(8,128)S(1)}, f32[2,32,128]{2,1,0:T(8,128)S(1)}, u32[]{:S(2)}, u32[]{:S(2)}) collective-permute-start(f32[2,32,128]{2,1,0:T(8,128)S(1)} %get-tuple-element.24), channel_id=1, source_target_pairs={{0,1},{1,0},{2,3},{3,2},{4,5},{5,4},{6,7},{7,6},{8,9},{9,8},{10,11... | collective-permute-start | bytes 98312 | tf_op jit(solution)/shard_map/ppermute | solution.py:225
  12.9 2.1 %collective-permute-start.5 = (bf16[2,3,16,128]{3,2,1,0:T(8,128)(2,1)S(1)}, bf16[2,3,16,128]{3,2,1,0:T(8,128)(2,1)S(1)}, u32[]{:S(2)}, u32[]{:S(2)}) collective-permute-start(bf16[2,3,16,128]{3,2,1,0:T(8,128)(2,1)S(1)} %pick.1), channel_id=1, source_target_pairs={{0,2},{2,0},{1,3},{3,1},{4,6},{6,4},{5,7},{7,5},{8,10},{10,8},{9,1... | collective-permute-start | bytes 73736 | tf_op jit(solution)/shard_map/ppermute | solution.py:249

commit v3 on v2

--- a/solution.py
+++ b/solution.py
@@ -9,6 +9,7 @@
 
 helm_shift = 1.0
 PIECES = 3
+SMEM = pl.BlockSpec(memory_space=pltpu.SMEM)
 VMEM = pl.BlockSpec(memory_space=pltpu.VMEM)
 ANY = pl.BlockSpec(memory_space=pl.ANY)
 HBM = pl.BlockSpec(memory_space=pltpu.HBM)
@@ -34,10 +35,10 @@
     return both[: a.shape[0]], both[a.shape[0] :]
 
 
-def load(sources, targets, sems):
+def load(sources, targets, sems, priority=0):
     copies = [pltpu.make_async_copy(a, b, sems.at[i]) for i, (a, b) in enumerate(zip(sources, targets))]
     for copy in copies:
-        copy.start()
+        copy.start(priority=priority)
     return copies
 
 
@@ -48,7 +49,7 @@
     copies = load(sources, (own, peer, slot, send, modes, stiff), sems)
     half = blocks.shape[0] // 2
     parts = [pl.ds(0, half), pl.ds(half, half)]
-    block_copies = load([coupling.at[0, 0, 0, part] for part in parts], [blocks.at[part] for part in parts], block_sems)
+    block_copies = load([coupling.at[0, 0, 0, part] for part in parts], [blocks.at[part] for part in parts], block_sems, 1)
     d = lax.axis_index("dom")
     count, cells = tiles.shape[1:]
     sums[...] = jnp.zeros_like(sums)
@@ -87,49 +88,21 @@
             outs[k][slots + j] = sums[(d ^ k) * slots + j].astype(jnp.bfloat16)
 
 
-def turn(slots, own_in, peer_in, slot_in, send_in, blocks, turned, table, own, peer, slot, send, sems):
-    copies = load((own_in, peer_in, slot_in, send_in), (own, peer, slot, send), sems)
+def turn(blocks, turned):
     for p in range(blocks.shape[0]):
         turned[p] = blocks[p].T
-    for copy in copies:
-        copy.wait()
-    pairs, (doms, caps) = own.shape[-1], send.shape[-2:]
-    table[...] = jnp.zeros_like(table)
-    table[0:1, :pairs] = own[0, 0]
-    table[1:2, :pairs] = peer[0, 0] * slots + slot[0, 0]
-    table[2 : 2 + doms, :caps] = send[0, 0, 0]
-
-
-def pick(doms, slots, *refs):
-    arrived, halo = dict(zip(filter(has_halo, exchange(doms)), refs)), refs[-1]
-    d = lax.axis_index("dom")
-    halo[...] = jnp.zeros_like(halo)
-    for k, ref in arrived.items():
-        for side, step in enumerate((-1, 1)):
-
-            @pl.when(d ^ k == d + step)
-            def _():
-                halo[side] = ref[2 * slots : 2 * slots + PIECES]
-
-
-def couple(doms, slots, subs, table_in, modes, stiff, turned, *refs):
-    arrived, columns = dict(zip(exchange(doms), refs)), refs[doms:-5]
-    total, table, foreign, back, sem = refs[-5:]
-    rows = stiff.shape[1]
-    copy = pltpu.make_async_copy(table_in, table, sem)
-    copy.start()
-    d = lax.axis_index("dom")
-    s = lax.axis_index("sub")
+
+
+def stencil(subs, modes, stiff, *refs):
+    columns, total = refs[:-1], refs[-1]
+    rows, cells = stiff.shape[1:]
+    count = modes.shape[0] // rows
     shift = helm_shift * lax.axis_index("mesh").astype(jnp.float32)
-    count, cells = foreign.shape[1:]
-    for k in range(doms):
-        for j in range(slots):
-            foreign[(d ^ k) * slots + j] = arrived[k][j]
-            back[(d ^ k) * slots + j] = arrived[k][slots + j].astype(jnp.float32)
     lane = lax.broadcasted_iota(jnp.int32, (rows, cells), 1)
     line = lax.broadcasted_iota(jnp.int32, (rows, cells), 0)
     first_lane, last_lane = lane == 0, lane == cells - 1
     first_line, last_line = line == 0, line == rows - 1
+    s = lax.axis_index("sub")
     if subs == 1:
         left = right = jnp.zeros(lane.shape, jnp.float32)
     elif subs == 2:
@@ -152,7 +125,28 @@
         for weight, near in zip(weights, near_by(here, m)):
             result = result + weight * (here - near)
         total[pl.ds(m, rows, stride=count), :] = result
-    copy.wait()
+
+
+def pick(doms, slots, *refs):
+    arrived, halo = dict(zip(filter(has_halo, exchange(doms)), refs)), refs[-1]
+    d = lax.axis_index("dom")
+    halo[...] = jnp.zeros_like(halo)
+    for k, ref in arrived.items():
+        for side, step in enumerate((-1, 1)):
+
+            @pl.when(d ^ k == d + step)
+            def _():
+                halo[side] = ref[2 * slots : 2 * slots + PIECES]
+
+
+def couple(doms, slots, own, peer, slot, send, turned, *refs):
+    arrived, (_, total, foreign, back) = dict(zip(exchange(doms), refs)), refs[doms:]
+    count = foreign.shape[1]
+    d = lax.axis_index("dom")
+    for k in range(doms):
+        for j in range(slots):
+            foreign[(d ^ k) * slots + j] = arrived[k][j]
+            back[(d ^ k) * slots + j] = arrived[k][slots + j].astype(jnp.float32)
 
     def subtract(row, term):
         part = pl.ds(pl.multiple_of(row * count, count), count)
@@ -160,11 +154,11 @@
 
     for g in range(doms):
         for j in range(slots):
-            subtract(table[2 + g, j], back[g * slots + j])
+            subtract(send[0, 0, 0, g, j], back[g * slots + j])
     for p in range(0, turned.shape[0], 2):
-        first, second = (foreign[table[1, q]] for q in (p, p + 1))
+        first, second = (foreign[peer[0, 0, 0, q] * slots + slot[0, 0, 0, q]] for q in (p, p + 1))
         for q, term in zip((p, p + 1), pair_dot(first, second, turned[p : p + 2])):
-            subtract(table[0, q], term)
+            subtract(own[0, 0, 0, q], term)
 
 
 def finish(total, modes, stiff, halo, out):
@@ -194,7 +188,7 @@
     params = pltpu.CompilerParams(vmem_limit_bytes=32 * 1024 * 1024)
     like = jax.ShapeDtypeStruct
     indices = inputs[:4]
-    *outgoing, column, blocks, modes, stiff = pl.pallas_call(
+    *outgoing, column, blocks, modes, stiff, own, peer, slot, send = pl.pallas_call(
         functools.partial(before, doms, slots, rows),
         out_shape=[like((2 * slots + PIECES * has_halo(k), count, cells), jnp.bfloat16) for k in range(doms)]
         + [
@@ -202,11 +196,11 @@
             like((pairs, cells, cells), jnp.bfloat16),
             like(flat.shape, jnp.float32),
             like(stiffness.shape, jnp.float32),
-        ],
+        ]
+        + [pltpu.SMEM(a.shape, a.dtype) for a in indices],
         in_specs=[HBM] * 7,
-        out_specs=[VMEM] * (doms + 4),
-        scratch_shapes=[pltpu.SMEM(a.shape, a.dtype) for a in indices]
-        + [
+        out_specs=[VMEM] * (doms + 4) + [SMEM] * 4,
+        scratch_shapes=[
             pltpu.VMEM((rows, count, cells), jnp.bfloat16),
             pltpu.VMEM((doms * slots, count, cells), jnp.float32),
             pltpu.SemaphoreType.DMA((len(inputs),)),
@@ -215,6 +209,7 @@
         compiler_params=params,
         name="before",
     )(*inputs, coupling)
+    indices = [pltpu.with_memory_space_constraint(a, pltpu.SMEM) for a in (own, peer, slot, send)]
     arrived = {}
     for k in exchange(doms):
         route = [(2 * d + h, 2 * (d ^ k) + 1 - h) for d in range(doms) for h in range(2)]
@@ -228,40 +223,47 @@
             lax.ppermute(column, "sub", [(i, i + 1) for i in range(subs - 1)]),
             lax.ppermute(column, "sub", [(i + 1, i) for i in range(subs - 1)]),
         ]
-    turned, table = pl.pallas_call(
-        functools.partial(turn, slots),
-        out_shape=[like(blocks.shape, blocks.dtype), like((-(-(2 + doms) // 8) * 8, cells), jnp.int32)],
-        in_specs=[HBM] * 4 + [VMEM],
-        out_specs=[VMEM] * 2,
-        scratch_shapes=[pltpu.VMEM(a.shape, a.dtype) for a in indices] + [pltpu.SemaphoreType.DMA((4,))],
-        compiler_params=params,
-        cost_estimate=pl.CostEstimate(flops=0, bytes_accessed=8 << 20, transcendentals=0),
+    cost = pl.CostEstimate(flops=0, bytes_accessed=8 << 20, transcendentals=0)
+    turned = pl.pallas_call(
+        turn,
+        out_shape=like(blocks.shape, blocks.dtype),
+        in_specs=[VMEM],
+        out_specs=VMEM,
+        compiler_params=params,
+        cost_estimate=cost,
         name="turn",
-    )(*indices, blocks)
+    )(blocks)
+    partial = pl.pallas_call(
+        functools.partial(stencil, subs),
+        out_shape=like(flat.shape, jnp.float32),
+        in_specs=[VMEM] * (2 + len(columns)),
+        out_specs=VMEM,
+        compiler_params=params,
+        name="stencil",
+    )(modes, stiff, *columns)
     halo = pl.pallas_call(
         functools.partial(pick, doms, slots),
         out_shape=like((2, PIECES, count, cells), jnp.bfloat16),
-        in_specs=[VMEM] * sum(map(has_halo, range(doms))) + [ANY],
+        in_specs=[VMEM] * sum(map(has_halo, range(doms))) + [ANY] * 2,
         out_specs=VMEM,
         compiler_params=params,
         name="pick",
-    )(*(arrived[k] for k in exchange(doms) if has_halo(k)), turned)
+    )(*(arrived[k] for k in exchange(doms) if has_halo(k)), turned, partial)
     halo = lax.ppermute(halo, "mesh", [(0, 1), (1, 0)])
     total = pl.pallas_call(
-        functools.partial(couple, doms, slots, subs),
-        out_shape=like((rows * count, cells), jnp.float32),
-        in_specs=[VMEM] * (4 + doms + len(columns)),
+        functools.partial(couple, doms, slots),
+        out_shape=like(partial.shape, partial.dtype),
+        in_specs=[SMEM] * 4 + [VMEM] * (2 + doms),
         out_specs=VMEM,
         scratch_shapes=[
-            pltpu.SMEM(table.shape, table.dtype),
             pltpu.VMEM((doms * slots, count, cells), jnp.bfloat16),
             pltpu.VMEM((doms * slots, count, cells), jnp.float32),
-            pltpu.SemaphoreType.DMA,
         ],
-        compiler_params=params,
-        cost_estimate=pl.CostEstimate(flops=0, bytes_accessed=8 << 20, transcendentals=0),
+        input_output_aliases={5 + doms: 0},
+        compiler_params=params,
+        cost_estimate=cost,
         name="couple",
-    )(table, modes, stiff, turned, *(arrived[k] for k in exchange(doms)), *columns)
+    )(*indices, turned, *(arrived[k] for k in exchange(doms)), partial)
     out = pl.pallas_call(
         finish,
         out_shape=like(flat.shape, jnp.float32),

time: 16 us -> 15.3 us (0.956)
  the two profiles are of different devices: /device:TPU:1 before, /device:TPU:0 now
where the time goes in v3:
time: 15.3 us; the launch traced here: 15 us
  starting transfers between devices  7.5 us (49%)
  Pallas kernels  5.29 us (35%)
  waiting for transfers between devices  2.17 us (14%)
    ppermute x4, starting transfers between devices, shards(): arrived[k] = lax.ppermute(outgoing[k], ('dom', 'mesh'), route)  5.48 us
    pallas_call x1, Pallas kernels, shards(): pl.pallas_call(functools.partial(before, doms, slots, rows), out_shape=[l...  2.46 us
    ppermute x1, starting transfers between devices, shards(): columns = [lax.ppermute(column, 'sub', [(0, 1), (1, 0)])]  1.75 us
    ppermute x1, waiting for transfers between devices, shards(): columns = [lax.ppermute(column, 'sub', [(0, 1), (1, 0)])]  1.3 us
    pallas_call x1, Pallas kernels, shards(): pl.pallas_call(turn, out_shape=like(blocks.shape, blocks.dtype), in_specs...  0.86 us
    pallas_call x1, Pallas kernels, shards(): pl.pallas_call(finish, out_shape=like(flat.shape, jnp.float32), in_specs=...  0.81 us
    pallas_call x1, Pallas kernels, shards(): pl.pallas_call(functools.partial(couple, doms, slots), out_shape=like(par...  0.74 us
    ppermute x4, waiting for transfers between devices, shards(): arrived[k] = lax.ppermute(outgoing[k], ('dom', 'mesh'), route)  0.7 us
  transfers between devices with their start and end apart: 6, of which 3 were waited for; matrix products, arithmetic and copies ran while one was open for 0% of the time, Pallas kernels for 14%

profile of v3, /device:TPU:0, one launch (start us, length us, event | category | flops | bytes accessed | tf_op | source)
XLA Modules:
  0.0 15.0 jit_solution(800965238414830385)
XLA Ops:
  0.0 2.5 %before.1 = (bf16[16,16,128]{2,1,0:T(8,128)(2,1)S(1)}, bf16[19,16,128]{2,1,0:T(8,128)(2,1)S(1)}, bf16[16,16,128]{2,1,0:T(8,128)(2,1)S(1)}, bf16[19,16,128]{2,1,0...) custom-call(s32[1,1,1,96]{3,2,1,0:T(1,128)} %own_in.1, ...), custom_call_target="tpu_custom_call" | custom-call | tf_op jit(solution)/shard_map/before/pallas_call | solution.py:191
  2.5 4.6 %collective-permute-start = (bf16[19,16,128]{2,1,0:T(8,128)(2,1)S(1)}, bf16[19,16,128]{2,1,0:T(8,128)(2,1)S(1)}, u32[]{:S(2)}, u32[]{:S(2)}) collective-permute-start(bf16[19,16,128]{2,1,0:T(8,128)(2,1)S(1)} %get-tuple-element.22), channel_id=1, source_target_pairs={{0,14},{2,12},{4,10},{6,8},{8,6},{10,4},{12,2},{14,0},{1,15},{3,13... | collective-permute-start | bytes 233480 | tf_op jit(solution)/shard_map/ppermute | solution.py:216
  7.0 0.0 collective-permute-start.1
  7.0 0.9 %collective-permute-start.2 = (bf16[16,16,128]{2,1,0:T(8,128)(2,1)S(1)}, bf16[16,16,128]{2,1,0:T(8,128)(2,1)S(1)}, u32[]{:S(2)}, u32[]{:S(2)}) collective-permute-start(bf16[16,16,128]{2,1,0:T(8,128)(2,1)S(1)} %get-tuple-element.24), channel_id=1, source_target_pairs={{0,10},{2,8},{4,14},{6,12},{8,2},{10,0},{12,6},{14,4},{1,11},{3,9}... | collective-permute-start | bytes 196616 | tf_op jit(solution)/shard_map/ppermute | solution.py:216
  7.9 0.0 collective-permute-start.3
  7.9 1.8 %collective-permute-start.4 = (f32[2,32,128]{2,1,0:T(8,128)S(1)}, f32[2,32,128]{2,1,0:T(8,128)S(1)}, u32[]{:S(2)}, u32[]{:S(2)}) collective-permute-start(f32[2,32,128]{2,1,0:T(8,128)S(1)} %get-tuple-element.28), channel_id=1, source_target_pairs={{0,1},{1,0},{2,3},{3,2},{4,5},{5,4},{6,7},{7,6},{8,9},{9,8},{10,11... | collective-permute-start | bytes 98312 | tf_op jit(solution)/shard_map/ppermute | solution.py:220
  9.7 0.9 %turn.1.turned.refs_2_ = bf16[96,128,128]{2,1,0:T(8,128)(2,1)S(1)} custom-call(bf16[96,128,128]{2,1,0:T(8,128)(2,1)S(1)} %get-tuple-element.21.blocks), custom_call_target="tpu_custom_call" | custom-call | bytes 8388608 | tf_op jit(solution)/shard_map/turn/pallas_call | solution.py:227
  10.6 1.3 %collective-permute-done.4.refs_0_ = f32[2,32,128]{2,1,0:T(8,128)S(1)} collective-permute-done((f32[2,32,128]{2,1,0:T(8,128)S(1)}, f32[2,32,128]{2,1,0:T(8,128)S(1)}, u32[]{:S(2)}, u32[]{:S(2)}) %collective-permute-start.4) | collective-permute-done | bytes 32800 | tf_op jit(solution)/shard_map/ppermute | solution.py:220
  11.9 0.4 %stencil.1.refs_4_.refs_3_ = f32[512,128]{1,0:T(8,128)S(1)} custom-call(f32[512,128]{1,0:T(8,128)S(1)} %get-tuple-element.26.modes, f32[1,32,128]{2,1,0:T(8,128)S(1)} %get-tuple-element.27.stiff, f32[2,32,128]{2,1,0:T(8,128)S(1)} %collective-permute-done.4.refs_0_), custom_call_target="tpu_custom_call" | custom-call | tf_op jit(solution)/shard_map/stencil/pallas_call | solution.py:236
  12.3 0.0 collective-permute-done.refs_0_
  12.3 0.7 %collective-permute-done.1.refs_1_ = bf16[19,16,128]{2,1,0:T(8,128)(2,1)S(1)} collective-permute-done((bf16[19,16,128]{2,1,0:T(8,128)(2,1)S(1)}, bf16[19,16,128]{2,1,0:T(8,128)(2,1)S(1)}, u32[]{:S(2)}, u32[]{:S(2)}) %collective-permute-start.1) | collective-permute-done | bytes 77856 | tf_op jit(solution)/shard_map/ppermute | solution.py:216
  13.0 0.3 %collective-permute-start.5 = (bf16[2,3,16,128]{3,2,1,0:T(8,128)(2,1)S(1)}, bf16[2,3,16,128]{3,2,1,0:T(8,128)(2,1)S(1)}, u32[]{:S(2)}, u32[]{:S(2)}) collective-permute-start(bf16[2,3,16,128]{3,2,1,0:T(8,128)(2,1)S(1)} %pick.1), channel_id=1, source_target_pairs={{0,2},{2,0},{1,3},{3,1},{4,6},{6,4},{5,7},{7,5},{8,10},{10,8},{9,1... | collective-permute-start | bytes 73736 | tf_op jit(solution)/shard_map/ppermute | solution.py:252
  13.3 0.0 collective-permute-done.2.refs_2_
  13.3 0.0 collective-permute-done.3.refs_3_
  13.3 0.7 %couple.1.total = f32[512,128]{1,0:T(8,128)S(1)} custom-call(s32[1,1,1,96]{3,2,1,0:T(1,128)S(4)} %get-tuple-element.17.own, s32[1,1,1,96]{3,2,1,0:T(1,128)S(4)} %get-tuple-element.18.peer, s32[1,1,1,96]{3,2,1,0:T(1,128)S(4)} %get-tuple-element.19.slot, s32[1,1,1,4,8]{4,3,2,1,0:T(4,128)S(4)} %get-tuple-element.20.send, ...), custom_call_target="tpu_custom_call", output_to_operand_aliasing={{}: (9, {})} | custom-call | bytes 8388608 | tf_op jit(solution)/shard_map/couple/pallas_call | solution.py:253
  14.0 0.2 %collective-permute-done.5.halo = bf16[2,3,16,128]{3,2,1,0:T(8,128)(2,1)S(1)} collective-permute-done((bf16[2,3,16,128]{3,2,1,0:T(8,128)(2,1)S(1)}, bf16[2,3,16,128]{3,2,1,0:T(8,128)(2,1)S(1)}, u32[]{:S(2)}, u32[]{:S(2)}) %collective-permute-start.5) | collective-permute-done | bytes 24608 | tf_op jit(solution)/shard_map/ppermute | solution.py:252
  14.2 0.8 %finish.1 = f32[512,128]{1,0:T(8,128)} custom-call(f32[512,128]{1,0:T(8,128)S(1)} %couple.1.total, f32[512,128]{1,0:T(8,128)S(1)} %get-tuple-element.26.modes, f32[1,32,128]{2,1,0:T(8,128)S(1)} %get-tuple-element.27.stiff, bf16[2,3,16,128]{3,2,1,0:T(8,128)(2,1)S(1)} %collective-permute-done.5.halo), custom_call_target="tpu_custom_call" | custom-call | tf_op jit(solution)/shard_map/finish/pallas_call | solution.py:267
  (1 shorter events, 0.0 us)
Async XLA Ops:
  2.5 9.8 %collective-permute-start = (bf16[19,16,128]{2,1,0:T(8,128)(2,1)S(1)}, bf16[19,16,128]{2,1,0:T(8,128)(2,1)S(1)}, u32[]{:S(2)}, u32[]{:S(2)}) collective-permute-start(bf16[19,16,128]{2,1,0:T(8,128)(2,1)S(1)} %get-tuple-element.22), channel_id=1, source_target_pairs={{0,14},{2,12},{4,10},{6,8},{8,6},{10,4},{12,2},{14,0},{1,15},{3,13... | collective-permute-start | bytes 233480 | tf_op jit(solution)/shard_map/ppermute | solution.py:216
  7.0 6.0 %collective-permute-start.1 = (bf16[19,16,128]{2,1,0:T(8,128)(2,1)S(1)}, bf16[19,16,128]{2,1,0:T(8,128)(2,1)S(1)}, u32[]{:S(2)}, u32[]{:S(2)}) collective-permute-start(bf16[19,16,128]{2,1,0:T(8,128)(2,1)S(1)} %get-tuple-element.23), channel_id=1, source_target_pairs={{0,6},{2,4},{4,2},{6,0},{8,14},{10,12},{12,10},{14,8},{1,7},{3,5},... | collective-permute-start | bytes 233480 | tf_op jit(solution)/shard_map/ppermute | solution.py:216
  7.0 6.3 %collective-permute-start.2 = (bf16[16,16,128]{2,1,0:T(8,128)(2,1)S(1)}, bf16[16,16,128]{2,1,0:T(8,128)(2,1)S(1)}, u32[]{:S(2)}, u32[]{:S(2)}) collective-permute-start(bf16[16,16,128]{2,1,0:T(8,128)(2,1)S(1)} %get-tuple-element.24), channel_id=1, source_target_pairs={{0,10},{2,8},{4,14},{6,12},{8,2},{10,0},{12,6},{14,4},{1,11},{3,9}... | collective-permute-start | bytes 196616 | tf_op jit(solution)/shard_map/ppermute | solution.py:216
  7.9 5.3 %collective-permute-start.3 = (bf16[16,16,128]{2,1,0:T(8,128)(2,1)S(1)}, bf16[16,16,128]{2,1,0:T(8,128)(2,1)S(1)}, u32[]{:S(2)}, u32[]{:S(2)}) collective-permute-start(bf16[16,16,128]{2,1,0:T(8,128)(2,1)S(1)} %get-tuple-element.25), channel_id=1, source_target_pairs={{0,2},{2,0},{4,6},{6,4},{8,10},{10,8},{12,14},{14,12},{1,3},{3,1},... | collective-permute-start | bytes 196616 | tf_op jit(solution)/shard_map/ppermute | solution.py:216
  7.9 3.9 %collective-permute-start.4 = (f32[2,32,128]{2,1,0:T(8,128)S(1)}, f32[2,32,128]{2,1,0:T(8,128)S(1)}, u32[]{:S(2)}, u32[]{:S(2)}) collective-permute-start(f32[2,32,128]{2,1,0:T(8,128)S(1)} %get-tuple-element.28), channel_id=1, source_target_pairs={{0,1},{1,0},{2,3},{3,2},{4,5},{5,4},{6,7},{7,6},{8,9},{9,8},{10,11... | collective-permute-start | bytes 98312 | tf_op jit(solution)/shard_map/ppermute | solution.py:220
  13.0 1.2 %collective-permute-start.5 = (bf16[2,3,16,128]{3,2,1,0:T(8,128)(2,1)S(1)}, bf16[2,3,16,128]{3,2,1,0:T(8,128)(2,1)S(1)}, u32[]{:S(2)}, u32[]{:S(2)}) collective-permute-start(bf16[2,3,16,128]{3,2,1,0:T(8,128)(2,1)S(1)} %pick.1), channel_id=1, source_target_pairs={{0,2},{2,0},{1,3},{3,1},{4,6},{6,4},{5,7},{7,5},{8,10},{10,8},{9,1... | collective-permute-start | bytes 73736 | tf_op jit(solution)/shard_map/ppermute | solution.py:252

commit v4 on v3

--- a/solution.py
+++ b/solution.py
@@ -140,8 +140,9 @@
 
 
 def couple(doms, slots, own, peer, slot, send, turned, *refs):
-    arrived, (_, total, foreign, back) = dict(zip(exchange(doms), refs)), refs[doms:]
+    arrived, (_, total, out, foreign, back) = dict(zip(exchange(doms), refs)), refs[doms:]
     count = foreign.shape[1]
+    rows = total.shape[0] // count
     d = lax.axis_index("dom")
     for k in range(doms):
         for j in range(slots):
@@ -159,18 +160,22 @@
         first, second = (foreign[peer[0, 0, 0, q] * slots + slot[0, 0, 0, q]] for q in (p, p + 1))
         for q, term in zip((p, p + 1), pair_dot(first, second, turned[p : p + 2])):
             subtract(own[0, 0, 0, q], term)
-
-
-def finish(total, modes, stiff, halo, out):
-    rows = stiff.shape[1]
-    count = total.shape[0] // rows
     for m in range(count):
         out[m * rows : (m + 1) * rows, :] = total[pl.ds(m, rows, stride=count), :]
+
+
+def finish(modes, stiff, halo, _, result, out, sem):
+    rows = stiff.shape[1]
+    count = modes.shape[0] // rows
     for side, row in enumerate((0, rows - 1)):
-        here = modes[pl.ds(row, count, stride=rows), :]
+        line = pl.ds(row, count, stride=rows)
+        here = modes[line, :]
         near = whole(halo[side, 0], halo[side, 1])
         weight = 0.5 * (stiff[0, row : row + 1, :] + whole(halo[side, 2, 0:1], halo[side, 2, 1:2]))
-        out[pl.ds(row, count, stride=rows), :] = total[row * count : (row + 1) * count, :] + weight * (here - near)
+        result[line, :] += weight * (here - near)
+    copy = pltpu.make_async_copy(result, out, sem)
+    copy.start()
+    copy.wait()
 
 
 def exchange(doms):
@@ -250,11 +255,11 @@
         name="pick",
     )(*(arrived[k] for k in exchange(doms) if has_halo(k)), turned, partial)
     halo = lax.ppermute(halo, "mesh", [(0, 1), (1, 0)])
-    total = pl.pallas_call(
+    _, result = pl.pallas_call(
         functools.partial(couple, doms, slots),
-        out_shape=like(partial.shape, partial.dtype),
+        out_shape=[like(partial.shape, partial.dtype)] * 2,
         in_specs=[SMEM] * 4 + [VMEM] * (2 + doms),
-        out_specs=VMEM,
+        out_specs=[VMEM] * 2,
         scratch_shapes=[
             pltpu.VMEM((doms * slots, count, cells), jnp.bfloat16),
             pltpu.VMEM((doms * slots, count, cells), jnp.float32),
@@ -264,14 +269,16 @@
         cost_estimate=cost,
         name="couple",
     )(*indices, turned, *(arrived[k] for k in exchange(doms)), partial)
-    out = pl.pallas_call(
+    _, out = pl.pallas_call(
         finish,
-        out_shape=like(flat.shape, jnp.float32),
+        out_shape=[like(flat.shape, jnp.float32)] * 2,
         in_specs=[VMEM] * 4,
-        out_specs=VMEM,
+        out_specs=[VMEM, HBM],
+        scratch_shapes=[pltpu.SemaphoreType.DMA],
+        input_output_aliases={3: 0},
         compiler_params=params,
         name="finish",
-    )(total, modes, stiff, halo)
+    )(modes, stiff, halo, result)
     return out.reshape(modes_in.shape)
 
 

time: 15.3 us -> 15.3 us (level)
  the two profiles are of different devices: /device:TPU:0 before, /device:TPU:1 now
where the time goes in v4:
time: 15.3 us; the launch traced here: 15.2 us
  starting transfers between devices  6.98 us (46%)
  Pallas kernels  5.35 us (35%)
  waiting for transfers between devices  2.78 us (18%)
    ppermute x4, starting transfers between devices, shards(): arrived[k] = lax.ppermute(outgoing[k], ('dom', 'mesh'), route)  5.54 us
    pallas_call x1, Pallas kernels, shards(): pl.pallas_call(functools.partial(before, doms, slots, rows), out_shape=[l...  2.45 us
    ppermute x4, waiting for transfers between devices, shards(): arrived[k] = lax.ppermute(outgoing[k], ('dom', 'mesh'), route)  1.79 us
    ppermute x1, starting transfers between devices, shards(): columns = [lax.ppermute(column, 'sub', [(0, 1), (1, 0)])]  1.21 us
    ppermute x1, waiting for transfers between devices, shards(): columns = [lax.ppermute(column, 'sub', [(0, 1), (1, 0)])]  0.98 us
    pallas_call x1, Pallas kernels, shards(): pl.pallas_call(functools.partial(couple, doms, slots), out_shape=[like(pa...  0.86 us
    pallas_call x1, Pallas kernels, shards(): pl.pallas_call(turn, out_shape=like(blocks.shape, blocks.dtype), in_specs...  0.86 us
    pallas_call x1, Pallas kernels, shards(): pl.pallas_call(finish, out_shape=[like(flat.shape, jnp.float32)] * 2, in_...  0.75 us
  transfers between devices with their start and end apart: 6, of which 3 were waited for; matrix products, arithmetic and copies ran while one was open for 0% of the time, Pallas kernels for 14%

profile of v4, /device:TPU:1, one launch (start us, length us, event | category | flops | bytes accessed | tf_op | source)
XLA Modules:
  0.0 15.2 jit_solution(8020283587117312964)
XLA Ops:
  0.0 2.5 %before.1 = (bf16[16,16,128]{2,1,0:T(8,128)(2,1)S(1)}, bf16[19,16,128]{2,1,0:T(8,128)(2,1)S(1)}, bf16[16,16,128]{2,1,0:T(8,128)(2,1)S(1)}, bf16[19,16,128]{2,1,0...) custom-call(s32[1,1,1,96]{3,2,1,0:T(1,128)} %own_in.1, ...), custom_call_target="tpu_custom_call" | custom-call | tf_op jit(solution)/shard_map/before/pallas_call | solution.py:196
  2.5 4.8 %collective-permute-start = (bf16[19,16,128]{2,1,0:T(8,128)(2,1)S(1)}, bf16[19,16,128]{2,1,0:T(8,128)(2,1)S(1)}, u32[]{:S(2)}, u32[]{:S(2)}) collective-permute-start(bf16[19,16,128]{2,1,0:T(8,128)(2,1)S(1)} %get-tuple-element.21), channel_id=1, source_target_pairs={{0,14},{2,12},{4,10},{6,8},{8,6},{10,4},{12,2},{14,0},{1,15},{3,13... | collective-permute-start | bytes 233480 | tf_op jit(solution)/shard_map/ppermute | solution.py:221
  7.2 0.0 collective-permute-start.1
  7.2 0.1 collective-permute-start.4
  7.3 0.7 %collective-permute-start.5 = (bf16[16,16,128]{2,1,0:T(8,128)(2,1)S(1)}, bf16[16,16,128]{2,1,0:T(8,128)(2,1)S(1)}, u32[]{:S(2)}, u32[]{:S(2)}) collective-permute-start(bf16[16,16,128]{2,1,0:T(8,128)(2,1)S(1)} %get-tuple-element.30), channel_id=1, source_target_pairs={{0,2},{2,0},{4,6},{6,4},{8,10},{10,8},{12,14},{14,12},{1,3},{3,1},... | collective-permute-start | bytes 196616 | tf_op jit(solution)/shard_map/ppermute | solution.py:221
  8.0 1.2 %collective-permute-start.2 = (f32[2,32,128]{2,1,0:T(8,128)S(1)}, f32[2,32,128]{2,1,0:T(8,128)S(1)}, u32[]{:S(2)}, u32[]{:S(2)}) collective-permute-start(f32[2,32,128]{2,1,0:T(8,128)S(1)} %get-tuple-element.24), channel_id=1, source_target_pairs={{0,1},{1,0},{2,3},{3,2},{4,5},{5,4},{6,7},{7,6},{8,9},{9,8},{10,11... | collective-permute-start | bytes 98312 | tf_op jit(solution)/shard_map/ppermute | solution.py:225
  9.2 0.9 %turn.1.refs_2_.turned = bf16[96,128,128]{2,1,0:T(8,128)(2,1)S(1)} custom-call(bf16[96,128,128]{2,1,0:T(8,128)(2,1)S(1)} %get-tuple-element.23.blocks), custom_call_target="tpu_custom_call" | custom-call | bytes 8388608 | tf_op jit(solution)/shard_map/turn/pallas_call | solution.py:232
  10.1 1.0 %collective-permute-done.2.refs_0_ = f32[2,32,128]{2,1,0:T(8,128)S(1)} collective-permute-done((f32[2,32,128]{2,1,0:T(8,128)S(1)}, f32[2,32,128]{2,1,0:T(8,128)S(1)}, u32[]{:S(2)}, u32[]{:S(2)}) %collective-permute-start.2) | collective-permute-done | bytes 32800 | tf_op jit(solution)/shard_map/ppermute | solution.py:225
  11.1 0.4 %stencil.1.refs_3_.refs_4_ = f32[512,128]{1,0:T(8,128)S(1)} custom-call(f32[512,128]{1,0:T(8,128)S(1)} %get-tuple-element.19.modes, f32[1,32,128]{2,1,0:T(8,128)S(1)} %get-tuple-element.20.stiff, f32[2,32,128]{2,1,0:T(8,128)S(1)} %collective-permute-done.2.refs_0_), custom_call_target="tpu_custom_call" | custom-call | tf_op jit(solution)/shard_map/stencil/pallas_call | solution.py:241
  11.5 0.0 collective-permute-done.refs_0_
  11.5 1.3 %collective-permute-done.1.refs_1_ = bf16[19,16,128]{2,1,0:T(8,128)(2,1)S(1)} collective-permute-done((bf16[19,16,128]{2,1,0:T(8,128)(2,1)S(1)}, bf16[19,16,128]{2,1,0:T(8,128)(2,1)S(1)}, u32[]{:S(2)}, u32[]{:S(2)}) %collective-permute-start.1) | collective-permute-done | bytes 77856 | tf_op jit(solution)/shard_map/ppermute | solution.py:221
  12.8 0.2 %collective-permute-start.3 = (bf16[2,3,16,128]{3,2,1,0:T(8,128)(2,1)S(1)}, bf16[2,3,16,128]{3,2,1,0:T(8,128)(2,1)S(1)}, u32[]{:S(2)}, u32[]{:S(2)}) collective-permute-start(bf16[2,3,16,128]{3,2,1,0:T(8,128)(2,1)S(1)} %pick.1), channel_id=1, source_target_pairs={{0,2},{2,0},{1,3},{3,1},{4,6},{6,4},{5,7},{7,5},{8,10},{10,8},{9,1... | collective-permute-start | bytes 73736 | tf_op jit(solution)/shard_map/ppermute | solution.py:257
  13.1 0.5 %collective-permute-done.4.refs_2_ = bf16[16,16,128]{2,1,0:T(8,128)(2,1)S(1)} collective-permute-done((bf16[16,16,128]{2,1,0:T(8,128)(2,1)S(1)}, bf16[16,16,128]{2,1,0:T(8,128)(2,1)S(1)}, u32[]{:S(2)}, u32[]{:S(2)}) %collective-permute-start.4) | collective-permute-done | bytes 65568 | tf_op jit(solution)/shard_map/ppermute | solution.py:221
  13.5 0.0 collective-permute-done.5.refs_3_
  13.5 0.9 %couple.1 = (f32[512,128]{1,0:T(8,128)S(1)}, f32[512,128]{1,0:T(8,128)S(1)}) custom-call(s32[1,1,1,96]{3,2,1,0:T(1,128)S(4)} %get-tuple-element.25.own, s32[1,1,1,96]{3,2,1,0:T(1,128)S(4)} %get-tuple-element.26.peer, s32[1,1,1,96]{3,2,1,0:T(1,128)S(4)} %get-tuple-element.27.slot, ...), custom_call_target="tpu_custom_call", output_to_operand_aliasing={{0}: (9, {})} | custom-call | bytes 8388608 | tf_op jit(solution)/shard_map/couple/pallas_call | solution.py:258
  14.4 0.0 collective-permute-done.3.halo
  14.4 0.7 %finish.1 = (f32[512,128]{1,0:T(8,128)S(1)}, f32[512,128]{1,0:T(8,128)}) custom-call(f32[512,128]{1,0:T(8,128)S(1)} %get-tuple-element.19.modes, f32[1,32,128]{2,1,0:T(8,128)S(1)} %get-tuple-element.20.stiff, bf16[2,3,16,128]{3,2,1,0:T(8,128)(2,1)S(1)} %collective-permute-done.3.halo, ...), custom_call_target="tpu_custom_call", output_to_operand_aliasing={{0}: (3, {})} | custom-call | tf_op jit(solution)/shard_map/finish/pallas_call | solution.py:272
  (1 shorter events, 0.0 us)
Async XLA Ops:
  2.5 9.0 %collective-permute-start = (bf16[19,16,128]{2,1,0:T(8,128)(2,1)S(1)}, bf16[19,16,128]{2,1,0:T(8,128)(2,1)S(1)}, u32[]{:S(2)}, u32[]{:S(2)}) collective-permute-start(bf16[19,16,128]{2,1,0:T(8,128)(2,1)S(1)} %get-tuple-element.21), channel_id=1, source_target_pairs={{0,14},{2,12},{4,10},{6,8},{8,6},{10,4},{12,2},{14,0},{1,15},{3,13... | collective-permute-start | bytes 233480 | tf_op jit(solution)/shard_map/ppermute | solution.py:221
  7.2 5.6 %collective-permute-start.1 = (bf16[19,16,128]{2,1,0:T(8,128)(2,1)S(1)}, bf16[19,16,128]{2,1,0:T(8,128)(2,1)S(1)}, u32[]{:S(2)}, u32[]{:S(2)}) collective-permute-start(bf16[19,16,128]{2,1,0:T(8,128)(2,1)S(1)} %get-tuple-element.22), channel_id=1, source_target_pairs={{0,6},{2,4},{4,2},{6,0},{8,14},{10,12},{12,10},{14,8},{1,7},{3,5},... | collective-permute-start | bytes 233480 | tf_op jit(solution)/shard_map/ppermute | solution.py:221
  7.2 6.3 %collective-permute-start.4 = (bf16[16,16,128]{2,1,0:T(8,128)(2,1)S(1)}, bf16[16,16,128]{2,1,0:T(8,128)(2,1)S(1)}, u32[]{:S(2)}, u32[]{:S(2)}) collective-permute-start(bf16[16,16,128]{2,1,0:T(8,128)(2,1)S(1)} %get-tuple-element.29), channel_id=1, source_target_pairs={{0,10},{2,8},{4,14},{6,12},{8,2},{10,0},{12,6},{14,4},{1,11},{3,9}... | collective-permute-start | bytes 196616 | tf_op jit(solution)/shard_map/ppermute | solution.py:221
  7.3 6.2 %collective-permute-start.5 = (bf16[16,16,128]{2,1,0:T(8,128)(2,1)S(1)}, bf16[16,16,128]{2,1,0:T(8,128)(2,1)S(1)}, u32[]{:S(2)}, u32[]{:S(2)}) collective-permute-start(bf16[16,16,128]{2,1,0:T(8,128)(2,1)S(1)} %get-tuple-element.30), channel_id=1, source_target_pairs={{0,2},{2,0},{4,6},{6,4},{8,10},{10,8},{12,14},{14,12},{1,3},{3,1},... | collective-permute-start | bytes 196616 | tf_op jit(solution)/shard_map/ppermute | solution.py:221
  8.0 3.1 %collective-permute-start.2 = (f32[2,32,128]{2,1,0:T(8,128)S(1)}, f32[2,32,128]{2,1,0:T(8,128)S(1)}, u32[]{:S(2)}, u32[]{:S(2)}) collective-permute-start(f32[2,32,128]{2,1,0:T(8,128)S(1)} %get-tuple-element.24), channel_id=1, source_target_pairs={{0,1},{1,0},{2,3},{3,2},{4,5},{5,4},{6,7},{7,6},{8,9},{9,8},{10,11... | collective-permute-start | bytes 98312 | tf_op jit(solution)/shard_map/ppermute | solution.py:225
  12.8 1.6 %collective-permute-start.3 = (bf16[2,3,16,128]{3,2,1,0:T(8,128)(2,1)S(1)}, bf16[2,3,16,128]{3,2,1,0:T(8,128)(2,1)S(1)}, u32[]{:S(2)}, u32[]{:S(2)}) collective-permute-start(bf16[2,3,16,128]{3,2,1,0:T(8,128)(2,1)S(1)} %pick.1), channel_id=1, source_target_pairs={{0,2},{2,0},{1,3},{3,1},{4,6},{6,4},{5,7},{7,5},{8,10},{10,8},{9,1... | collective-permute-start | bytes 73736 | tf_op jit(solution)/shard_map/ppermute | solution.py:257

commit v5 on v4

--- a/solution.py
+++ b/solution.py
@@ -59,11 +59,11 @@
         tiles[r] = modes[pl.ds(r, count, stride=rows), :].astype(jnp.bfloat16)
 
     for k in filter(has_halo, range(doms)):
-        row = jnp.where(d ^ k > d, rows - 1, 0)
-        edge = modes[pl.ds(row, count, stride=rows), :]
+        last = d ^ k > d
+        edge = jnp.where(last, modes[pl.ds(rows - 1, count, stride=rows), :], modes[pl.ds(0, count, stride=rows), :])
         for i, piece in enumerate(pieces(edge)):
             outs[k][2 * slots + i] = piece
-        edge = jnp.broadcast_to(stiff[0, pl.ds(row, 1), :], edge.shape)
+        edge = jnp.broadcast_to(jnp.where(last, stiff[0, rows - 1 : rows, :], stiff[0, 0:1, :]), edge.shape)
         line = lax.broadcasted_iota(jnp.int32, edge.shape, 0)
         high, low = (p.astype(jnp.float32) for p in pieces(edge))
         outs[k][2 * slots + 2] = jnp.where(line == 0, high, low).astype(jnp.bfloat16)

time: 15.3 us -> 15.3 us (level)
  no operation moved by 1% of the time
where the time goes in v5:
time: 15.3 us; the launch traced here: 15.2 us
  starting transfers between devices  6.98 us (46%)
  Pallas kernels  5.36 us (35%)
  waiting for transfers between devices  2.77 us (18%)
    ppermute x4, starting transfers between devices, shards(): arrived[k] = lax.ppermute(outgoing[k], ('dom', 'mesh'), route)  5.53 us
    pallas_call x1, Pallas kernels, shards(): pl.pallas_call(functools.partial(before, doms, slots, rows), out_shape=[l...  2.45 us
    ppermute x4, waiting for transfers between devices, shards(): arrived[k] = lax.ppermute(outgoing[k], ('dom', 'mesh'), route)  1.79 us
    ppermute x1, starting transfers between devices, shards(): columns = [lax.ppermute(column, 'sub', [(0, 1), (1, 0)])]  1.21 us
    ppermute x1, waiting for transfers between devices, shards(): columns = [lax.ppermute(column, 'sub', [(0, 1), (1, 0)])]  0.98 us
    pallas_call x1, Pallas kernels, shards(): pl.pallas_call(functools.partial(couple, doms, slots), out_shape=[like(pa...  0.87 us
    pallas_call x1, Pallas kernels, shards(): pl.pallas_call(turn, out_shape=like(blocks.shape, blocks.dtype), in_specs...  0.86 us
    pallas_call x1, Pallas kernels, shards(): pl.pallas_call(finish, out_shape=[like(flat.shape, jnp.float32)] * 2, in_...  0.75 us
  transfers between devices with their start and end apart: 6, of which 3 were waited for; matrix products, arithmetic and copies ran while one was open for 0% of the time, Pallas kernels for 14%

profile of v5, /device:TPU:1, one launch (start us, length us, event | category | flops | bytes accessed | tf_op | source)
XLA Modules:
  0.0 15.2 jit_solution(18176500699919740500)
XLA Ops:
  0.0 2.5 %before.1 = (bf16[16,16,128]{2,1,0:T(8,128)(2,1)S(1)}, bf16[19,16,128]{2,1,0:T(8,128)(2,1)S(1)}, bf16[16,16,128]{2,1,0:T(8,128)(2,1)S(1)}, bf16[19,16,128]{2,1,0...) custom-call(s32[1,1,1,96]{3,2,1,0:T(1,128)} %own_in.1, ...), custom_call_target="tpu_custom_call" | custom-call | tf_op jit(solution)/shard_map/before/pallas_call | solution.py:196
  2.5 4.8 %collective-permute-start = (bf16[19,16,128]{2,1,0:T(8,128)(2,1)S(1)}, bf16[19,16,128]{2,1,0:T(8,128)(2,1)S(1)}, u32[]{:S(2)}, u32[]{:S(2)}) collective-permute-start(bf16[19,16,128]{2,1,0:T(8,128)(2,1)S(1)} %get-tuple-element.21), channel_id=1, source_target_pairs={{0,14},{2,12},{4,10},{6,8},{8,6},{10,4},{12,2},{14,0},{1,15},{3,13... | collective-permute-start | bytes 233480 | tf_op jit(solution)/shard_map/ppermute | solution.py:221
  7.2 0.0 collective-permute-start.1
  7.2 0.1 collective-permute-start.4
  7.3 0.7 %collective-permute-start.5 = (bf16[16,16,128]{2,1,0:T(8,128)(2,1)S(1)}, bf16[16,16,128]{2,1,0:T(8,128)(2,1)S(1)}, u32[]{:S(2)}, u32[]{:S(2)}) collective-permute-start(bf16[16,16,128]{2,1,0:T(8,128)(2,1)S(1)} %get-tuple-element.30), channel_id=1, source_target_pairs={{0,2},{2,0},{4,6},{6,4},{8,10},{10,8},{12,14},{14,12},{1,3},{3,1},... | collective-permute-start | bytes 196616 | tf_op jit(solution)/shard_map/ppermute | solution.py:221
  8.0 1.2 %collective-permute-start.2 = (f32[2,32,128]{2,1,0:T(8,128)S(1)}, f32[2,32,128]{2,1,0:T(8,128)S(1)}, u32[]{:S(2)}, u32[]{:S(2)}) collective-permute-start(f32[2,32,128]{2,1,0:T(8,128)S(1)} %get-tuple-element.24), channel_id=1, source_target_pairs={{0,1},{1,0},{2,3},{3,2},{4,5},{5,4},{6,7},{7,6},{8,9},{9,8},{10,11... | collective-permute-start | bytes 98312 | tf_op jit(solution)/shard_map/ppermute | solution.py:225
  9.2 0.9 %turn.1.refs_2_.turned = bf16[96,128,128]{2,1,0:T(8,128)(2,1)S(1)} custom-call(bf16[96,128,128]{2,1,0:T(8,128)(2,1)S(1)} %get-tuple-element.23.blocks), custom_call_target="tpu_custom_call" | custom-call | bytes 8388608 | tf_op jit(solution)/shard_map/turn/pallas_call | solution.py:232
  10.1 1.0 %collective-permute-done.2.refs_0_ = f32[2,32,128]{2,1,0:T(8,128)S(1)} collective-permute-done((f32[2,32,128]{2,1,0:T(8,128)S(1)}, f32[2,32,128]{2,1,0:T(8,128)S(1)}, u32[]{:S(2)}, u32[]{:S(2)}) %collective-permute-start.2) | collective-permute-done | bytes 32800 | tf_op jit(solution)/shard_map/ppermute | solution.py:225
  11.1 0.4 %stencil.1.refs_3_.refs_4_ = f32[512,128]{1,0:T(8,128)S(1)} custom-call(f32[512,128]{1,0:T(8,128)S(1)} %get-tuple-element.19.modes, f32[1,32,128]{2,1,0:T(8,128)S(1)} %get-tuple-element.20.stiff, f32[2,32,128]{2,1,0:T(8,128)S(1)} %collective-permute-done.2.refs_0_), custom_call_target="tpu_custom_call" | custom-call | tf_op jit(solution)/shard_map/stencil/pallas_call | solution.py:241
  11.5 0.0 collective-permute-done.refs_0_
  11.5 1.3 %collective-permute-done.1.refs_1_ = bf16[19,16,128]{2,1,0:T(8,128)(2,1)S(1)} collective-permute-done((bf16[19,16,128]{2,1,0:T(8,128)(2,1)S(1)}, bf16[19,16,128]{2,1,0:T(8,128)(2,1)S(1)}, u32[]{:S(2)}, u32[]{:S(2)}) %collective-permute-start.1) | collective-permute-done | bytes 77856 | tf_op jit(solution)/shard_map/ppermute | solution.py:221
  12.8 0.2 %collective-permute-start.3 = (bf16[2,3,16,128]{3,2,1,0:T(8,128)(2,1)S(1)}, bf16[2,3,16,128]{3,2,1,0:T(8,128)(2,1)S(1)}, u32[]{:S(2)}, u32[]{:S(2)}) collective-permute-start(bf16[2,3,16,128]{3,2,1,0:T(8,128)(2,1)S(1)} %pick.1), channel_id=1, source_target_pairs={{0,2},{2,0},{1,3},{3,1},{4,6},{6,4},{5,7},{7,5},{8,10},{10,8},{9,1... | collective-permute-start | bytes 73736 | tf_op jit(solution)/shard_map/ppermute | solution.py:257
  13.1 0.5 %collective-permute-done.4.refs_2_ = bf16[16,16,128]{2,1,0:T(8,128)(2,1)S(1)} collective-permute-done((bf16[16,16,128]{2,1,0:T(8,128)(2,1)S(1)}, bf16[16,16,128]{2,1,0:T(8,128)(2,1)S(1)}, u32[]{:S(2)}, u32[]{:S(2)}) %collective-permute-start.4) | collective-permute-done | bytes 65568 | tf_op jit(solution)/shard_map/ppermute | solution.py:221
  13.5 0.0 collective-permute-done.5.refs_3_
  13.5 0.9 %couple.1 = (f32[512,128]{1,0:T(8,128)S(1)}, f32[512,128]{1,0:T(8,128)S(1)}) custom-call(s32[1,1,1,96]{3,2,1,0:T(1,128)S(4)} %get-tuple-element.25.own, s32[1,1,1,96]{3,2,1,0:T(1,128)S(4)} %get-tuple-element.26.peer, s32[1,1,1,96]{3,2,1,0:T(1,128)S(4)} %get-tuple-element.27.slot, ...), custom_call_target="tpu_custom_call", output_to_operand_aliasing={{0}: (9, {})} | custom-call | bytes 8388608 | tf_op jit(solution)/shard_map/couple/pallas_call | solution.py:258
  14.4 0.0 collective-permute-done.3.halo
  14.4 0.7 %finish.1 = (f32[512,128]{1,0:T(8,128)S(1)}, f32[512,128]{1,0:T(8,128)}) custom-call(f32[512,128]{1,0:T(8,128)S(1)} %get-tuple-element.19.modes, f32[1,32,128]{2,1,0:T(8,128)S(1)} %get-tuple-element.20.stiff, bf16[2,3,16,128]{3,2,1,0:T(8,128)(2,1)S(1)} %collective-permute-done.3.halo, ...), custom_call_target="tpu_custom_call", output_to_operand_aliasing={{0}: (3, {})} | custom-call | tf_op jit(solution)/shard_map/finish/pallas_call | solution.py:272
  (1 shorter events, 0.0 us)
Async XLA Ops:
  2.5 9.0 %collective-permute-start = (bf16[19,16,128]{2,1,0:T(8,128)(2,1)S(1)}, bf16[19,16,128]{2,1,0:T(8,128)(2,1)S(1)}, u32[]{:S(2)}, u32[]{:S(2)}) collective-permute-start(bf16[19,16,128]{2,1,0:T(8,128)(2,1)S(1)} %get-tuple-element.21), channel_id=1, source_target_pairs={{0,14},{2,12},{4,10},{6,8},{8,6},{10,4},{12,2},{14,0},{1,15},{3,13... | collective-permute-start | bytes 233480 | tf_op jit(solution)/shard_map/ppermute | solution.py:221
  7.2 5.6 %collective-permute-start.1 = (bf16[19,16,128]{2,1,0:T(8,128)(2,1)S(1)}, bf16[19,16,128]{2,1,0:T(8,128)(2,1)S(1)}, u32[]{:S(2)}, u32[]{:S(2)}) collective-permute-start(bf16[19,16,128]{2,1,0:T(8,128)(2,1)S(1)} %get-tuple-element.22), channel_id=1, source_target_pairs={{0,6},{2,4},{4,2},{6,0},{8,14},{10,12},{12,10},{14,8},{1,7},{3,5},... | collective-permute-start | bytes 233480 | tf_op jit(solution)/shard_map/ppermute | solution.py:221
  7.2 6.3 %collective-permute-start.4 = (bf16[16,16,128]{2,1,0:T(8,128)(2,1)S(1)}, bf16[16,16,128]{2,1,0:T(8,128)(2,1)S(1)}, u32[]{:S(2)}, u32[]{:S(2)}) collective-permute-start(bf16[16,16,128]{2,1,0:T(8,128)(2,1)S(1)} %get-tuple-element.29), channel_id=1, source_target_pairs={{0,10},{2,8},{4,14},{6,12},{8,2},{10,0},{12,6},{14,4},{1,11},{3,9}... | collective-permute-start | bytes 196616 | tf_op jit(solution)/shard_map/ppermute | solution.py:221
  7.3 6.2 %collective-permute-start.5 = (bf16[16,16,128]{2,1,0:T(8,128)(2,1)S(1)}, bf16[16,16,128]{2,1,0:T(8,128)(2,1)S(1)}, u32[]{:S(2)}, u32[]{:S(2)}) collective-permute-start(bf16[16,16,128]{2,1,0:T(8,128)(2,1)S(1)} %get-tuple-element.30), channel_id=1, source_target_pairs={{0,2},{2,0},{4,6},{6,4},{8,10},{10,8},{12,14},{14,12},{1,3},{3,1},... | collective-permute-start | bytes 196616 | tf_op jit(solution)/shard_map/ppermute | solution.py:221
  8.0 3.1 %collective-permute-start.2 = (f32[2,32,128]{2,1,0:T(8,128)S(1)}, f32[2,32,128]{2,1,0:T(8,128)S(1)}, u32[]{:S(2)}, u32[]{:S(2)}) collective-permute-start(f32[2,32,128]{2,1,0:T(8,128)S(1)} %get-tuple-element.24), channel_id=1, source_target_pairs={{0,1},{1,0},{2,3},{3,2},{4,5},{5,4},{6,7},{7,6},{8,9},{9,8},{10,11... | collective-permute-start | bytes 98312 | tf_op jit(solution)/shard_map/ppermute | solution.py:225
  12.8 1.6 %collective-permute-start.3 = (bf16[2,3,16,128]{3,2,1,0:T(8,128)(2,1)S(1)}, bf16[2,3,16,128]{3,2,1,0:T(8,128)(2,1)S(1)}, u32[]{:S(2)}, u32[]{:S(2)}) collective-permute-start(bf16[2,3,16,128]{3,2,1,0:T(8,128)(2,1)S(1)} %pick.1), channel_id=1, source_target_pairs={{0,2},{2,0},{1,3},{3,1},{4,6},{6,4},{5,7},{7,5},{8,10},{10,8},{9,1... | collective-permute-start | bytes 73736 | tf_op jit(solution)/shard_map/ppermute | solution.py:257

commit v6 on v3

--- a/solution.py
+++ b/solution.py
@@ -59,11 +59,11 @@
         tiles[r] = modes[pl.ds(r, count, stride=rows), :].astype(jnp.bfloat16)
 
     for k in filter(has_halo, range(doms)):
-        row = jnp.where(d ^ k > d, rows - 1, 0)
-        edge = modes[pl.ds(row, count, stride=rows), :]
+        last = d ^ k > d
+        edge = jnp.where(last, modes[pl.ds(rows - 1, count, stride=rows), :], modes[pl.ds(0, count, stride=rows), :])
         for i, piece in enumerate(pieces(edge)):
             outs[k][2 * slots + i] = piece
-        edge = jnp.broadcast_to(stiff[0, pl.ds(row, 1), :], edge.shape)
+        edge = jnp.broadcast_to(jnp.where(last, stiff[0, rows - 1 : rows, :], stiff[0, 0:1, :]), edge.shape)
         line = lax.broadcasted_iota(jnp.int32, edge.shape, 0)
         high, low = (p.astype(jnp.float32) for p in pieces(edge))
         outs[k][2 * slots + 2] = jnp.where(line == 0, high, low).astype(jnp.bfloat16)

time: 15.3 us -> 15.3 us (level)
  no operation moved by 1% of the time
where the time goes in v6:
time: 15.3 us; the launch traced here: 15 us
  starting transfers between devices  7.5 us (49%)
  Pallas kernels  5.3 us (35%)
  waiting for transfers between devices  2.15 us (14%)
    ppermute x4, starting transfers between devices, shards(): arrived[k] = lax.ppermute(outgoing[k], ('dom', 'mesh'), route)  5.48 us
    pallas_call x1, Pallas kernels, shards(): pl.pallas_call(functools.partial(before, doms, slots, rows), out_shape=[l...  2.46 us
    ppermute x1, starting transfers between devices, shards(): columns = [lax.ppermute(column, 'sub', [(0, 1), (1, 0)])]  1.75 us
    ppermute x1, waiting for transfers between devices, shards(): columns = [lax.ppermute(column, 'sub', [(0, 1), (1, 0)])]  1.3 us
    pallas_call x1, Pallas kernels, shards(): pl.pallas_call(turn, out_shape=like(blocks.shape, blocks.dtype), in_specs...  0.86 us
    pallas_call x1, Pallas kernels, shards(): pl.pallas_call(finish, out_shape=like(flat.shape, jnp.float32), in_specs=...  0.81 us
    pallas_call x1, Pallas kernels, shards(): pl.pallas_call(functools.partial(couple, doms, slots), out_shape=like(par...  0.75 us
    ppermute x4, waiting for transfers between devices, shards(): arrived[k] = lax.ppermute(outgoing[k], ('dom', 'mesh'), route)  0.69 us
  transfers between devices with their start and end apart: 6, of which 3 were waited for; matrix products, arithmetic and copies ran while one was open for 0% of the time, Pallas kernels for 14%

profile of v6, /device:TPU:0, one launch (start us, length us, event | category | flops | bytes accessed | tf_op | source)
XLA Modules:
  0.0 15.0 jit_solution(1027477436765488172)
XLA Ops:
  0.0 2.5 %before.1 = (bf16[16,16,128]{2,1,0:T(8,128)(2,1)S(1)}, bf16[19,16,128]{2,1,0:T(8,128)(2,1)S(1)}, bf16[16,16,128]{2,1,0:T(8,128)(2,1)S(1)}, bf16[19,16,128]{2,1,0...) custom-call(s32[1,1,1,96]{3,2,1,0:T(1,128)} %own_in.1, ...), custom_call_target="tpu_custom_call" | custom-call | tf_op jit(solution)/shard_map/before/pallas_call | solution.py:191
  2.5 4.6 %collective-permute-start = (bf16[19,16,128]{2,1,0:T(8,128)(2,1)S(1)}, bf16[19,16,128]{2,1,0:T(8,128)(2,1)S(1)}, u32[]{:S(2)}, u32[]{:S(2)}) collective-permute-start(bf16[19,16,128]{2,1,0:T(8,128)(2,1)S(1)} %get-tuple-element.22), channel_id=1, source_target_pairs={{0,14},{2,12},{4,10},{6,8},{8,6},{10,4},{12,2},{14,0},{1,15},{3,13... | collective-permute-start | bytes 233480 | tf_op jit(solution)/shard_map/ppermute | solution.py:216
  7.0 0.0 collective-permute-start.1
  7.0 0.9 %collective-permute-start.2 = (bf16[16,16,128]{2,1,0:T(8,128)(2,1)S(1)}, bf16[16,16,128]{2,1,0:T(8,128)(2,1)S(1)}, u32[]{:S(2)}, u32[]{:S(2)}) collective-permute-start(bf16[16,16,128]{2,1,0:T(8,128)(2,1)S(1)} %get-tuple-element.24), channel_id=1, source_target_pairs={{0,10},{2,8},{4,14},{6,12},{8,2},{10,0},{12,6},{14,4},{1,11},{3,9}... | collective-permute-start | bytes 196616 | tf_op jit(solution)/shard_map/ppermute | solution.py:216
  7.9 0.0 collective-permute-start.3
  7.9 1.7 %collective-permute-start.4 = (f32[2,32,128]{2,1,0:T(8,128)S(1)}, f32[2,32,128]{2,1,0:T(8,128)S(1)}, u32[]{:S(2)}, u32[]{:S(2)}) collective-permute-start(f32[2,32,128]{2,1,0:T(8,128)S(1)} %get-tuple-element.28), channel_id=1, source_target_pairs={{0,1},{1,0},{2,3},{3,2},{4,5},{5,4},{6,7},{7,6},{8,9},{9,8},{10,11... | collective-permute-start | bytes 98312 | tf_op jit(solution)/shard_map/ppermute | solution.py:220
  9.7 0.9 %turn.1.turned.refs_2_ = bf16[96,128,128]{2,1,0:T(8,128)(2,1)S(1)} custom-call(bf16[96,128,128]{2,1,0:T(8,128)(2,1)S(1)} %get-tuple-element.21.blocks), custom_call_target="tpu_custom_call" | custom-call | bytes 8388608 | tf_op jit(solution)/shard_map/turn/pallas_call | solution.py:227
  10.6 1.3 %collective-permute-done.4.refs_0_ = f32[2,32,128]{2,1,0:T(8,128)S(1)} collective-permute-done((f32[2,32,128]{2,1,0:T(8,128)S(1)}, f32[2,32,128]{2,1,0:T(8,128)S(1)}, u32[]{:S(2)}, u32[]{:S(2)}) %collective-permute-start.4) | collective-permute-done | bytes 32800 | tf_op jit(solution)/shard_map/ppermute | solution.py:220
  11.9 0.4 %stencil.1.refs_4_.refs_3_ = f32[512,128]{1,0:T(8,128)S(1)} custom-call(f32[512,128]{1,0:T(8,128)S(1)} %get-tuple-element.26.modes, f32[1,32,128]{2,1,0:T(8,128)S(1)} %get-tuple-element.27.stiff, f32[2,32,128]{2,1,0:T(8,128)S(1)} %collective-permute-done.4.refs_0_), custom_call_target="tpu_custom_call" | custom-call | tf_op jit(solution)/shard_map/stencil/pallas_call | solution.py:236
  12.3 0.0 collective-permute-done.refs_0_
  12.3 0.7 %collective-permute-done.1.refs_1_ = bf16[19,16,128]{2,1,0:T(8,128)(2,1)S(1)} collective-permute-done((bf16[19,16,128]{2,1,0:T(8,128)(2,1)S(1)}, bf16[19,16,128]{2,1,0:T(8,128)(2,1)S(1)}, u32[]{:S(2)}, u32[]{:S(2)}) %collective-permute-start.1) | collective-permute-done | bytes 77856 | tf_op jit(solution)/shard_map/ppermute | solution.py:216
  13.0 0.3 %collective-permute-start.5 = (bf16[2,3,16,128]{3,2,1,0:T(8,128)(2,1)S(1)}, bf16[2,3,16,128]{3,2,1,0:T(8,128)(2,1)S(1)}, u32[]{:S(2)}, u32[]{:S(2)}) collective-permute-start(bf16[2,3,16,128]{3,2,1,0:T(8,128)(2,1)S(1)} %pick.1), channel_id=1, source_target_pairs={{0,2},{2,0},{1,3},{3,1},{4,6},{6,4},{5,7},{7,5},{8,10},{10,8},{9,1... | collective-permute-start | bytes 73736 | tf_op jit(solution)/shard_map/ppermute | solution.py:252
  13.3 0.0 collective-permute-done.2.refs_2_
  13.3 0.0 collective-permute-done.3.refs_3_
  13.3 0.8 %couple.1.total = f32[512,128]{1,0:T(8,128)S(1)} custom-call(s32[1,1,1,96]{3,2,1,0:T(1,128)S(4)} %get-tuple-element.17.own, s32[1,1,1,96]{3,2,1,0:T(1,128)S(4)} %get-tuple-element.18.peer, s32[1,1,1,96]{3,2,1,0:T(1,128)S(4)} %get-tuple-element.19.slot, s32[1,1,1,4,8]{4,3,2,1,0:T(4,128)S(4)} %get-tuple-element.20.send, ...), custom_call_target="tpu_custom_call", output_to_operand_aliasing={{}: (9, {})} | custom-call | bytes 8388608 | tf_op jit(solution)/shard_map/couple/pallas_call | solution.py:253
  14.0 0.2 %collective-permute-done.5.halo = bf16[2,3,16,128]{3,2,1,0:T(8,128)(2,1)S(1)} collective-permute-done((bf16[2,3,16,128]{3,2,1,0:T(8,128)(2,1)S(1)}, bf16[2,3,16,128]{3,2,1,0:T(8,128)(2,1)S(1)}, u32[]{:S(2)}, u32[]{:S(2)}) %collective-permute-start.5) | collective-permute-done | bytes 24608 | tf_op jit(solution)/shard_map/ppermute | solution.py:252
  14.2 0.8 %finish.1 = f32[512,128]{1,0:T(8,128)} custom-call(f32[512,128]{1,0:T(8,128)S(1)} %couple.1.total, f32[512,128]{1,0:T(8,128)S(1)} %get-tuple-element.26.modes, f32[1,32,128]{2,1,0:T(8,128)S(1)} %get-tuple-element.27.stiff, bf16[2,3,16,128]{3,2,1,0:T(8,128)(2,1)S(1)} %collective-permute-done.5.halo), custom_call_target="tpu_custom_call" | custom-call | tf_op jit(solution)/shard_map/finish/pallas_call | solution.py:267
  (1 shorter events, 0.0 us)
Async XLA Ops:
  2.5 9.8 %collective-permute-start = (bf16[19,16,128]{2,1,0:T(8,128)(2,1)S(1)}, bf16[19,16,128]{2,1,0:T(8,128)(2,1)S(1)}, u32[]{:S(2)}, u32[]{:S(2)}) collective-permute-start(bf16[19,16,128]{2,1,0:T(8,128)(2,1)S(1)} %get-tuple-element.22), channel_id=1, source_target_pairs={{0,14},{2,12},{4,10},{6,8},{8,6},{10,4},{12,2},{14,0},{1,15},{3,13... | collective-permute-start | bytes 233480 | tf_op jit(solution)/shard_map/ppermute | solution.py:216
  7.0 6.0 %collective-permute-start.1 = (bf16[19,16,128]{2,1,0:T(8,128)(2,1)S(1)}, bf16[19,16,128]{2,1,0:T(8,128)(2,1)S(1)}, u32[]{:S(2)}, u32[]{:S(2)}) collective-permute-start(bf16[19,16,128]{2,1,0:T(8,128)(2,1)S(1)} %get-tuple-element.23), channel_id=1, source_target_pairs={{0,6},{2,4},{4,2},{6,0},{8,14},{10,12},{12,10},{14,8},{1,7},{3,5},... | collective-permute-start | bytes 233480 | tf_op jit(solution)/shard_map/ppermute | solution.py:216
  7.0 6.3 %collective-permute-start.2 = (bf16[16,16,128]{2,1,0:T(8,128)(2,1)S(1)}, bf16[16,16,128]{2,1,0:T(8,128)(2,1)S(1)}, u32[]{:S(2)}, u32[]{:S(2)}) collective-permute-start(bf16[16,16,128]{2,1,0:T(8,128)(2,1)S(1)} %get-tuple-element.24), channel_id=1, source_target_pairs={{0,10},{2,8},{4,14},{6,12},{8,2},{10,0},{12,6},{14,4},{1,11},{3,9}... | collective-permute-start | bytes 196616 | tf_op jit(solution)/shard_map/ppermute | solution.py:216
  7.9 5.3 %collective-permute-start.3 = (bf16[16,16,128]{2,1,0:T(8,128)(2,1)S(1)}, bf16[16,16,128]{2,1,0:T(8,128)(2,1)S(1)}, u32[]{:S(2)}, u32[]{:S(2)}) collective-permute-start(bf16[16,16,128]{2,1,0:T(8,128)(2,1)S(1)} %get-tuple-element.25), channel_id=1, source_target_pairs={{0,2},{2,0},{4,6},{6,4},{8,10},{10,8},{12,14},{14,12},{1,3},{3,1},... | collective-permute-start | bytes 196616 | tf_op jit(solution)/shard_map/ppermute | solution.py:216
  7.9 3.9 %collective-permute-start.4 = (f32[2,32,128]{2,1,0:T(8,128)S(1)}, f32[2,32,128]{2,1,0:T(8,128)S(1)}, u32[]{:S(2)}, u32[]{:S(2)}) collective-permute-start(f32[2,32,128]{2,1,0:T(8,128)S(1)} %get-tuple-element.28), channel_id=1, source_target_pairs={{0,1},{1,0},{2,3},{3,2},{4,5},{5,4},{6,7},{7,6},{8,9},{9,8},{10,11... | collective-permute-start | bytes 98312 | tf_op jit(solution)/shard_map/ppermute | solution.py:220
  13.0 1.2 %collective-permute-start.5 = (bf16[2,3,16,128]{3,2,1,0:T(8,128)(2,1)S(1)}, bf16[2,3,16,128]{3,2,1,0:T(8,128)(2,1)S(1)}, u32[]{:S(2)}, u32[]{:S(2)}) collective-permute-start(bf16[2,3,16,128]{3,2,1,0:T(8,128)(2,1)S(1)} %pick.1), channel_id=1, source_target_pairs={{0,2},{2,0},{1,3},{3,1},{4,6},{6,4},{5,7},{7,5},{8,10},{10,8},{9,1... | collective-permute-start | bytes 73736 | tf_op jit(solution)/shard_map/ppermute | solution.py:252

commit v7 on v6

--- a/solution.py
+++ b/solution.py
@@ -42,7 +42,7 @@
     return copies
 
 
-def before(doms, slots, rows, own_in, peer_in, slot_in, send_in, modes_in, stiff_in, coupling, *refs):
+def before(doms, subs, slots, rows, own_in, peer_in, slot_in, send_in, modes_in, stiff_in, coupling, *refs):
     outs, (column, blocks, modes, stiff) = refs[:doms], refs[doms : doms + 4]
     own, peer, slot, send, tiles, sums, sems, block_sems = refs[doms + 4 :]
     sources = (own_in, peer_in, slot_in, send_in, modes_in, stiff_in)
@@ -75,8 +75,11 @@
     for m in range(count + 1):
         here = stiff[0] if m == count else modes[m * rows : (m + 1) * rows, :]
         ends = [jnp.where(lane == m, end, packed) for end, packed in zip((here[:, :1], here[:, -1:]), ends)]
-    for side in range(2):
-        column[side] = ends[side]
+    if subs == 2:
+        column[0] = jnp.where(lax.axis_index("sub") == 0, ends[1], ends[0])
+    else:
+        for side in range(2):
+            column[side] = ends[side]
     for c, copy in enumerate(block_copies):
         copy.wait()
         for p in range(c * half, (c + 1) * half, 2):
@@ -106,7 +109,7 @@
     if subs == 1:
         left = right = jnp.zeros(lane.shape, jnp.float32)
     elif subs == 2:
-        left, right = jnp.where(s == 1, columns[0][1], 0.0), jnp.where(s == 0, columns[0][0], 0.0)
+        left, right = jnp.where(s == 1, columns[0][0], 0.0), jnp.where(s == 0, columns[0][0], 0.0)
     else:
         left, right = columns[0][1], columns[1][0]
 
@@ -189,10 +192,10 @@
     like = jax.ShapeDtypeStruct
     indices = inputs[:4]
     *outgoing, column, blocks, modes, stiff, own, peer, slot, send = pl.pallas_call(
-        functools.partial(before, doms, slots, rows),
+        functools.partial(before, doms, subs, slots, rows),
         out_shape=[like((2 * slots + PIECES * has_halo(k), count, cells), jnp.bfloat16) for k in range(doms)]
         + [
-            like((2, rows, cells), jnp.float32),
+            like((1 if subs == 2 else 2, rows, cells), jnp.float32),
             like((pairs, cells, cells), jnp.bfloat16),
             like(flat.shape, jnp.float32),
             like(stiffness.shape, jnp.float32),

time: 15.3 us -> 15.2 us (level)
    ppermute x4, waiting for transfers between devices: 0.69 us -> 0.88 us  [shards(): arrived[k] = lax.ppermute(outgoing[k], ('dom', 'mesh'), route)]
    ppermute x1, waiting for transfers between devices: 1.3 us -> 1.13 us  [shards(): columns = [lax.ppermute(column, 'sub', [(0, 1), (1, 0)])]]
where the time goes in v7:
time: 15.2 us; the launch traced here: 15 us
  starting transfers between devices  7.51 us (49%)
  Pallas kernels  5.3 us (35%)
  waiting for transfers between devices  2.16 us (14%)
    ppermute x4, starting transfers between devices, shards(): arrived[k] = lax.ppermute(outgoing[k], ('dom', 'mesh'), route)  5.49 us
    pallas_call x1, Pallas kernels, shards(): pl.pallas_call(functools.partial(before, doms, subs, slots, rows), out_sh...  2.45 us
    ppermute x1, starting transfers between devices, shards(): columns = [lax.ppermute(column, 'sub', [(0, 1), (1, 0)])]  1.74 us
    ppermute x1, waiting for transfers between devices, shards(): columns = [lax.ppermute(column, 'sub', [(0, 1), (1, 0)])]  1.13 us
    ppermute x4, waiting for transfers between devices, shards(): arrived[k] = lax.ppermute(outgoing[k], ('dom', 'mesh'), route)  0.88 us
    pallas_call x1, Pallas kernels, shards(): pl.pallas_call(turn, out_shape=like(blocks.shape, blocks.dtype), in_specs...  0.86 us
    pallas_call x1, Pallas kernels, shards(): pl.pallas_call(finish, out_shape=like(flat.shape, jnp.float32), in_specs=...  0.81 us
    pallas_call x1, Pallas kernels, shards(): pl.pallas_call(functools.partial(couple, doms, slots), out_shape=like(par...  0.75 us
  transfers between devices with their start and end apart: 6, of which 3 were waited for; matrix products, arithmetic and copies ran while one was open for 0% of the time, Pallas kernels for 14%

profile of v7, /device:TPU:0, one launch (start us, length us, event | category | flops | bytes accessed | tf_op | source)
XLA Modules:
  0.0 15.0 jit_solution(9041364541588299114)
XLA Ops:
  0.0 2.5 %before.1 = (bf16[16,16,128]{2,1,0:T(8,128)(2,1)S(1)}, bf16[19,16,128]{2,1,0:T(8,128)(2,1)S(1)}, bf16[16,16,128]{2,1,0:T(8,128)(2,1)S(1)}, bf16[19,16,128]{2,1,0...) custom-call(s32[1,1,1,96]{3,2,1,0:T(1,128)} %own_in.1, ...), custom_call_target="tpu_custom_call" | custom-call | tf_op jit(solution)/shard_map/before/pallas_call | solution.py:194
  2.5 4.6 %collective-permute-start = (bf16[19,16,128]{2,1,0:T(8,128)(2,1)S(1)}, bf16[19,16,128]{2,1,0:T(8,128)(2,1)S(1)}, u32[]{:S(2)}, u32[]{:S(2)}) collective-permute-start(bf16[19,16,128]{2,1,0:T(8,128)(2,1)S(1)} %get-tuple-element.22), channel_id=1, source_target_pairs={{0,14},{2,12},{4,10},{6,8},{8,6},{10,4},{12,2},{14,0},{1,15},{3,13... | collective-permute-start | bytes 233480 | tf_op jit(solution)/shard_map/ppermute | solution.py:219
  7.0 0.0 collective-permute-start.1
  7.0 0.9 %collective-permute-start.2 = (bf16[16,16,128]{2,1,0:T(8,128)(2,1)S(1)}, bf16[16,16,128]{2,1,0:T(8,128)(2,1)S(1)}, u32[]{:S(2)}, u32[]{:S(2)}) collective-permute-start(bf16[16,16,128]{2,1,0:T(8,128)(2,1)S(1)} %get-tuple-element.24), channel_id=1, source_target_pairs={{0,10},{2,8},{4,14},{6,12},{8,2},{10,0},{12,6},{14,4},{1,11},{3,9}... | collective-permute-start | bytes 196616 | tf_op jit(solution)/shard_map/ppermute | solution.py:219
  8.0 0.0 collective-permute-start.3
  8.0 1.7 %collective-permute-start.4 = (f32[1,32,128]{2,1,0:T(8,128)S(1)}, f32[1,32,128]{2,1,0:T(8,128)S(1)}, u32[]{:S(2)}, u32[]{:S(2)}) collective-permute-start(f32[1,32,128]{2,1,0:T(8,128)S(1)} %get-tuple-element.28), channel_id=1, source_target_pairs={{0,1},{1,0},{2,3},{3,2},{4,5},{5,4},{6,7},{7,6},{8,9},{9,8},{10,11... | collective-permute-start | bytes 49160 | tf_op jit(solution)/shard_map/ppermute | solution.py:223
  9.7 0.9 %turn.1.turned.refs_2_ = bf16[96,128,128]{2,1,0:T(8,128)(2,1)S(1)} custom-call(bf16[96,128,128]{2,1,0:T(8,128)(2,1)S(1)} %get-tuple-element.21.blocks), custom_call_target="tpu_custom_call" | custom-call | bytes 8388608 | tf_op jit(solution)/shard_map/turn/pallas_call | solution.py:230
  10.6 1.1 %collective-permute-done.4.refs_0_ = f32[1,32,128]{2,1,0:T(8,128)S(1)} collective-permute-done((f32[1,32,128]{2,1,0:T(8,128)S(1)}, f32[1,32,128]{2,1,0:T(8,128)S(1)}, u32[]{:S(2)}, u32[]{:S(2)}) %collective-permute-start.4) | collective-permute-done | bytes 16416 | tf_op jit(solution)/shard_map/ppermute | solution.py:223
  11.7 0.4 %stencil.1.refs_4_.refs_3_ = f32[512,128]{1,0:T(8,128)S(1)} custom-call(f32[512,128]{1,0:T(8,128)S(1)} %get-tuple-element.26.modes, f32[1,32,128]{2,1,0:T(8,128)S(1)} %get-tuple-element.27.stiff, f32[1,32,128]{2,1,0:T(8,128)S(1)} %collective-permute-done.4.refs_0_), custom_call_target="tpu_custom_call" | custom-call | tf_op jit(solution)/shard_map/stencil/pallas_call | solution.py:239
  12.1 0.0 collective-permute-done.refs_0_
  12.1 0.9 %collective-permute-done.1.refs_1_ = bf16[19,16,128]{2,1,0:T(8,128)(2,1)S(1)} collective-permute-done((bf16[19,16,128]{2,1,0:T(8,128)(2,1)S(1)}, bf16[19,16,128]{2,1,0:T(8,128)(2,1)S(1)}, u32[]{:S(2)}, u32[]{:S(2)}) %collective-permute-start.1) | collective-permute-done | bytes 77856 | tf_op jit(solution)/shard_map/ppermute | solution.py:219
  13.0 0.3 %collective-permute-start.5 = (bf16[2,3,16,128]{3,2,1,0:T(8,128)(2,1)S(1)}, bf16[2,3,16,128]{3,2,1,0:T(8,128)(2,1)S(1)}, u32[]{:S(2)}, u32[]{:S(2)}) collective-permute-start(bf16[2,3,16,128]{3,2,1,0:T(8,128)(2,1)S(1)} %pick.1), channel_id=1, source_target_pairs={{0,2},{2,0},{1,3},{3,1},{4,6},{6,4},{5,7},{7,5},{8,10},{10,8},{9,1... | collective-permute-start | bytes 73736 | tf_op jit(solution)/shard_map/ppermute | solution.py:255
  13.3 0.0 collective-permute-done.2.refs_2_
  13.3 0.0 collective-permute-done.3.refs_3_
  13.3 0.8 %couple.1.total = f32[512,128]{1,0:T(8,128)S(1)} custom-call(s32[1,1,1,96]{3,2,1,0:T(1,128)S(4)} %get-tuple-element.17.own, s32[1,1,1,96]{3,2,1,0:T(1,128)S(4)} %get-tuple-element.18.peer, s32[1,1,1,96]{3,2,1,0:T(1,128)S(4)} %get-tuple-element.19.slot, s32[1,1,1,4,8]{4,3,2,1,0:T(4,128)S(4)} %get-tuple-element.20.send, ...), custom_call_target="tpu_custom_call", output_to_operand_aliasing={{}: (9, {})} | custom-call | bytes 8388608 | tf_op jit(solution)/shard_map/couple/pallas_call | solution.py:256
  14.1 0.2 %collective-permute-done.5.halo = bf16[2,3,16,128]{3,2,1,0:T(8,128)(2,1)S(1)} collective-permute-done((bf16[2,3,16,128]{3,2,1,0:T(8,128)(2,1)S(1)}, bf16[2,3,16,128]{3,2,1,0:T(8,128)(2,1)S(1)}, u32[]{:S(2)}, u32[]{:S(2)}) %collective-permute-start.5) | collective-permute-done | bytes 24608 | tf_op jit(solution)/shard_map/ppermute | solution.py:255
  14.2 0.8 %finish.1 = f32[512,128]{1,0:T(8,128)} custom-call(f32[512,128]{1,0:T(8,128)S(1)} %couple.1.total, f32[512,128]{1,0:T(8,128)S(1)} %get-tuple-element.26.modes, f32[1,32,128]{2,1,0:T(8,128)S(1)} %get-tuple-element.27.stiff, bf16[2,3,16,128]{3,2,1,0:T(8,128)(2,1)S(1)} %collective-permute-done.5.halo), custom_call_target="tpu_custom_call" | custom-call | tf_op jit(solution)/shard_map/finish/pallas_call | solution.py:270
  (1 shorter events, 0.0 us)
Async XLA Ops:
  2.5 9.7 %collective-permute-start = (bf16[19,16,128]{2,1,0:T(8,128)(2,1)S(1)}, bf16[19,16,128]{2,1,0:T(8,128)(2,1)S(1)}, u32[]{:S(2)}, u32[]{:S(2)}) collective-permute-start(bf16[19,16,128]{2,1,0:T(8,128)(2,1)S(1)} %get-tuple-element.22), channel_id=1, source_target_pairs={{0,14},{2,12},{4,10},{6,8},{8,6},{10,4},{12,2},{14,0},{1,15},{3,13... | collective-permute-start | bytes 233480 | tf_op jit(solution)/shard_map/ppermute | solution.py:219
  7.0 6.0 %collective-permute-start.1 = (bf16[19,16,128]{2,1,0:T(8,128)(2,1)S(1)}, bf16[19,16,128]{2,1,0:T(8,128)(2,1)S(1)}, u32[]{:S(2)}, u32[]{:S(2)}) collective-permute-start(bf16[19,16,128]{2,1,0:T(8,128)(2,1)S(1)} %get-tuple-element.23), channel_id=1, source_target_pairs={{0,6},{2,4},{4,2},{6,0},{8,14},{10,12},{12,10},{14,8},{1,7},{3,5},... | collective-permute-start | bytes 233480 | tf_op jit(solution)/shard_map/ppermute | solution.py:219
  7.0 6.3 %collective-permute-start.2 = (bf16[16,16,128]{2,1,0:T(8,128)(2,1)S(1)}, bf16[16,16,128]{2,1,0:T(8,128)(2,1)S(1)}, u32[]{:S(2)}, u32[]{:S(2)}) collective-permute-start(bf16[16,16,128]{2,1,0:T(8,128)(2,1)S(1)} %get-tuple-element.24), channel_id=1, source_target_pairs={{0,10},{2,8},{4,14},{6,12},{8,2},{10,0},{12,6},{14,4},{1,11},{3,9}... | collective-permute-start | bytes 196616 | tf_op jit(solution)/shard_map/ppermute | solution.py:219
  8.0 5.3 %collective-permute-start.3 = (bf16[16,16,128]{2,1,0:T(8,128)(2,1)S(1)}, bf16[16,16,128]{2,1,0:T(8,128)(2,1)S(1)}, u32[]{:S(2)}, u32[]{:S(2)}) collective-permute-start(bf16[16,16,128]{2,1,0:T(8,128)(2,1)S(1)} %get-tuple-element.25), channel_id=1, source_target_pairs={{0,2},{2,0},{4,6},{6,4},{8,10},{10,8},{12,14},{14,12},{1,3},{3,1},... | collective-permute-start | bytes 196616 | tf_op jit(solution)/shard_map/ppermute | solution.py:219
  8.0 3.7 %collective-permute-start.4 = (f32[1,32,128]{2,1,0:T(8,128)S(1)}, f32[1,32,128]{2,1,0:T(8,128)S(1)}, u32[]{:S(2)}, u32[]{:S(2)}) collective-permute-start(f32[1,32,128]{2,1,0:T(8,128)S(1)} %get-tuple-element.28), channel_id=1, source_target_pairs={{0,1},{1,0},{2,3},{3,2},{4,5},{5,4},{6,7},{7,6},{8,9},{9,8},{10,11... | collective-permute-start | bytes 49160 | tf_op jit(solution)/shard_map/ppermute | solution.py:223
  13.0 1.2 %collective-permute-start.5 = (bf16[2,3,16,128]{3,2,1,0:T(8,128)(2,1)S(1)}, bf16[2,3,16,128]{3,2,1,0:T(8,128)(2,1)S(1)}, u32[]{:S(2)}, u32[]{:S(2)}) collective-permute-start(bf16[2,3,16,128]{3,2,1,0:T(8,128)(2,1)S(1)} %pick.1), channel_id=1, source_target_pairs={{0,2},{2,0},{1,3},{3,1},{4,6},{6,4},{5,7},{7,5},{8,10},{10,8},{9,1... | collective-permute-start | bytes 73736 | tf_op jit(solution)/shard_map/ppermute | solution.py:255

commit v8 on v7

--- a/solution.py
+++ b/solution.py
@@ -143,8 +143,9 @@
 
 
 def couple(doms, slots, own, peer, slot, send, turned, *refs):
-    arrived, (_, total, foreign, back) = dict(zip(exchange(doms), refs)), refs[doms:]
+    arrived, (_, total, out, foreign, back) = dict(zip(exchange(doms), refs)), refs[doms:]
     count = foreign.shape[1]
+    rows = total.shape[0] // count
     d = lax.axis_index("dom")
     for k in range(doms):
         for j in range(slots):
@@ -162,18 +163,28 @@
         first, second = (foreign[peer[0, 0, 0, q] * slots + slot[0, 0, 0, q]] for q in (p, p + 1))
         for q, term in zip((p, p + 1), pair_dot(first, second, turned[p : p + 2])):
             subtract(own[0, 0, 0, q], term)
-
-
-def finish(total, modes, stiff, halo, out):
-    rows = stiff.shape[1]
-    count = total.shape[0] // rows
     for m in range(count):
         out[m * rows : (m + 1) * rows, :] = total[pl.ds(m, rows, stride=count), :]
-    for side, row in enumerate((0, rows - 1)):
-        here = modes[pl.ds(row, count, stride=rows), :]
+
+
+def finish(modes, stiff, halo, result, out, ends, sems):
+    rows, cells = stiff.shape[1:]
+    count = result.shape[0]
+    group = ends.shape[2]
+    middle = pl.ds(group, rows - 2 * group)
+    copies = [pltpu.make_async_copy(result.at[:, middle], out.at[:, middle], sems.at[2])]
+    copies[0].start()
+    line = lax.broadcasted_iota(jnp.int32, (group, cells), 0)
+    for side, (row, first) in enumerate(((0, 0), (rows - 1, rows - group))):
         near = whole(halo[side, 0], halo[side, 1])
         weight = 0.5 * (stiff[0, row : row + 1, :] + whole(halo[side, 2, 0:1], halo[side, 2, 1:2]))
-        out[pl.ds(row, count, stride=rows), :] = total[row * count : (row + 1) * count, :] + weight * (here - near)
+        added = weight * (modes[pl.ds(row, count, stride=rows), :] - near)
+        for m in range(count):
+            ends[side, m] = result[m, first : first + group] + jnp.where(line == row - first, added[m : m + 1], 0.0)
+        copies.append(pltpu.make_async_copy(ends.at[side], out.at[:, pl.ds(first, group)], sems.at[side]))
+        copies[-1].start()
+    for copy in copies:
+        copy.wait()
 
 
 def exchange(doms):
@@ -253,11 +264,11 @@
         name="pick",
     )(*(arrived[k] for k in exchange(doms) if has_halo(k)), turned, partial)
     halo = lax.ppermute(halo, "mesh", [(0, 1), (1, 0)])
-    total = pl.pallas_call(
+    _, result = pl.pallas_call(
         functools.partial(couple, doms, slots),
-        out_shape=like(partial.shape, partial.dtype),
+        out_shape=[like(partial.shape, partial.dtype)] * 2,
         in_specs=[SMEM] * 4 + [VMEM] * (2 + doms),
-        out_specs=VMEM,
+        out_specs=[VMEM] * 2,
         scratch_shapes=[
             pltpu.VMEM((doms * slots, count, cells), jnp.bfloat16),
             pltpu.VMEM((doms * slots, count, cells), jnp.float32),
@@ -269,12 +280,13 @@
     )(*indices, turned, *(arrived[k] for k in exchange(doms)), partial)
     out = pl.pallas_call(
         finish,
-        out_shape=like(flat.shape, jnp.float32),
+        out_shape=like((count, rows, cells), jnp.float32),
         in_specs=[VMEM] * 4,
-        out_specs=VMEM,
+        out_specs=HBM,
+        scratch_shapes=[pltpu.VMEM((2, count, 8, cells), jnp.float32), pltpu.SemaphoreType.DMA((3,))],
         compiler_params=params,
         name="finish",
-    )(total, modes, stiff, halo)
+    )(modes, stiff, halo, result.reshape(count, rows, cells))
     return out.reshape(modes_in.shape)
 
 

time: 15.2 us -> 15.2 us (level)
  no operation moved by 1% of the time
where the time goes in v8:
time: 15.2 us; the launch traced here: 14.9 us
  starting transfers between devices  7.5 us (49%)
  Pallas kernels  5.32 us (35%)
  waiting for transfers between devices  2.06 us (14%)
    ppermute x4, starting transfers between devices, shards(): arrived[k] = lax.ppermute(outgoing[k], ('dom', 'mesh'), route)  5.48 us
    pallas_call x1, Pallas kernels, shards(): pl.pallas_call(functools.partial(before, doms, subs, slots, rows), out_sh...  2.45 us
    ppermute x1, starting transfers between devices, shards(): columns = [lax.ppermute(column, 'sub', [(0, 1), (1, 0)])]  1.75 us
    ppermute x1, waiting for transfers between devices, shards(): columns = [lax.ppermute(column, 'sub', [(0, 1), (1, 0)])]  1.13 us
    ppermute x4, waiting for transfers between devices, shards(): arrived[k] = lax.ppermute(outgoing[k], ('dom', 'mesh'), route)  0.88 us
    pallas_call x1, Pallas kernels, shards(): pl.pallas_call(functools.partial(couple, doms, slots), out_shape=[like(pa...  0.86 us
    pallas_call x1, Pallas kernels, shards(): pl.pallas_call(turn, out_shape=like(blocks.shape, blocks.dtype), in_specs...  0.86 us
    pallas_call x1, Pallas kernels, shards(): pl.pallas_call(finish, out_shape=like((count, rows, cells), jnp.float32),...  0.72 us
  transfers between devices with their start and end apart: 6, of which 3 were waited for; matrix products, arithmetic and copies ran while one was open for 0% of the time, Pallas kernels for 14%

profile of v8, /device:TPU:0, one launch (start us, length us, event | category | flops | bytes accessed | tf_op | source)
XLA Modules:
  0.0 14.9 jit_solution(9510315818444936590)
XLA Ops:
  0.0 2.5 %before.1 = (bf16[16,16,128]{2,1,0:T(8,128)(2,1)S(1)}, bf16[19,16,128]{2,1,0:T(8,128)(2,1)S(1)}, bf16[16,16,128]{2,1,0:T(8,128)(2,1)S(1)}, bf16[19,16,128]{2,1,0...) custom-call(s32[1,1,1,96]{3,2,1,0:T(1,128)} %own_in.1, ...), custom_call_target="tpu_custom_call" | custom-call | tf_op jit(solution)/shard_map/before/pallas_call | solution.py:205
  2.5 4.6 %collective-permute-start = (bf16[19,16,128]{2,1,0:T(8,128)(2,1)S(1)}, bf16[19,16,128]{2,1,0:T(8,128)(2,1)S(1)}, u32[]{:S(2)}, u32[]{:S(2)}) collective-permute-start(bf16[19,16,128]{2,1,0:T(8,128)(2,1)S(1)} %get-tuple-element.20), channel_id=1, source_target_pairs={{0,14},{2,12},{4,10},{6,8},{8,6},{10,4},{12,2},{14,0},{1,15},{3,13... | collective-permute-start | bytes 233480 | tf_op jit(solution)/shard_map/ppermute | solution.py:230
  7.0 0.0 collective-permute-start.1
  7.0 0.9 %collective-permute-start.4 = (bf16[16,16,128]{2,1,0:T(8,128)(2,1)S(1)}, bf16[16,16,128]{2,1,0:T(8,128)(2,1)S(1)}, u32[]{:S(2)}, u32[]{:S(2)}) collective-permute-start(bf16[16,16,128]{2,1,0:T(8,128)(2,1)S(1)} %get-tuple-element.28), channel_id=1, source_target_pairs={{0,10},{2,8},{4,14},{6,12},{8,2},{10,0},{12,6},{14,4},{1,11},{3,9}... | collective-permute-start | bytes 196616 | tf_op jit(solution)/shard_map/ppermute | solution.py:230
  7.9 0.0 collective-permute-start.5
  7.9 1.7 %collective-permute-start.2 = (f32[1,32,128]{2,1,0:T(8,128)S(1)}, f32[1,32,128]{2,1,0:T(8,128)S(1)}, u32[]{:S(2)}, u32[]{:S(2)}) collective-permute-start(f32[1,32,128]{2,1,0:T(8,128)S(1)} %get-tuple-element.23), channel_id=1, source_target_pairs={{0,1},{1,0},{2,3},{3,2},{4,5},{5,4},{6,7},{7,6},{8,9},{9,8},{10,11... | collective-permute-start | bytes 49160 | tf_op jit(solution)/shard_map/ppermute | solution.py:234
  9.7 0.9 %turn.1.refs_2_.turned = bf16[96,128,128]{2,1,0:T(8,128)(2,1)S(1)} custom-call(bf16[96,128,128]{2,1,0:T(8,128)(2,1)S(1)} %get-tuple-element.22.blocks), custom_call_target="tpu_custom_call" | custom-call | bytes 8388608 | tf_op jit(solution)/shard_map/turn/pallas_call | solution.py:241
  10.6 1.1 %collective-permute-done.2.refs_0_ = f32[1,32,128]{2,1,0:T(8,128)S(1)} collective-permute-done((f32[1,32,128]{2,1,0:T(8,128)S(1)}, f32[1,32,128]{2,1,0:T(8,128)S(1)}, u32[]{:S(2)}, u32[]{:S(2)}) %collective-permute-start.2) | collective-permute-done | bytes 16416 | tf_op jit(solution)/shard_map/ppermute | solution.py:234
  11.7 0.4 %stencil.1.refs_3_.refs_4_ = f32[512,128]{1,0:T(8,128)S(1)} custom-call(f32[512,128]{1,0:T(8,128)S(1)} %get-tuple-element.18.modes, f32[1,32,128]{2,1,0:T(8,128)S(1)} %get-tuple-element.19.stiff, f32[1,32,128]{2,1,0:T(8,128)S(1)} %collective-permute-done.2.refs_0_), custom_call_target="tpu_custom_call" | custom-call | tf_op jit(solution)/shard_map/stencil/pallas_call | solution.py:250
  12.1 0.0 collective-permute-done.refs_0_
  12.1 0.9 %collective-permute-done.1.refs_1_ = bf16[19,16,128]{2,1,0:T(8,128)(2,1)S(1)} collective-permute-done((bf16[19,16,128]{2,1,0:T(8,128)(2,1)S(1)}, bf16[19,16,128]{2,1,0:T(8,128)(2,1)S(1)}, u32[]{:S(2)}, u32[]{:S(2)}) %collective-permute-start.1) | collective-permute-done | bytes 77856 | tf_op jit(solution)/shard_map/ppermute | solution.py:230
  13.0 0.3 %collective-permute-start.3 = (bf16[2,3,16,128]{3,2,1,0:T(8,128)(2,1)S(1)}, bf16[2,3,16,128]{3,2,1,0:T(8,128)(2,1)S(1)}, u32[]{:S(2)}, u32[]{:S(2)}) collective-permute-start(bf16[2,3,16,128]{3,2,1,0:T(8,128)(2,1)S(1)} %pick.1), channel_id=1, source_target_pairs={{0,2},{2,0},{1,3},{3,1},{4,6},{6,4},{5,7},{7,5},{8,10},{10,8},{9,1... | collective-permute-start | bytes 73736 | tf_op jit(solution)/shard_map/ppermute | solution.py:266
  13.3 0.0 collective-permute-done.4.refs_2_
  13.3 0.0 collective-permute-done.5.refs_3_
  13.3 0.9 %couple.1 = (f32[512,128]{1,0:T(8,128)S(1)}, f32[512,128]{1,0:T(8,128)S(1)}) custom-call(s32[1,1,1,96]{3,2,1,0:T(1,128)S(4)} %get-tuple-element.24.own, s32[1,1,1,96]{3,2,1,0:T(1,128)S(4)} %get-tuple-element.25.peer, s32[1,1,1,96]{3,2,1,0:T(1,128)S(4)} %get-tuple-element.26.slot, ...), custom_call_target="tpu_custom_call", output_to_operand_aliasing={{0}: (9, {})} | custom-call | bytes 8388608 | tf_op jit(solution)/shard_map/couple/pallas_call | solution.py:267
  14.1 0.1 collective-permute-done.3.halo
  14.2 0.7 %finish.1 = f32[16,32,128]{2,1,0:T(8,128)} custom-call(f32[512,128]{1,0:T(8,128)S(1)} %get-tuple-element.18.modes, f32[1,32,128]{2,1,0:T(8,128)S(1)} %get-tuple-element.19.stiff, bf16[2,3,16,128]{3,2,1,0:T(8,128)(2,1)S(1)} %collective-permute-done.3.halo, f32[16,32,128]{2,1,0:T(8,128)S(1)} %bitcast.3), custom_call_target="tpu_custom_call" | custom-call | tf_op jit(solution)/shard_map/finish/pallas_call | solution.py:281
  (1 shorter events, 0.0 us)
Async XLA Ops:
  2.5 9.7 %collective-permute-start = (bf16[19,16,128]{2,1,0:T(8,128)(2,1)S(1)}, bf16[19,16,128]{2,1,0:T(8,128)(2,1)S(1)}, u32[]{:S(2)}, u32[]{:S(2)}) collective-permute-start(bf16[19,16,128]{2,1,0:T(8,128)(2,1)S(1)} %get-tuple-element.20), channel_id=1, source_target_pairs={{0,14},{2,12},{4,10},{6,8},{8,6},{10,4},{12,2},{14,0},{1,15},{3,13... | collective-permute-start | bytes 233480 | tf_op jit(solution)/shard_map/ppermute | solution.py:230
  7.0 6.0 %collective-permute-start.1 = (bf16[19,16,128]{2,1,0:T(8,128)(2,1)S(1)}, bf16[19,16,128]{2,1,0:T(8,128)(2,1)S(1)}, u32[]{:S(2)}, u32[]{:S(2)}) collective-permute-start(bf16[19,16,128]{2,1,0:T(8,128)(2,1)S(1)} %get-tuple-element.21), channel_id=1, source_target_pairs={{0,6},{2,4},{4,2},{6,0},{8,14},{10,12},{12,10},{14,8},{1,7},{3,5},... | collective-permute-start | bytes 233480 | tf_op jit(solution)/shard_map/ppermute | solution.py:230
  7.0 6.3 %collective-permute-start.4 = (bf16[16,16,128]{2,1,0:T(8,128)(2,1)S(1)}, bf16[16,16,128]{2,1,0:T(8,128)(2,1)S(1)}, u32[]{:S(2)}, u32[]{:S(2)}) collective-permute-start(bf16[16,16,128]{2,1,0:T(8,128)(2,1)S(1)} %get-tuple-element.28), channel_id=1, source_target_pairs={{0,10},{2,8},{4,14},{6,12},{8,2},{10,0},{12,6},{14,4},{1,11},{3,9}... | collective-permute-start | bytes 196616 | tf_op jit(solution)/shard_map/ppermute | solution.py:230
  7.9 5.3 %collective-permute-start.5 = (bf16[16,16,128]{2,1,0:T(8,128)(2,1)S(1)}, bf16[16,16,128]{2,1,0:T(8,128)(2,1)S(1)}, u32[]{:S(2)}, u32[]{:S(2)}) collective-permute-start(bf16[16,16,128]{2,1,0:T(8,128)(2,1)S(1)} %get-tuple-element.29), channel_id=1, source_target_pairs={{0,2},{2,0},{4,6},{6,4},{8,10},{10,8},{12,14},{14,12},{1,3},{3,1},... | collective-permute-start | bytes 196616 | tf_op jit(solution)/shard_map/ppermute | solution.py:230
  7.9 3.7 %collective-permute-start.2 = (f32[1,32,128]{2,1,0:T(8,128)S(1)}, f32[1,32,128]{2,1,0:T(8,128)S(1)}, u32[]{:S(2)}, u32[]{:S(2)}) collective-permute-start(f32[1,32,128]{2,1,0:T(8,128)S(1)} %get-tuple-element.23), channel_id=1, source_target_pairs={{0,1},{1,0},{2,3},{3,2},{4,5},{5,4},{6,7},{7,6},{8,9},{9,8},{10,11... | collective-permute-start | bytes 49160 | tf_op jit(solution)/shard_map/ppermute | solution.py:234
  13.0 1.2 %collective-permute-start.3 = (bf16[2,3,16,128]{3,2,1,0:T(8,128)(2,1)S(1)}, bf16[2,3,16,128]{3,2,1,0:T(8,128)(2,1)S(1)}, u32[]{:S(2)}, u32[]{:S(2)}) collective-permute-start(bf16[2,3,16,128]{3,2,1,0:T(8,128)(2,1)S(1)} %pick.1), channel_id=1, source_target_pairs={{0,2},{2,0},{1,3},{3,1},{4,6},{6,4},{5,7},{7,5},{8,10},{10,8},{9,1... | collective-permute-start | bytes 73736 | tf_op jit(solution)/shard_map/ppermute | solution.py:266

commit v9 on v7

--- a/solution.py
+++ b/solution.py
@@ -76,7 +76,8 @@
         here = stiff[0] if m == count else modes[m * rows : (m + 1) * rows, :]
         ends = [jnp.where(lane == m, end, packed) for end, packed in zip((here[:, :1], here[:, -1:]), ends)]
     if subs == 2:
-        column[0] = jnp.where(lax.axis_index("sub") == 0, ends[1], ends[0])
+        column[0] = jnp.zeros_like(column[0])
+        column[0, :rows] = jnp.where(lax.axis_index("sub") == 0, ends[1], ends[0])
     else:
         for side in range(2):
             column[side] = ends[side]
@@ -96,7 +97,7 @@
         turned[p] = blocks[p].T
 
 
-def stencil(subs, modes, stiff, *refs):
+def stencil(subs, modes, stiff, _, *refs):
     columns, total = refs[:-1], refs[-1]
     rows, cells = stiff.shape[1:]
     count = modes.shape[0] // rows
@@ -109,7 +110,7 @@
     if subs == 1:
         left = right = jnp.zeros(lane.shape, jnp.float32)
     elif subs == 2:
-        left, right = jnp.where(s == 1, columns[0][0], 0.0), jnp.where(s == 0, columns[0][0], 0.0)
+        left, right = jnp.where(s == 1, columns[0][0, :rows], 0.0), jnp.where(s == 0, columns[0][0, :rows], 0.0)
     else:
         left, right = columns[0][1], columns[1][0]
 
@@ -142,14 +143,19 @@
                 halo[side] = ref[2 * slots : 2 * slots + PIECES]
 
 
-def couple(doms, slots, own, peer, slot, send, turned, *refs):
-    arrived, (_, total, foreign, back) = dict(zip(exchange(doms), refs)), refs[doms:]
+def couple(doms, slots, own, peer, slot, send, turned, modes, stiff, halo, *refs):
+    arrived, (_, total, out, foreign, back, held, sems) = dict(zip(exchange(doms), refs)), refs[doms:]
     count = foreign.shape[1]
+    rows = total.shape[0] // count
     d = lax.axis_index("dom")
     for k in range(doms):
         for j in range(slots):
             foreign[(d ^ k) * slots + j] = arrived[k][j]
             back[(d ^ k) * slots + j] = arrived[k][slots + j].astype(jnp.float32)
+    for side, row in enumerate((0, rows - 1)):
+        near = whole(halo[side, 0], halo[side, 1])
+        weight = 0.5 * (stiff[0, row : row + 1, :] + whole(halo[side, 2, 0:1], halo[side, 2, 1:2]))
+        total[row * count : (row + 1) * count, :] += weight * (modes[pl.ds(row, count, stride=rows), :] - near)
 
     def subtract(row, term):
         part = pl.ds(pl.multiple_of(row * count, count), count)
@@ -162,18 +168,16 @@
         first, second = (foreign[peer[0, 0, 0, q] * slots + slot[0, 0, 0, q]] for q in (p, p + 1))
         for q, term in zip((p, p + 1), pair_dot(first, second, turned[p : p + 2])):
             subtract(own[0, 0, 0, q], term)
-
-
-def finish(total, modes, stiff, halo, out):
-    rows = stiff.shape[1]
-    count = total.shape[0] // rows
-    for m in range(count):
-        out[m * rows : (m + 1) * rows, :] = total[pl.ds(m, rows, stride=count), :]
-    for side, row in enumerate((0, rows - 1)):
-        here = modes[pl.ds(row, count, stride=rows), :]
-        near = whole(halo[side, 0], halo[side, 1])
-        weight = 0.5 * (stiff[0, row : row + 1, :] + whole(halo[side, 2, 0:1], halo[side, 2, 1:2]))
-        out[pl.ds(row, count, stride=rows), :] = total[row * count : (row + 1) * count, :] + weight * (here - near)
+    copies = []
+    for i in range(2):
+        some = range(i * count // 2, (i + 1) * count // 2)
+        for m in some:
+            held[m * rows : (m + 1) * rows, :] = total[pl.ds(m, rows, stride=count), :]
+        part = pl.ds(some[0] * rows, len(some) * rows)
+        copies.append(pltpu.make_async_copy(held.at[part], out.at[part], sems.at[i]))
+        copies[-1].start()
+    for copy in copies:
+        copy.wait()
 
 
 def exchange(doms):
@@ -195,7 +199,7 @@
         functools.partial(before, doms, subs, slots, rows),
         out_shape=[like((2 * slots + PIECES * has_halo(k), count, cells), jnp.bfloat16) for k in range(doms)]
         + [
-            like((1 if subs == 2 else 2, rows, cells), jnp.float32),
+            like((1, (slots + 1) * count, cells) if subs == 2 else (2, rows, cells), jnp.float32),
             like((pairs, cells, cells), jnp.bfloat16),
             like(flat.shape, jnp.float32),
             like(stiffness.shape, jnp.float32),
@@ -236,45 +240,39 @@
         cost_estimate=cost,
         name="turn",
     )(blocks)
+    picked = pl.pallas_call(
+        functools.partial(pick, doms, slots),
+        out_shape=like((2, PIECES, count, cells), jnp.bfloat16),
+        in_specs=[VMEM] * sum(map(has_halo, range(doms))) + [ANY],
+        out_specs=VMEM,
+        compiler_params=params,
+        name="pick",
+    )(*(arrived[k] for k in exchange(doms) if has_halo(k)), turned)
     partial = pl.pallas_call(
         functools.partial(stencil, subs),
         out_shape=like(flat.shape, jnp.float32),
-        in_specs=[VMEM] * (2 + len(columns)),
+        in_specs=[VMEM, VMEM, ANY] + [VMEM] * len(columns),
         out_specs=VMEM,
         compiler_params=params,
         name="stencil",
-    )(modes, stiff, *columns)
-    halo = pl.pallas_call(
-        functools.partial(pick, doms, slots),
-        out_shape=like((2, PIECES, count, cells), jnp.bfloat16),
-        in_specs=[VMEM] * sum(map(has_halo, range(doms))) + [ANY] * 2,
-        out_specs=VMEM,
-        compiler_params=params,
-        name="pick",
-    )(*(arrived[k] for k in exchange(doms) if has_halo(k)), turned, partial)
-    halo = lax.ppermute(halo, "mesh", [(0, 1), (1, 0)])
-    total = pl.pallas_call(
+    )(modes, stiff, picked, *columns)
+    halo = lax.ppermute(picked, "mesh", [(0, 1), (1, 0)])
+    _, out = pl.pallas_call(
         functools.partial(couple, doms, slots),
-        out_shape=like(partial.shape, partial.dtype),
-        in_specs=[SMEM] * 4 + [VMEM] * (2 + doms),
-        out_specs=VMEM,
+        out_shape=[like(partial.shape, partial.dtype)] * 2,
+        in_specs=[SMEM] * 4 + [VMEM] * (5 + doms),
+        out_specs=[VMEM, HBM],
         scratch_shapes=[
             pltpu.VMEM((doms * slots, count, cells), jnp.bfloat16),
             pltpu.VMEM((doms * slots, count, cells), jnp.float32),
+            pltpu.VMEM(flat.shape, jnp.float32),
+            pltpu.SemaphoreType.DMA((2,)),
         ],
-        input_output_aliases={5 + doms: 0},
+        input_output_aliases={8 + doms: 0},
         compiler_params=params,
         cost_estimate=cost,
         name="couple",
-    )(*indices, turned, *(arrived[k] for k in exchange(doms)), partial)
-    out = pl.pallas_call(
-        finish,
-        out_shape=like(flat.shape, jnp.float32),
-        in_specs=[VMEM] * 4,
-        out_specs=VMEM,
-        compiler_params=params,
-        name="finish",
-    )(total, modes, stiff, halo)
+    )(*indices, turned, modes, stiff, halo, *(arrived[k] for k in exchange(doms)), partial)
     return out.reshape(modes_in.shape)
 
 

time: 15.2 us -> 15 us (0.987)
  waiting for transfers between devices: 2.16 us -> 1.99 us
    ppermute x1, waiting for transfers between devices: 1.13 us -> 0.01 us  [shards(): columns = [lax.ppermute(column, 'sub', [(0, 1), (1, 0)])]]
    ppermute x4, waiting for transfers between devices: 0.88 us -> 1.99 us  [shards(): arrived[k] = lax.ppermute(outgoing[k], ('dom', 'mesh'), route)]
    ppermute x1, starting transfers between devices: 1.74 us -> 1.49 us  [shards(): columns = [lax.ppermute(column, 'sub', [(0, 1), (1, 0)])]]
    ppermute x4, starting transfers between devices: 5.49 us -> 5.73 us  [shards(): arrived[k] = lax.ppermute(outgoing[k], ('dom', 'mesh'), route)]
    pallas_call x2 -> x1, Pallas kernels: 1.56 us -> 1.53 us  [shards(): pl.pallas_call(functools.partial(couple, doms, slots), out_shape=[like(pa...]
  transfers between devices with their start and end apart: 6 -> 6, of which waited for: 3 -> 2; matrix products, arithmetic and copies ran while one was open for 0% -> 0% of each run, Pallas kernels for 14% -> 9%
where the time goes in v9:
time: 15 us; the launch traced here: 14.9 us
  starting transfers between devices  7.6 us (51%)
  Pallas kernels  5.27 us (35%)
  waiting for transfers between devices  1.99 us (13%)
    ppermute x4, starting transfers between devices, shards(): arrived[k] = lax.ppermute(outgoing[k], ('dom', 'mesh'), route)  5.73 us
    pallas_call x1, Pallas kernels, shards(): pl.pallas_call(functools.partial(before, doms, subs, slots, rows), out_sh...  2.46 us
    ppermute x4, waiting for transfers between devices, shards(): arrived[k] = lax.ppermute(outgoing[k], ('dom', 'mesh'), route)  1.99 us
    pallas_call x1, Pallas kernels, shards(): pl.pallas_call(functools.partial(couple, doms, slots), out_shape=[like(pa...  1.53 us
    ppermute x1, starting transfers between devices, shards(): columns = [lax.ppermute(column, 'sub', [(0, 1), (1, 0)])]  1.49 us
    pallas_call x1, Pallas kernels, shards(): pl.pallas_call(turn, out_shape=like(blocks.shape, blocks.dtype), in_specs...  0.86 us
    pallas_call x1, Pallas kernels, shards(): pl.pallas_call(functools.partial(stencil, subs), out_shape=like(flat.shap...  0.42 us
    ppermute x1, starting transfers between devices, shards(): halo = lax.ppermute(picked, 'mesh', [(0, 1), (1, 0)])  0.38 us
  transfers between devices with their start and end apart: 6, of which 2 were waited for; matrix products, arithmetic and copies ran while one was open for 0% of the time, Pallas kernels for 9%

profile of v9, /device:TPU:0, one launch (start us, length us, event | category | flops | bytes accessed | tf_op | source)
XLA Modules:
  0.0 14.9 jit_solution(15444017759669904260)
XLA Ops:
  0.0 2.5 %before.1 = (bf16[16,16,128]{2,1,0:T(8,128)(2,1)S(1)}, bf16[19,16,128]{2,1,0:T(8,128)(2,1)S(1)}, bf16[16,16,128]{2,1,0:T(8,128)(2,1)S(1)}, bf16[19,16,128]{2,1,0...) custom-call(s32[1,1,1,96]{3,2,1,0:T(1,128)} %own_in.1, ...), custom_call_target="tpu_custom_call" | custom-call | tf_op jit(solution)/shard_map/before/pallas_call | solution.py:198
  2.5 4.6 %collective-permute-start = (bf16[19,16,128]{2,1,0:T(8,128)(2,1)S(1)}, bf16[19,16,128]{2,1,0:T(8,128)(2,1)S(1)}, u32[]{:S(2)}, u32[]{:S(2)}) collective-permute-start(bf16[19,16,128]{2,1,0:T(8,128)(2,1)S(1)} %get-tuple-element.25), channel_id=1, source_target_pairs={{0,14},{2,12},{4,10},{6,8},{8,6},{10,4},{12,2},{14,0},{1,15},{3,13... | collective-permute-start | bytes 233480 | tf_op jit(solution)/shard_map/ppermute | solution.py:223
  7.0 0.0 collective-permute-start.1
  7.0 1.5 %collective-permute-start.5 = (f32[1,144,128]{2,1,0:T(8,128)S(1)}, f32[1,144,128]{2,1,0:T(8,128)S(1)}, u32[]{:S(2)}, u32[]{:S(2)}) collective-permute-start(f32[1,144,128]{2,1,0:T(8,128)S(1)} %get-tuple-element.29), channel_id=1, source_target_pairs={{0,1},{1,0},{2,3},{3,2},{4,5},{5,4},{6,7},{7,6},{8,9},{9,8},{10,11... | collective-permute-start | bytes 221192 | tf_op jit(solution)/shard_map/ppermute | solution.py:227
  8.5 0.6 %collective-permute-start.3 = (bf16[16,16,128]{2,1,0:T(8,128)(2,1)S(1)}, bf16[16,16,128]{2,1,0:T(8,128)(2,1)S(1)}, u32[]{:S(2)}, u32[]{:S(2)}) collective-permute-start(bf16[16,16,128]{2,1,0:T(8,128)(2,1)S(1)} %get-tuple-element.27), channel_id=1, source_target_pairs={{0,10},{2,8},{4,14},{6,12},{8,2},{10,0},{12,6},{14,4},{1,11},{3,9}... | collective-permute-start | bytes 196616 | tf_op jit(solution)/shard_map/ppermute | solution.py:223
  9.2 0.5 %collective-permute-start.4 = (bf16[16,16,128]{2,1,0:T(8,128)(2,1)S(1)}, bf16[16,16,128]{2,1,0:T(8,128)(2,1)S(1)}, u32[]{:S(2)}, u32[]{:S(2)}) collective-permute-start(bf16[16,16,128]{2,1,0:T(8,128)(2,1)S(1)} %get-tuple-element.28), channel_id=1, source_target_pairs={{0,2},{2,0},{4,6},{6,4},{8,10},{10,8},{12,14},{14,12},{1,3},{3,1},... | collective-permute-start | bytes 196616 | tf_op jit(solution)/shard_map/ppermute | solution.py:223
  9.7 0.9 %turn.1.refs_2_.turned = bf16[96,128,128]{2,1,0:T(8,128)(2,1)S(1)} custom-call(bf16[96,128,128]{2,1,0:T(8,128)(2,1)S(1)} %get-tuple-element.22.blocks), custom_call_target="tpu_custom_call" | custom-call | bytes 8388608 | tf_op jit(solution)/shard_map/turn/pallas_call | solution.py:234
  10.6 0.0 collective-permute-done.refs_0_
  10.6 1.0 %collective-permute-done.1.refs_1_ = bf16[19,16,128]{2,1,0:T(8,128)(2,1)S(1)} collective-permute-done((bf16[19,16,128]{2,1,0:T(8,128)(2,1)S(1)}, bf16[19,16,128]{2,1,0:T(8,128)(2,1)S(1)}, u32[]{:S(2)}, u32[]{:S(2)}) %collective-permute-start.1) | collective-permute-done | bytes 77856 | tf_op jit(solution)/shard_map/ppermute | solution.py:223
  11.6 0.4 %collective-permute-start.2 = (bf16[2,3,16,128]{3,2,1,0:T(8,128)(2,1)S(1)}, bf16[2,3,16,128]{3,2,1,0:T(8,128)(2,1)S(1)}, u32[]{:S(2)}, u32[]{:S(2)}) collective-permute-start(bf16[2,3,16,128]{3,2,1,0:T(8,128)(2,1)S(1)} %pick.1._), channel_id=1, source_target_pairs={{0,2},{2,0},{1,3},{3,1},{4,6},{6,4},{5,7},{7,5},{8,10},{10,8},{9,1... | collective-permute-start | bytes 73736 | tf_op jit(solution)/shard_map/ppermute | solution.py:259
  12.0 0.0 collective-permute-done.5.refs_0_
  12.0 0.4 %stencil.1.refs_4_ = f32[512,128]{1,0:T(8,128)S(1)} custom-call(f32[512,128]{1,0:T(8,128)S(1)} %get-tuple-element.23.modes, f32[1,32,128]{2,1,0:T(8,128)S(1)} %get-tuple-element.24.stiff, bf16[2,3,16,128]{3,2,1,0:T(8,128)(2,1)S(1)} %pick.1._, f32[1,144,128]{2,1,0:T(8,128)S(1)} %collective-permute-done.5.refs_0_), custom_call_target="tpu_custom_call" | custom-call | tf_op jit(solution)/shard_map/stencil/pallas_call | solution.py:251
  12.4 0.9 %collective-permute-done.3.refs_2_ = bf16[16,16,128]{2,1,0:T(8,128)(2,1)S(1)} collective-permute-done((bf16[16,16,128]{2,1,0:T(8,128)(2,1)S(1)}, bf16[16,16,128]{2,1,0:T(8,128)(2,1)S(1)}, u32[]{:S(2)}, u32[]{:S(2)}) %collective-permute-start.3) | collective-permute-done | bytes 65568 | tf_op jit(solution)/shard_map/ppermute | solution.py:223
  13.4 0.0 collective-permute-done.4.refs_3_
  13.4 0.0 collective-permute-done.2.halo
  13.4 1.5 %couple.1 = (f32[512,128]{1,0:T(8,128)S(1)}, f32[512,128]{1,0:T(8,128)}) custom-call(s32[1,1,1,96]{3,2,1,0:T(1,128)S(4)} %get-tuple-element.18.own, s32[1,1,1,96]{3,2,1,0:T(1,128)S(4)} %get-tuple-element.19.peer, s32[1,1,1,96]{3,2,1,0:T(1,128)S(4)} %get-tuple-element.20.slot, ...), custom_call_target="tpu_custom_call", output_to_operand_aliasing={{0}: (12, {})} | custom-call | bytes 8388608 | tf_op jit(solution)/shard_map/couple/pallas_call | solution.py:260
  (1 shorter events, 0.0 us)
Async XLA Ops:
  2.5 8.1 %collective-permute-start = (bf16[19,16,128]{2,1,0:T(8,128)(2,1)S(1)}, bf16[19,16,128]{2,1,0:T(8,128)(2,1)S(1)}, u32[]{:S(2)}, u32[]{:S(2)}) collective-permute-start(bf16[19,16,128]{2,1,0:T(8,128)(2,1)S(1)} %get-tuple-element.25), channel_id=1, source_target_pairs={{0,14},{2,12},{4,10},{6,8},{8,6},{10,4},{12,2},{14,0},{1,15},{3,13... | collective-permute-start | bytes 233480 | tf_op jit(solution)/shard_map/ppermute | solution.py:223
  7.0 4.6 %collective-permute-start.1 = (bf16[19,16,128]{2,1,0:T(8,128)(2,1)S(1)}, bf16[19,16,128]{2,1,0:T(8,128)(2,1)S(1)}, u32[]{:S(2)}, u32[]{:S(2)}) collective-permute-start(bf16[19,16,128]{2,1,0:T(8,128)(2,1)S(1)} %get-tuple-element.26), channel_id=1, source_target_pairs={{0,6},{2,4},{4,2},{6,0},{8,14},{10,12},{12,10},{14,8},{1,7},{3,5},... | collective-permute-start | bytes 233480 | tf_op jit(solution)/shard_map/ppermute | solution.py:223
  7.0 5.0 %collective-permute-start.5 = (f32[1,144,128]{2,1,0:T(8,128)S(1)}, f32[1,144,128]{2,1,0:T(8,128)S(1)}, u32[]{:S(2)}, u32[]{:S(2)}) collective-permute-start(f32[1,144,128]{2,1,0:T(8,128)S(1)} %get-tuple-element.29), channel_id=1, source_target_pairs={{0,1},{1,0},{2,3},{3,2},{4,5},{5,4},{6,7},{7,6},{8,9},{9,8},{10,11... | collective-permute-start | bytes 221192 | tf_op jit(solution)/shard_map/ppermute | solution.py:227
  8.5 4.8 %collective-permute-start.3 = (bf16[16,16,128]{2,1,0:T(8,128)(2,1)S(1)}, bf16[16,16,128]{2,1,0:T(8,128)(2,1)S(1)}, u32[]{:S(2)}, u32[]{:S(2)}) collective-permute-start(bf16[16,16,128]{2,1,0:T(8,128)(2,1)S(1)} %get-tuple-element.27), channel_id=1, source_target_pairs={{0,10},{2,8},{4,14},{6,12},{8,2},{10,0},{12,6},{14,4},{1,11},{3,9}... | collective-permute-start | bytes 196616 | tf_op jit(solution)/shard_map/ppermute | solution.py:223
  9.2 4.2 %collective-permute-start.4 = (bf16[16,16,128]{2,1,0:T(8,128)(2,1)S(1)}, bf16[16,16,128]{2,1,0:T(8,128)(2,1)S(1)}, u32[]{:S(2)}, u32[]{:S(2)}) collective-permute-start(bf16[16,16,128]{2,1,0:T(8,128)(2,1)S(1)} %get-tuple-element.28), channel_id=1, source_target_pairs={{0,2},{2,0},{4,6},{6,4},{8,10},{10,8},{12,14},{14,12},{1,3},{3,1},... | collective-permute-start | bytes 196616 | tf_op jit(solution)/shard_map/ppermute | solution.py:223
  11.6 1.8 %collective-permute-start.2 = (bf16[2,3,16,128]{3,2,1,0:T(8,128)(2,1)S(1)}, bf16[2,3,16,128]{3,2,1,0:T(8,128)(2,1)S(1)}, u32[]{:S(2)}, u32[]{:S(2)}) collective-permute-start(bf16[2,3,16,128]{3,2,1,0:T(8,128)(2,1)S(1)} %pick.1._), channel_id=1, source_target_pairs={{0,2},{2,0},{1,3},{3,1},{4,6},{6,4},{5,7},{7,5},{8,10},{10,8},{9,1... | collective-permute-start | bytes 73736 | tf_op jit(solution)/shard_map/ppermute | solution.py:259

commit v10 on v9

--- a/solution.py
+++ b/solution.py
@@ -97,8 +97,9 @@
         turned[p] = blocks[p].T
 
 
-def stencil(subs, modes, stiff, _, *refs):
-    columns, total = refs[:-1], refs[-1]
+def stencil(doms, subs, slots, send, modes, stiff, _, *refs):
+    early = [k for k in exchange(doms) if has_halo(k)]
+    arrived, columns, total = refs[: len(early)], refs[len(early) : -1], refs[-1]
     rows, cells = stiff.shape[1:]
     count = modes.shape[0] // rows
     shift = helm_shift * lax.axis_index("mesh").astype(jnp.float32)
@@ -129,6 +130,14 @@
         for weight, near in zip(weights, near_by(here, m)):
             result = result + weight * (here - near)
         total[pl.ds(m, rows, stride=count), :] = result
+    take_back(lax.axis_index("dom"), count, slots, send, total, zip(early, arrived))
+
+
+def take_back(d, count, slots, send, total, arrived):
+    for k, ref in arrived:
+        for j in range(slots):
+            part = pl.ds(pl.multiple_of(send[0, 0, 0, d ^ k, j] * count, count), count)
+            total[part, :] -= ref[slots + j].astype(jnp.float32)
 
 
 def pick(doms, slots, *refs):
@@ -144,14 +153,13 @@
 
 
 def couple(doms, slots, own, peer, slot, send, turned, modes, stiff, halo, *refs):
-    arrived, (_, total, out, foreign, back, held, sems) = dict(zip(exchange(doms), refs)), refs[doms:]
+    arrived, (_, total, out, foreign, held, sems) = dict(zip(exchange(doms), refs)), refs[doms:]
     count = foreign.shape[1]
     rows = total.shape[0] // count
     d = lax.axis_index("dom")
     for k in range(doms):
         for j in range(slots):
             foreign[(d ^ k) * slots + j] = arrived[k][j]
-            back[(d ^ k) * slots + j] = arrived[k][slots + j].astype(jnp.float32)
     for side, row in enumerate((0, rows - 1)):
         near = whole(halo[side, 0], halo[side, 1])
         weight = 0.5 * (stiff[0, row : row + 1, :] + whole(halo[side, 2, 0:1], halo[side, 2, 1:2]))
@@ -161,9 +169,7 @@
         part = pl.ds(pl.multiple_of(row * count, count), count)
         total[part, :] -= term
 
-    for g in range(doms):
-        for j in range(slots):
-            subtract(send[0, 0, 0, g, j], back[g * slots + j])
+    take_back(d, count, slots, send, total, ((k, arrived[k]) for k in range(doms) if not has_halo(k)))
     for p in range(0, turned.shape[0], 2):
         first, second = (foreign[peer[0, 0, 0, q] * slots + slot[0, 0, 0, q]] for q in (p, p + 1))
         for q, term in zip((p, p + 1), pair_dot(first, second, turned[p : p + 2])):
@@ -249,13 +255,13 @@
         name="pick",
     )(*(arrived[k] for k in exchange(doms) if has_halo(k)), turned)
     partial = pl.pallas_call(
-        functools.partial(stencil, subs),
+        functools.partial(stencil, doms, subs, slots),
         out_shape=like(flat.shape, jnp.float32),
-        in_specs=[VMEM, VMEM, ANY] + [VMEM] * len(columns),
+        in_specs=[SMEM, VMEM, VMEM, ANY] + [VMEM] * (sum(map(has_halo, range(doms))) + len(columns)),
         out_specs=VMEM,
         compiler_params=params,
         name="stencil",
-    )(modes, stiff, picked, *columns)
+    )(indices[3], modes, stiff, picked, *(arrived[k] for k in exchange(doms) if has_halo(k)), *columns)
     halo = lax.ppermute(picked, "mesh", [(0, 1), (1, 0)])
     _, out = pl.pallas_call(
         functools.partial(couple, doms, slots),
@@ -264,7 +270,6 @@
         out_specs=[VMEM, HBM],
         scratch_shapes=[
             pltpu.VMEM((doms * slots, count, cells), jnp.bfloat16),
-            pltpu.VMEM((doms * slots, count, cells), jnp.float32),
             pltpu.VMEM(flat.shape, jnp.float32),
             pltpu.SemaphoreType.DMA((2,)),
         ],

time: 15 us -> 14.9 us (level)
  no operation moved by 1% of the time
where the time goes in v10:
time: 14.9 us; the launch traced here: 14.8 us
  starting transfers between devices  7.61 us (51%)
  Pallas kernels  5.22 us (35%)
  waiting for transfers between devices  1.92 us (13%)
    ppermute x4, starting transfers between devices, shards(): arrived[k] = lax.ppermute(outgoing[k], ('dom', 'mesh'), route)  5.74 us
    pallas_call x1, Pallas kernels, shards(): pl.pallas_call(functools.partial(before, doms, subs, slots, rows), out_sh...  2.46 us
    ppermute x4, waiting for transfers between devices, shards(): arrived[k] = lax.ppermute(outgoing[k], ('dom', 'mesh'), route)  1.91 us
    ppermute x1, starting transfers between devices, shards(): columns = [lax.ppermute(column, 'sub', [(0, 1), (1, 0)])]  1.49 us
    pallas_call x1, Pallas kernels, shards(): pl.pallas_call(functools.partial(couple, doms, slots), out_shape=[like(pa...  1.41 us
    pallas_call x1, Pallas kernels, shards(): pl.pallas_call(turn, out_shape=like(blocks.shape, blocks.dtype), in_specs...  0.86 us
    pallas_call x1, Pallas kernels, shards(): pl.pallas_call(functools.partial(stencil, doms, subs, slots), out_shape=l...  0.48 us
    ppermute x1, starting transfers between devices, shards(): halo = lax.ppermute(picked, 'mesh', [(0, 1), (1, 0)])  0.39 us
  transfers between devices with their start and end apart: 6, of which 2 were waited for; matrix products, arithmetic and copies ran while one was open for 0% of the time, Pallas kernels for 9%

profile of v10, /device:TPU:0, one launch (start us, length us, event | category | flops | bytes accessed | tf_op | source)
XLA Modules:
  0.0 14.8 jit_solution(15646055684635323287)
XLA Ops:
  0.0 2.5 %before.1 = (bf16[16,16,128]{2,1,0:T(8,128)(2,1)S(1)}, bf16[19,16,128]{2,1,0:T(8,128)(2,1)S(1)}, bf16[16,16,128]{2,1,0:T(8,128)(2,1)S(1)}, bf16[19,16,128]{2,1,0...) custom-call(s32[1,1,1,96]{3,2,1,0:T(1,128)} %own_in.1, ...), custom_call_target="tpu_custom_call" | custom-call | tf_op jit(solution)/shard_map/before/pallas_call | solution.py:204
  2.5 4.6 %collective-permute-start = (bf16[19,16,128]{2,1,0:T(8,128)(2,1)S(1)}, bf16[19,16,128]{2,1,0:T(8,128)(2,1)S(1)}, u32[]{:S(2)}, u32[]{:S(2)}) collective-permute-start(bf16[19,16,128]{2,1,0:T(8,128)(2,1)S(1)} %get-tuple-element.25), channel_id=1, source_target_pairs={{0,14},{2,12},{4,10},{6,8},{8,6},{10,4},{12,2},{14,0},{1,15},{3,13... | collective-permute-start | bytes 233480 | tf_op jit(solution)/shard_map/ppermute | solution.py:229
  7.0 0.0 collective-permute-start.1
  7.0 1.5 %collective-permute-start.5 = (f32[1,144,128]{2,1,0:T(8,128)S(1)}, f32[1,144,128]{2,1,0:T(8,128)S(1)}, u32[]{:S(2)}, u32[]{:S(2)}) collective-permute-start(f32[1,144,128]{2,1,0:T(8,128)S(1)} %get-tuple-element.29), channel_id=1, source_target_pairs={{0,1},{1,0},{2,3},{3,2},{4,5},{5,4},{6,7},{7,6},{8,9},{9,8},{10,11... | collective-permute-start | bytes 221192 | tf_op jit(solution)/shard_map/ppermute | solution.py:233
  8.5 0.6 %collective-permute-start.3 = (bf16[16,16,128]{2,1,0:T(8,128)(2,1)S(1)}, bf16[16,16,128]{2,1,0:T(8,128)(2,1)S(1)}, u32[]{:S(2)}, u32[]{:S(2)}) collective-permute-start(bf16[16,16,128]{2,1,0:T(8,128)(2,1)S(1)} %get-tuple-element.27), channel_id=1, source_target_pairs={{0,10},{2,8},{4,14},{6,12},{8,2},{10,0},{12,6},{14,4},{1,11},{3,9}... | collective-permute-start | bytes 196616 | tf_op jit(solution)/shard_map/ppermute | solution.py:229
  9.2 0.5 %collective-permute-start.4 = (bf16[16,16,128]{2,1,0:T(8,128)(2,1)S(1)}, bf16[16,16,128]{2,1,0:T(8,128)(2,1)S(1)}, u32[]{:S(2)}, u32[]{:S(2)}) collective-permute-start(bf16[16,16,128]{2,1,0:T(8,128)(2,1)S(1)} %get-tuple-element.28), channel_id=1, source_target_pairs={{0,2},{2,0},{4,6},{6,4},{8,10},{10,8},{12,14},{14,12},{1,3},{3,1},... | collective-permute-start | bytes 196616 | tf_op jit(solution)/shard_map/ppermute | solution.py:229
  9.7 0.9 %turn.1.refs_2_.turned = bf16[96,128,128]{2,1,0:T(8,128)(2,1)S(1)} custom-call(bf16[96,128,128]{2,1,0:T(8,128)(2,1)S(1)} %get-tuple-element.22.blocks), custom_call_target="tpu_custom_call" | custom-call | bytes 8388608 | tf_op jit(solution)/shard_map/turn/pallas_call | solution.py:240
  10.6 0.0 collective-permute-done.refs_0_
  10.6 1.0 %collective-permute-done.1.refs_1_ = bf16[19,16,128]{2,1,0:T(8,128)(2,1)S(1)} collective-permute-done((bf16[19,16,128]{2,1,0:T(8,128)(2,1)S(1)}, bf16[19,16,128]{2,1,0:T(8,128)(2,1)S(1)}, u32[]{:S(2)}, u32[]{:S(2)}) %collective-permute-start.1) | collective-permute-done | bytes 77856 | tf_op jit(solution)/shard_map/ppermute | solution.py:229
  11.6 0.4 %collective-permute-start.2 = (bf16[2,3,16,128]{3,2,1,0:T(8,128)(2,1)S(1)}, bf16[2,3,16,128]{3,2,1,0:T(8,128)(2,1)S(1)}, u32[]{:S(2)}, u32[]{:S(2)}) collective-permute-start(bf16[2,3,16,128]{3,2,1,0:T(8,128)(2,1)S(1)} %pick.1._), channel_id=1, source_target_pairs={{0,2},{2,0},{1,3},{3,1},{4,6},{6,4},{5,7},{7,5},{8,10},{10,8},{9,1... | collective-permute-start | bytes 73736 | tf_op jit(solution)/shard_map/ppermute | solution.py:265
  12.0 0.0 collective-permute-done.5.refs_2_
  12.0 0.5 %stencil.1.refs_4_ = f32[512,128]{1,0:T(8,128)S(1)} custom-call(s32[1,1,1,4,8]{4,3,2,1,0:T(4,128)S(4)} %get-tuple-element.21.send, f32[512,128]{1,0:T(8,128)S(1)} %get-tuple-element.23.modes, f32[1,32,128]{2,1,0:T(8,128)S(1)} %get-tuple-element.24.stiff, bf16[2,3,16,128]{3,2,1,0:T(8,128)(2,1)S(1)} %pick.1._, ...), custom_call_target="tpu_custom_call" | custom-call | tf_op jit(solution)/shard_map/stencil/pallas_call | solution.py:257
  12.5 0.9 %collective-permute-done.3.refs_2_ = bf16[16,16,128]{2,1,0:T(8,128)(2,1)S(1)} collective-permute-done((bf16[16,16,128]{2,1,0:T(8,128)(2,1)S(1)}, bf16[16,16,128]{2,1,0:T(8,128)(2,1)S(1)}, u32[]{:S(2)}, u32[]{:S(2)}) %collective-permute-start.3) | collective-permute-done | bytes 65568 | tf_op jit(solution)/shard_map/ppermute | solution.py:229
  13.4 0.0 collective-permute-done.4.refs_3_
  13.4 0.0 collective-permute-done.2.halo
  13.4 1.4 %couple.1 = (f32[512,128]{1,0:T(8,128)S(1)}, f32[512,128]{1,0:T(8,128)}) custom-call(s32[1,1,1,96]{3,2,1,0:T(1,128)S(4)} %get-tuple-element.18.own, s32[1,1,1,96]{3,2,1,0:T(1,128)S(4)} %get-tuple-element.19.peer, s32[1,1,1,96]{3,2,1,0:T(1,128)S(4)} %get-tuple-element.20.slot, ...), custom_call_target="tpu_custom_call", output_to_operand_aliasing={{0}: (12, {})} | custom-call | bytes 8388608 | tf_op jit(solution)/shard_map/couple/pallas_call | solution.py:266
  (1 shorter events, 0.0 us)
Async XLA Ops:
  2.5 8.1 %collective-permute-start = (bf16[19,16,128]{2,1,0:T(8,128)(2,1)S(1)}, bf16[19,16,128]{2,1,0:T(8,128)(2,1)S(1)}, u32[]{:S(2)}, u32[]{:S(2)}) collective-permute-start(bf16[19,16,128]{2,1,0:T(8,128)(2,1)S(1)} %get-tuple-element.25), channel_id=1, source_target_pairs={{0,14},{2,12},{4,10},{6,8},{8,6},{10,4},{12,2},{14,0},{1,15},{3,13... | collective-permute-start | bytes 233480 | tf_op jit(solution)/shard_map/ppermute | solution.py:229
  7.0 4.6 %collective-permute-start.1 = (bf16[19,16,128]{2,1,0:T(8,128)(2,1)S(1)}, bf16[19,16,128]{2,1,0:T(8,128)(2,1)S(1)}, u32[]{:S(2)}, u32[]{:S(2)}) collective-permute-start(bf16[19,16,128]{2,1,0:T(8,128)(2,1)S(1)} %get-tuple-element.26), channel_id=1, source_target_pairs={{0,6},{2,4},{4,2},{6,0},{8,14},{10,12},{12,10},{14,8},{1,7},{3,5},... | collective-permute-start | bytes 233480 | tf_op jit(solution)/shard_map/ppermute | solution.py:229
  7.0 5.0 %collective-permute-start.5 = (f32[1,144,128]{2,1,0:T(8,128)S(1)}, f32[1,144,128]{2,1,0:T(8,128)S(1)}, u32[]{:S(2)}, u32[]{:S(2)}) collective-permute-start(f32[1,144,128]{2,1,0:T(8,128)S(1)} %get-tuple-element.29), channel_id=1, source_target_pairs={{0,1},{1,0},{2,3},{3,2},{4,5},{5,4},{6,7},{7,6},{8,9},{9,8},{10,11... | collective-permute-start | bytes 221192 | tf_op jit(solution)/shard_map/ppermute | solution.py:233
  8.5 4.8 %collective-permute-start.3 = (bf16[16,16,128]{2,1,0:T(8,128)(2,1)S(1)}, bf16[16,16,128]{2,1,0:T(8,128)(2,1)S(1)}, u32[]{:S(2)}, u32[]{:S(2)}) collective-permute-start(bf16[16,16,128]{2,1,0:T(8,128)(2,1)S(1)} %get-tuple-element.27), channel_id=1, source_target_pairs={{0,10},{2,8},{4,14},{6,12},{8,2},{10,0},{12,6},{14,4},{1,11},{3,9}... | collective-permute-start | bytes 196616 | tf_op jit(solution)/shard_map/ppermute | solution.py:229
  9.2 4.2 %collective-permute-start.4 = (bf16[16,16,128]{2,1,0:T(8,128)(2,1)S(1)}, bf16[16,16,128]{2,1,0:T(8,128)(2,1)S(1)}, u32[]{:S(2)}, u32[]{:S(2)}) collective-permute-start(bf16[16,16,128]{2,1,0:T(8,128)(2,1)S(1)} %get-tuple-element.28), channel_id=1, source_target_pairs={{0,2},{2,0},{4,6},{6,4},{8,10},{10,8},{12,14},{14,12},{1,3},{3,1},... | collective-permute-start | bytes 196616 | tf_op jit(solution)/shard_map/ppermute | solution.py:229
  11.6 1.8 %collective-permute-start.2 = (bf16[2,3,16,128]{3,2,1,0:T(8,128)(2,1)S(1)}, bf16[2,3,16,128]{3,2,1,0:T(8,128)(2,1)S(1)}, u32[]{:S(2)}, u32[]{:S(2)}) collective-permute-start(bf16[2,3,16,128]{3,2,1,0:T(8,128)(2,1)S(1)} %pick.1._), channel_id=1, source_target_pairs={{0,2},{2,0},{1,3},{3,1},{4,6},{6,4},{5,7},{7,5},{8,10},{10,8},{9,1... | collective-permute-start | bytes 73736 | tf_op jit(solution)/shard_map/ppermute | solution.py:265

commit v11 on v10

--- a/solution.py
+++ b/solution.py
@@ -47,8 +47,9 @@
     own, peer, slot, send, tiles, sums, sems, block_sems = refs[doms + 4 :]
     sources = (own_in, peer_in, slot_in, send_in, modes_in, stiff_in)
     copies = load(sources, (own, peer, slot, send, modes, stiff), sems)
-    half = blocks.shape[0] // 2
-    parts = [pl.ds(0, half), pl.ds(half, half)]
+    pairs = blocks.shape[0]
+    cuts = (0, pairs // 2 + 4, pairs)
+    parts = [pl.ds(a, b - a) for a, b in zip(cuts, cuts[1:])]
     block_copies = load([coupling.at[0, 0, 0, part] for part in parts], [blocks.at[part] for part in parts], block_sems, 1)
     d = lax.axis_index("dom")
     count, cells = tiles.shape[1:]
@@ -83,7 +84,7 @@
             column[side] = ends[side]
     for c, copy in enumerate(block_copies):
         copy.wait()
-        for p in range(c * half, (c + 1) * half, 2):
+        for p in range(cuts[c], cuts[c + 1], 2):
             terms = pair_dot(tiles[own[0, 0, 0, p]], tiles[own[0, 0, 0, p + 1]], blocks[p : p + 2])
             for q, term in zip((p, p + 1), terms):
                 sums[peer[0, 0, 0, q] * slots + slot[0, 0, 0, q]] += term

time: 14.9 us -> 14.9 us (level)
  no operation moved by 1% of the time
where the time goes in v11:
time: 14.9 us; the launch traced here: 14.6 us
  starting transfers between devices  7.61 us (51%)
  Pallas kernels  5.18 us (35%)
  waiting for transfers between devices  1.81 us (12%)
    ppermute x4, starting transfers between devices, shards(): arrived[k] = lax.ppermute(outgoing[k], ('dom', 'mesh'), route)  5.74 us
    pallas_call x1, Pallas kernels, shards(): pl.pallas_call(functools.partial(before, doms, subs, slots, rows), out_sh...  2.42 us
    ppermute x4, waiting for transfers between devices, shards(): arrived[k] = lax.ppermute(outgoing[k], ('dom', 'mesh'), route)  1.81 us
    ppermute x1, starting transfers between devices, shards(): columns = [lax.ppermute(column, 'sub', [(0, 1), (1, 0)])]  1.49 us
    pallas_call x1, Pallas kernels, shards(): pl.pallas_call(functools.partial(couple, doms, slots), out_shape=[like(pa...  1.41 us
    pallas_call x1, Pallas kernels, shards(): pl.pallas_call(turn, out_shape=like(blocks.shape, blocks.dtype), in_specs...  0.86 us
    pallas_call x1, Pallas kernels, shards(): pl.pallas_call(functools.partial(stencil, doms, subs, slots), out_shape=l...  0.48 us
    ppermute x1, starting transfers between devices, shards(): halo = lax.ppermute(picked, 'mesh', [(0, 1), (1, 0)])  0.38 us
  transfers between devices with their start and end apart: 6, of which 2 were waited for; matrix products, arithmetic and copies ran while one was open for 0% of the time, Pallas kernels for 9%

profile of v11, /device:TPU:0, one launch (start us, length us, event | category | flops | bytes accessed | tf_op | source)
XLA Modules:
  0.0 14.6 jit_solution(10527227976197314205)
XLA Ops:
  0.0 2.4 %before.1 = (bf16[16,16,128]{2,1,0:T(8,128)(2,1)S(1)}, bf16[19,16,128]{2,1,0:T(8,128)(2,1)S(1)}, bf16[16,16,128]{2,1,0:T(8,128)(2,1)S(1)}, bf16[19,16,128]{2,1,0...) custom-call(s32[1,1,1,96]{3,2,1,0:T(1,128)} %own_in.1, ...), custom_call_target="tpu_custom_call" | custom-call | tf_op jit(solution)/shard_map/before/pallas_call | solution.py:205
  2.4 4.6 %collective-permute-start = (bf16[19,16,128]{2,1,0:T(8,128)(2,1)S(1)}, bf16[19,16,128]{2,1,0:T(8,128)(2,1)S(1)}, u32[]{:S(2)}, u32[]{:S(2)}) collective-permute-start(bf16[19,16,128]{2,1,0:T(8,128)(2,1)S(1)} %get-tuple-element.25), channel_id=1, source_target_pairs={{0,14},{2,12},{4,10},{6,8},{8,6},{10,4},{12,2},{14,0},{1,15},{3,13... | collective-permute-start | bytes 233480 | tf_op jit(solution)/shard_map/ppermute | solution.py:230
  7.0 0.0 collective-permute-start.1
  7.0 1.5 %collective-permute-start.5 = (f32[1,144,128]{2,1,0:T(8,128)S(1)}, f32[1,144,128]{2,1,0:T(8,128)S(1)}, u32[]{:S(2)}, u32[]{:S(2)}) collective-permute-start(f32[1,144,128]{2,1,0:T(8,128)S(1)} %get-tuple-element.29), channel_id=1, source_target_pairs={{0,1},{1,0},{2,3},{3,2},{4,5},{5,4},{6,7},{7,6},{8,9},{9,8},{10,11... | collective-permute-start | bytes 221192 | tf_op jit(solution)/shard_map/ppermute | solution.py:234
  8.5 0.6 %collective-permute-start.3 = (bf16[16,16,128]{2,1,0:T(8,128)(2,1)S(1)}, bf16[16,16,128]{2,1,0:T(8,128)(2,1)S(1)}, u32[]{:S(2)}, u32[]{:S(2)}) collective-permute-start(bf16[16,16,128]{2,1,0:T(8,128)(2,1)S(1)} %get-tuple-element.27), channel_id=1, source_target_pairs={{0,10},{2,8},{4,14},{6,12},{8,2},{10,0},{12,6},{14,4},{1,11},{3,9}... | collective-permute-start | bytes 196616 | tf_op jit(solution)/shard_map/ppermute | solution.py:230
  9.1 0.5 %collective-permute-start.4 = (bf16[16,16,128]{2,1,0:T(8,128)(2,1)S(1)}, bf16[16,16,128]{2,1,0:T(8,128)(2,1)S(1)}, u32[]{:S(2)}, u32[]{:S(2)}) collective-permute-start(bf16[16,16,128]{2,1,0:T(8,128)(2,1)S(1)} %get-tuple-element.28), channel_id=1, source_target_pairs={{0,2},{2,0},{4,6},{6,4},{8,10},{10,8},{12,14},{14,12},{1,3},{3,1},... | collective-permute-start | bytes 196616 | tf_op jit(solution)/shard_map/ppermute | solution.py:230
  9.7 0.9 %turn.1.refs_2_.turned = bf16[96,128,128]{2,1,0:T(8,128)(2,1)S(1)} custom-call(bf16[96,128,128]{2,1,0:T(8,128)(2,1)S(1)} %get-tuple-element.22.blocks), custom_call_target="tpu_custom_call" | custom-call | bytes 8388608 | tf_op jit(solution)/shard_map/turn/pallas_call | solution.py:241
  10.5 0.0 collective-permute-done.refs_0_
  10.5 1.0 %collective-permute-done.1.refs_1_ = bf16[19,16,128]{2,1,0:T(8,128)(2,1)S(1)} collective-permute-done((bf16[19,16,128]{2,1,0:T(8,128)(2,1)S(1)}, bf16[19,16,128]{2,1,0:T(8,128)(2,1)S(1)}, u32[]{:S(2)}, u32[]{:S(2)}) %collective-permute-start.1) | collective-permute-done | bytes 77856 | tf_op jit(solution)/shard_map/ppermute | solution.py:230
  11.6 0.4 %collective-permute-start.2 = (bf16[2,3,16,128]{3,2,1,0:T(8,128)(2,1)S(1)}, bf16[2,3,16,128]{3,2,1,0:T(8,128)(2,1)S(1)}, u32[]{:S(2)}, u32[]{:S(2)}) collective-permute-start(bf16[2,3,16,128]{3,2,1,0:T(8,128)(2,1)S(1)} %pick.1._), channel_id=1, source_target_pairs={{0,2},{2,0},{1,3},{3,1},{4,6},{6,4},{5,7},{7,5},{8,10},{10,8},{9,1... | collective-permute-start | bytes 73736 | tf_op jit(solution)/shard_map/ppermute | solution.py:266
  12.0 0.0 collective-permute-done.5.refs_2_
  12.0 0.5 %stencil.1.refs_4_ = f32[512,128]{1,0:T(8,128)S(1)} custom-call(s32[1,1,1,4,8]{4,3,2,1,0:T(4,128)S(4)} %get-tuple-element.21.send, f32[512,128]{1,0:T(8,128)S(1)} %get-tuple-element.23.modes, f32[1,32,128]{2,1,0:T(8,128)S(1)} %get-tuple-element.24.stiff, bf16[2,3,16,128]{3,2,1,0:T(8,128)(2,1)S(1)} %pick.1._, ...), custom_call_target="tpu_custom_call" | custom-call | tf_op jit(solution)/shard_map/stencil/pallas_call | solution.py:258
  12.5 0.8 %collective-permute-done.3.refs_2_ = bf16[16,16,128]{2,1,0:T(8,128)(2,1)S(1)} collective-permute-done((bf16[16,16,128]{2,1,0:T(8,128)(2,1)S(1)}, bf16[16,16,128]{2,1,0:T(8,128)(2,1)S(1)}, u32[]{:S(2)}, u32[]{:S(2)}) %collective-permute-start.3) | collective-permute-done | bytes 65568 | tf_op jit(solution)/shard_map/ppermute | solution.py:230
  13.2 0.0 collective-permute-done.4.refs_3_
  13.2 0.0 collective-permute-done.2.halo
  13.2 1.4 %couple.1 = (f32[512,128]{1,0:T(8,128)S(1)}, f32[512,128]{1,0:T(8,128)}) custom-call(s32[1,1,1,96]{3,2,1,0:T(1,128)S(4)} %get-tuple-element.18.own, s32[1,1,1,96]{3,2,1,0:T(1,128)S(4)} %get-tuple-element.19.peer, s32[1,1,1,96]{3,2,1,0:T(1,128)S(4)} %get-tuple-element.20.slot, ...), custom_call_target="tpu_custom_call", output_to_operand_aliasing={{0}: (12, {})} | custom-call | bytes 8388608 | tf_op jit(solution)/shard_map/couple/pallas_call | solution.py:267
  (1 shorter events, 0.0 us)
Async XLA Ops:
  2.4 8.1 %collective-permute-start = (bf16[19,16,128]{2,1,0:T(8,128)(2,1)S(1)}, bf16[19,16,128]{2,1,0:T(8,128)(2,1)S(1)}, u32[]{:S(2)}, u32[]{:S(2)}) collective-permute-start(bf16[19,16,128]{2,1,0:T(8,128)(2,1)S(1)} %get-tuple-element.25), channel_id=1, source_target_pairs={{0,14},{2,12},{4,10},{6,8},{8,6},{10,4},{12,2},{14,0},{1,15},{3,13... | collective-permute-start | bytes 233480 | tf_op jit(solution)/shard_map/ppermute | solution.py:230
  7.0 4.6 %collective-permute-start.1 = (bf16[19,16,128]{2,1,0:T(8,128)(2,1)S(1)}, bf16[19,16,128]{2,1,0:T(8,128)(2,1)S(1)}, u32[]{:S(2)}, u32[]{:S(2)}) collective-permute-start(bf16[19,16,128]{2,1,0:T(8,128)(2,1)S(1)} %get-tuple-element.26), channel_id=1, source_target_pairs={{0,6},{2,4},{4,2},{6,0},{8,14},{10,12},{12,10},{14,8},{1,7},{3,5},... | collective-permute-start | bytes 233480 | tf_op jit(solution)/shard_map/ppermute | solution.py:230
  7.0 5.0 %collective-permute-start.5 = (f32[1,144,128]{2,1,0:T(8,128)S(1)}, f32[1,144,128]{2,1,0:T(8,128)S(1)}, u32[]{:S(2)}, u32[]{:S(2)}) collective-permute-start(f32[1,144,128]{2,1,0:T(8,128)S(1)} %get-tuple-element.29), channel_id=1, source_target_pairs={{0,1},{1,0},{2,3},{3,2},{4,5},{5,4},{6,7},{7,6},{8,9},{9,8},{10,11... | collective-permute-start | bytes 221192 | tf_op jit(solution)/shard_map/ppermute | solution.py:234
  8.5 4.7 %collective-permute-start.3 = (bf16[16,16,128]{2,1,0:T(8,128)(2,1)S(1)}, bf16[16,16,128]{2,1,0:T(8,128)(2,1)S(1)}, u32[]{:S(2)}, u32[]{:S(2)}) collective-permute-start(bf16[16,16,128]{2,1,0:T(8,128)(2,1)S(1)} %get-tuple-element.27), channel_id=1, source_target_pairs={{0,10},{2,8},{4,14},{6,12},{8,2},{10,0},{12,6},{14,4},{1,11},{3,9}... | collective-permute-start | bytes 196616 | tf_op jit(solution)/shard_map/ppermute | solution.py:230
  9.1 4.1 %collective-permute-start.4 = (bf16[16,16,128]{2,1,0:T(8,128)(2,1)S(1)}, bf16[16,16,128]{2,1,0:T(8,128)(2,1)S(1)}, u32[]{:S(2)}, u32[]{:S(2)}) collective-permute-start(bf16[16,16,128]{2,1,0:T(8,128)(2,1)S(1)} %get-tuple-element.28), channel_id=1, source_target_pairs={{0,2},{2,0},{4,6},{6,4},{8,10},{10,8},{12,14},{14,12},{1,3},{3,1},... | collective-permute-start | bytes 196616 | tf_op jit(solution)/shard_map/ppermute | solution.py:230
  11.6 1.6 %collective-permute-start.2 = (bf16[2,3,16,128]{3,2,1,0:T(8,128)(2,1)S(1)}, bf16[2,3,16,128]{3,2,1,0:T(8,128)(2,1)S(1)}, u32[]{:S(2)}, u32[]{:S(2)}) collective-permute-start(bf16[2,3,16,128]{3,2,1,0:T(8,128)(2,1)S(1)} %pick.1._), channel_id=1, source_target_pairs={{0,2},{2,0},{1,3},{3,1},{4,6},{6,4},{5,7},{7,5},{8,10},{10,8},{9,1... | collective-permute-start | bytes 73736 | tf_op jit(solution)/shard_map/ppermute | solution.py:266
